TPU v7x, 32 devices: a whole 2x2x4 slice. The times are simulated.
32 devices in a mesh: section: 2 (over core), dp: 16 (over z, y, x).
Axes of the slice: x: 2, y: 2, z: 4, core: 2. Of those that a mesh axis runs over, the one named last changes fastest.
Arguments:
- images: bfloat16 [2, 64, 14, 14, 1024], P(None, 'dp'), may hold values from 0 to 18
- out_grad: bfloat16 [2, 64, 7, 7, 2048], P(None, 'dp'), may hold values from -13.5 to 13.5
- live_counts: int32 [16, 2], replicated, may hold values from 2 to 4, as said below
- w_reduce0: bfloat16 [1024, 512], replicated, may hold values from -0.1875 to 0.1875
- w_short: bfloat16 [1024, 2048], replicated, may hold values from -0.1875 to 0.1875
- short_gain: float32 [2048], replicated, may hold values from 0.25 to 1.75
- short_bias: float32 [2048], replicated, may hold values from -2 to 2
- w_reduce1: bfloat16 [2048, 512], replicated, may hold values from -0.125 to 0.125
- w_mid: bfloat16 [2, 4608, 512], P('section'), may hold values from -0.09375 to 0.09375
- w_expand: bfloat16 [2, 512, 2048], P('section'), may hold values from -0.25 to 0.25
- gain_narrow: float32 [2, 2, 512], P('section'), may hold values from 0.25 to 1.75
- bias_narrow: float32 [2, 2, 512], P('section'), may hold values from -2 to 2
- gain_wide: float32 [2, 2048], P('section'), may hold values from 0.25 to 1.75
- bias_wide: float32 [2, 2048], P('section'), may hold values from -2 to 2
Outputs:
- block_out: bfloat16 [2, 64, 7, 7, 2048], P('section', 'dp')
- image_grad: bfloat16 [2, 64, 14, 14, 1024], P('section', 'dp')
- grad_reduce0: float32 [1024, 512], P(('section', 'dp'))
- grad_short: float32 [1024, 2048], P(('section', 'dp'))
- grad_short_norm: float32 [2, 2048], P(None, ('section', 'dp'))
- grad_reduce1: float32 [2048, 512], P(('section', 'dp'))
- grad_mid: float32 [2, 4608, 512], P('section', 'dp')
- grad_expand: float32 [2, 512, 2048], P('section', 'dp')
- grad_gain_narrow: float32 [2, 2, 512], P('section')
- grad_bias_narrow: float32 [2, 2, 512], P('section')
- grad_gain_wide: float32 [2, 2048], P('section')
- grad_bias_wide: float32 [2, 2048], P('section')
Inputs may be any that keep to these rules, and one draw needn't show every extreme that they name: `live_counts`: slots of a dp index are live from its first one; in every micro-batch some dp index has all 4 slots live.
All inputs are finite; a program needn't handle non-finite values.
Results may differ from a plain program's by a relative error of at most 0.022.
Values may be sent and summed in bfloat16 or wider, within the bound.
No kernel may reach another device: no remote copies, remote signals or barrier semaphores. Data moves between devices by JAX's collectives and lax.ppermute only.
A program may use at most 192 MiB of HBM per device.

v0:
```python
import jax
import jax.numpy as jnp
from jax import lax
from jax.experimental import pallas as pl
from jax.experimental.pallas import tpu as pltpu
from jax.sharding import PartitionSpec as P


EPSILON = 1e-05
F32 = jnp.float32
BF16 = jnp.bfloat16
VMEM = pl.BlockSpec(memory_space=pltpu.VMEM)
SMEM = pl.BlockSpec(memory_space=pltpu.SMEM)
ANY = pl.BlockSpec(memory_space=pl.ANY)


def spec(shape, dtype=F32):
    return jax.ShapeDtypeStruct(shape, dtype)


class Late:
    def __init__(self, source, target, sem):
        self.copy = pltpu.make_async_copy(source, target, sem)
        self.copy.start()
        self.target = target
        self.shape = target.shape
        self.waiting = True

    def get(self):
        if self.waiting:
            self.copy.wait()
            self.waiting = False
        return self.target

    def __getitem__(self, index):
        return self.get()[index]


class Out:
    def __init__(self, buffer, target, sem):
        self.ref = buffer
        self.shape = buffer.shape
        self.copy = pltpu.make_async_copy(buffer, target, sem)
        self.sent = False

    def __setitem__(self, index, value):
        self.ref[index] = value

    def send(self):
        self.copy.start()
        self.sent = True


def stage(kernel, outs, out_places, args, places, scratch=()):
    kinds = {"g": VMEM, "s": SMEM, "a": ANY, "d": ANY}
    late = [n for n, kind in enumerate(places) if kind == "d"]
    late_out = [n for n, kind in enumerate(out_places) if kind == "d"]
    buffers = [pltpu.VMEM(args[n].shape, args[n].dtype) for n in late]
    buffers += [pltpu.VMEM(outs[n].shape, outs[n].dtype) for n in late_out]
    args = [
        pltpu.with_memory_space_constraint(arg, pltpu.VMEM) if kind == "g" else arg
        for arg, kind in zip(args, places)
    ]

    def run(*refs):
        inputs = list(refs[: len(args)])
        results = list(refs[len(args) : len(args) + len(outs)])
        rest = refs[len(args) + len(outs) :]
        own, held, sem = rest[: len(scratch)], rest[len(scratch) : -1], rest[-1]
        for place, n in enumerate(late):
            inputs[n] = Late(inputs[n], held[place], sem.at[place])
        waiting = []
        for place, n in enumerate(late_out):
            place += len(late)
            results[n] = Out(held[place], results[n], sem.at[place])
            waiting.append(results[n])
        kernel(*inputs, *results, *own)
        for one in inputs:
            if isinstance(one, Late):
                one.get()
        for one in waiting:
            if not one.sent:
                one.send()
        for one in waiting:
            one.copy.wait()

    return pl.pallas_call(
        run,
        out_shape=list(outs),
        in_specs=[kinds[kind] for kind in places],
        out_specs=[kinds[kind] for kind in out_places],
        scratch_shapes=list(scratch) + buffers + [pltpu.SemaphoreType.DMA((max(1, len(buffers)),))],
        compiler_params=pltpu.CompilerParams(vmem_limit_bytes=58 << 20),
    )(*args)


def split(value, size):
    if size & (size - 1) == 0:
        return value >> (size.bit_length() - 1), value & (size - 1)
    return value // size, value % size


class Geometry:
    def __init__(self, slots, side):
        self.slots = slots
        self.side = side
        self.pitch = side + 1
        self.line = self.pitch * slots
        self.rows = self.pitch * self.line
        self.pixels = side * side

    def mask(self, start, step, width, count=None):
        row = start + lax.broadcasted_iota(jnp.int32, (step, 128), 0)
        position, image = split(row, self.slots)
        line, column = split(position, self.pitch)
        line = split(line, self.pitch)[1]
        good = (column < self.side) & (line < self.side)
        if count is not None:
            good = good & (image < count)
        value = jnp.where(good, 1.0, 0.0).astype(F32)
        return jnp.concatenate([value] * (width // 128), axis=1) if width > 128 else value


def over_rows(rows, step, body, init):
    def one(i, carry):
        return body(pl.multiple_of(i * step, step), carry)

    return lax.fori_loop(0, rows // step, one, init)


def fold_rows(block):
    rows, width = block.shape
    return jnp.sum(block.reshape(rows // 8, 8, width), axis=0)


def step_of(width):
    return 64 if width <= 512 else 16


def local_stats(z_ref, geo, count, planes):
    rows, width = z_ref.shape
    step = step_of(width)
    total = (count * (geo.pixels * planes)).astype(F32)

    def plain(start, acc):
        return acc + fold_rows(z_ref[pl.ds(start, step), :] * geo.mask(start, step, width, count))

    zero = jnp.zeros((8, width), F32)
    average = jnp.sum(over_rows(rows, step, plain, zero), axis=0, keepdims=True) / total

    def squared(start, acc):
        centered = z_ref[pl.ds(start, step), :] - average
        return acc + fold_rows(centered * centered * geo.mask(start, step, width, count))

    spread = jnp.sum(over_rows(rows, step, squared, zero), axis=0, keepdims=True)
    return average, spread


def send_short(out_ref, values):
    values = values.astype(BF16)
    for device in range(out_ref.shape[0]):
        out_ref[device] = values


def packed_stats(pairs):
    average = jnp.concatenate([pair[0] for pair in pairs], axis=1)
    spread = jnp.concatenate([pair[1] for pair in pairs], axis=1)
    high = average.astype(BF16).astype(F32)
    half = spread.shape[1] // 2
    return jnp.concatenate(
        [
            jnp.concatenate([high, spread[:, :half]], axis=1),
            jnp.concatenate([average - high, spread[:, half:]], axis=1),
        ],
        axis=0,
    )


class Unpacked:
    def __init__(self, got):
        self.devices = got.shape[0]
        width = got.shape[2] * 2 // 3
        self.average, self.spread = [], []
        for device in range(self.devices):
            rows = got[device].astype(F32)
            self.average.append(rows[0:1, :width] + rows[1:2, :width])
            self.spread.append(jnp.concatenate([rows[0:1, width:], rows[1:2, width:]], axis=1))
        self.shape = (self.devices, 2, width)

    def __getitem__(self, index):
        device, row, lanes = index
        return (self.average if row.start == 0 else self.spread)[device][:, lanes]


def send_rows(out_ref, values):
    lane = 0
    for pair in values:
        width = pair[0].shape[1]
        for row, value in enumerate(pair):
            for device in range(out_ref.shape[0]):
                out_ref[device, row : row + 1, lane : lane + width] = value
        lane += width


def total_of(counts, section, pixels):
    total = counts[section, 0]
    for device in range(1, counts.shape[1]):
        total = total + counts[section, device]
    return (total * pixels).astype(F32)


def combined(got_ref, lanes, counts, section, pixels):
    devices = got_ref.shape[0]
    total = total_of(counts, section, pixels)
    sizes = [(counts[section, device] * pixels).astype(F32) for device in range(devices)]
    average = sizes[0] * got_ref[0, 0:1, lanes]
    for device in range(1, devices):
        average = average + sizes[device] * got_ref[device, 0:1, lanes]
    average = average / total
    spread = jnp.zeros_like(average)
    for device in range(devices):
        apart = got_ref[device, 0:1, lanes] - average
        spread = spread + (got_ref[device, 1:2, lanes] + sizes[device] * (apart * apart))
    return average, lax.rsqrt(spread / total + EPSILON)


def summed(got_ref):
    total = got_ref[0].astype(F32)
    for device in range(1, got_ref.shape[0]):
        total = total + got_ref[device].astype(F32)
    return total


def sigmoid(values):
    return 1.0 / (1.0 + jnp.exp(-values))


def slope(values):
    part = sigmoid(values)
    return part * (1.0 + values * (1.0 - part))


class Choice:
    def __init__(self, section, wanted, own, other, target, sem):
        self.mine = section == wanted
        self.copies = (
            pltpu.make_async_copy(own.at[0], target, sem),
            pltpu.make_async_copy(other.at[0], target, sem),
        )

    def start(self):
        @pl.when(self.mine)
        def _():
            self.copies[0].start()

        @pl.when(jnp.logical_not(self.mine))
        def _():
            self.copies[1].start()

    def wait(self):
        @pl.when(self.mine)
        def _():
            self.copies[0].wait()

        @pl.when(jnp.logical_not(self.mine))
        def _():
            self.copies[1].wait()


def dot(left, right):
    return jnp.dot(left, right, preferred_element_type=F32)


def dot_back(left, right):
    return lax.dot_general(left, right, (((1,), (1,)), ((), ())), preferred_element_type=F32)


def dot_rows(left, right):
    return lax.dot_general(left, right, (((0,), (0,)), ((), ())), preferred_element_type=F32)


def turned(values, shift):
    shift = shift % values.shape[0]
    if shift == 0:
        return values
    return jnp.concatenate([values[-shift:], values[:-shift]], axis=0)


def taps_of(stride):
    found = []
    for tap_row in range(3):
        for column in range(3):
            if stride == 1:
                found.append((0, tap_row - 1, column - 1))
            else:
                plane = 2 * (tap_row != 1) + (column != 1)
                found.append((plane, -(tap_row == 0), -(column == 0)))
    return found


def first_kernel(geo, place, counts, images, weight, x_out, z_out, sent, raw, slabs, sem):
    section = place[1]
    count = counts[section, place[0]]
    load = pltpu.make_async_copy(images.at[section], raw, sem.at[0])
    load.start()
    used = geo.side * geo.slots
    x_ref = x_out.ref
    for plane in range(4):
        last = (plane + 1) * geo.rows
        x_ref[last - geo.line : last, :] = jnp.zeros((geo.line, x_ref.shape[1]), BF16)
        slabs[plane, used : geo.line, :] = jnp.zeros((geo.slots, x_ref.shape[1]), F32)
    load.wait()
    for line in range(geo.side):
        for plane in range(4):
            for column in range(geo.side):
                at = column * geo.slots
                slabs[plane, at : at + geo.slots, :] = raw[
                    2 * line + plane // 2, 2 * column + plane % 2
                ].astype(F32)
            at = plane * geo.rows + line * geo.line
            x_ref[at : at + geo.line, :] = slabs[plane].astype(BF16)
    x_out.send()
    weight = weight.get()
    z_ref = z_out.ref
    for plane in range(4):
        at = plane * geo.rows
        z_ref[at : at + geo.rows, :] = dot(x_ref[at : at + geo.rows, :], weight[...])
    z_out.send()
    send_rows(sent, (local_stats(z_ref, geo, count, 4),))


def short_kernel(geo, place, counts, x_any, weight, z_out, stats, x_vmem, sem):
    count = counts[place[1], place[0]]
    load = pltpu.make_async_copy(x_any.at[pl.ds(0, geo.rows)], x_vmem, sem.at[0])
    load.start()
    load.wait()
    z_ref = z_out.ref
    z_ref[...] = dot(x_vmem[...], weight.get()[...])
    z_out.send()
    average, spread = local_stats(z_ref, geo, count, 1)
    stats[0:1, :] = average
    stats[1:2, :] = spread


def tap_kernel(geo, planes, block, place, counts, got, z_in, narrow, own, other, *rest):
    if planes == 4:
        stats, taps, z_out, moments, sent, active, weight, sem = rest
    else:
        taps, z_out, moments, sent, active, weight, sem = rest
    section = place[1]
    count = counts[section, place[0]]
    choice = Choice(section, block, own, other, weight, sem.at[0])
    choice.start()
    average, inverse = combined(got, slice(None), counts, section, geo.pixels * planes)
    moments[0:1, :] = average
    moments[1:2, :] = inverse
    gain = narrow[0:1, :] * inverse
    offset = narrow[2:3, :]
    z_ref = z_in.get()
    rows_of, width = z_ref.shape

    def activate(start, carry):
        pre = (z_ref[pl.ds(start, 64), :] - average) * gain + offset
        active[pl.ds(start, 64), :] = pre * sigmoid(pre) * geo.mask(start, 64, width)
        return carry

    over_rows(rows_of, 64, activate, 0)
    ready = {}
    for tap, (plane, line, column) in enumerate(taps_of(2 if planes == 4 else 1)):
        if (plane, column) not in ready:
            values = active[plane * geo.rows : (plane + 1) * geo.rows, :]
            if column != 0:
                values = pltpu.roll(values, (-column * geo.slots) % geo.rows, 0)
            ready[plane, column] = values.astype(BF16)
        taps.ref[:, tap * width : (tap + 1) * width] = turned(ready[plane, column], -line * geo.line)
    taps.send()
    choice.wait()
    z_out.ref[...] = dot(taps.ref[...], weight[...])
    z_out.send()
    values = local_stats(z_out.ref, geo, count, 1)
    if planes == 4:
        send_short(sent, packed_stats((values, (stats[0:1, :], stats[1:2, :]))))
    else:
        send_rows(sent, (values,))


def expand_kernel(geo, block, extra, place, counts, got, z_in, narrow, own, other, *rest):
    if extra:
        a_out, z_out, moments, moments_s, sent, weight, sem = rest
    else:
        a_out, z_out, moments, sent, weight, sem = rest
    section = place[1]
    count = counts[section, place[0]]
    choice = Choice(section, block, own, other, weight, sem.at[0])
    choice.start()
    if extra:
        got = Unpacked(got)
    average, inverse = combined(got, slice(0, z_in.shape[1]), counts, section, geo.pixels)
    moments[0:1, :] = average
    moments[1:2, :] = inverse
    gain = narrow[1:2, :] * inverse
    offset = narrow[3:4, :]
    z_ref = z_in.get()

    def activate(start, carry):
        pre = (z_ref[pl.ds(start, 64), :] - average) * gain + offset
        a_out.ref[pl.ds(start, 64), :] = (pre * sigmoid(pre)).astype(BF16)
        return carry

    over_rows(geo.rows, 64, activate, 0)
    a_out.send()
    choice.wait()
    z_out.ref[...] = dot(a_out.ref[...], weight[...])
    z_out.send()
    send_rows(sent, (local_stats(z_out.ref, geo, count, 1),))
    sent.send()
    if extra:
        lanes = slice(z_ref.shape[1], got.shape[2])
        for row, value in enumerate(combined(got, lanes, counts, section, geo.pixels)):
            moments_s[row : row + 1, :] = value


def join_kernel(geo, place, counts, got, z3, zs, moments_s, wide, short, weight, joined, u_out, moments, sent):
    section = place[1]
    count = counts[section, place[0]]
    average_c, inverse_c = combined(got, slice(None), counts, section, geo.pixels)
    average_s, inverse_s = moments_s[0:1, :], moments_s[1:2, :]
    for number, value in enumerate((average_c, inverse_c, average_s, inverse_s)):
        moments[number : number + 1, :] = value
    gain_c = wide[0:1, :] * inverse_c
    gain_s = short[0:1, :] * inverse_s
    offset = wide[1:2, :] + short[1:2, :]
    z3, zs = z3.get(), zs.get()

    def activate(start, carry):
        rows = pl.ds(start, 16)
        pre = (z3[rows, :] - average_c) * gain_c + (zs[rows, :] - average_s) * gain_s + offset
        joined.ref[rows, :] = (pre * sigmoid(pre)).astype(BF16)
        return carry

    over_rows(geo.rows, 16, activate, 0)
    joined.send()
    u_out.ref[...] = dot(joined.ref[...], weight.get()[...])
    u_out.send()
    send_rows(sent, (local_stats(u_out.ref, geo, count, 1),))


def turn_kernel(geo, place, counts, got, u3, joined, wide, out_grad, block_out, g_out, moments, sent, raw, flat, sem):
    section = place[1]
    count = counts[section, place[0]]
    load = pltpu.make_async_copy(out_grad.at[section], raw, sem.at[0])
    load.start()
    average, inverse = combined(got, slice(None), counts, section, geo.pixels)
    moments[0:1, :] = average
    moments[1:2, :] = inverse
    g_ref = g_out.ref
    width = g_ref.shape[1]
    empty = jnp.zeros((geo.slots, width), F32)
    for line in range(geo.side):
        at = line * geo.line + geo.side * geo.slots
        g_ref[at : at + geo.slots, :] = empty
    g_ref[geo.rows - geo.line : geo.rows, :] = jnp.zeros((geo.line, width), F32)
    load.wait()
    for line in range(geo.side):
        for column in range(geo.side):
            at = line * geo.line + column * geo.slots
            g_ref[at : at + geo.slots, :] = raw[line, column].astype(F32)
    weight = wide[0:1, :]
    offset = wide[1:2, :]
    u3, joined = u3.get(), joined.get()

    def activate(start, carry):
        plain, scaled = carry
        rows = pl.ds(start, 16)
        normed = (u3[rows, :] - average) * inverse
        pre = normed * weight + offset + joined[rows, :].astype(F32)
        part = sigmoid(pre)
        flat[rows, :] = pre * part
        upstream = g_ref[rows, :] * geo.mask(start, 16, width, count) * (part * (1.0 + pre * (1.0 - part)))
        g_ref[rows, :] = upstream
        return plain + fold_rows(upstream), scaled + fold_rows(upstream * normed)

    zero = jnp.zeros((8, width), F32)
    plain, scaled = over_rows(geo.rows, 16, activate, (zero, zero))
    g_out.send()
    send_rows(sent, ((jnp.sum(plain, axis=0, keepdims=True), jnp.sum(scaled, axis=0, keepdims=True)),))
    sent.send()
    for line in range(geo.side):
        for column in range(geo.side):
            at = line * geo.line + column * geo.slots
            block_out.ref[0, line, column] = flat[at : at + geo.slots, :].astype(BF16)


def norm_grad(geo, rows_of, z_ref, g_ref, average, inverse, gain, plain, scaled, total, count, out_ref):
    width = z_ref.shape[1]
    step = step_of(width)
    factor = gain * inverse
    plain_part = plain / total
    scaled_part = scaled / total * inverse

    def one(start, carry):
        rows = pl.ds(start, step)
        centered = z_ref[rows, :] - average
        value = factor * (g_ref[rows, :] - plain_part - centered * scaled_part)
        out_ref[rows, :] = (value * geo.mask(start, step, width, count)).astype(out_ref.dtype)
        return carry

    over_rows(rows_of, step, one, 0)


def silu_back(geo, z_ref, average, inverse, gain, offset, g_ref):
    rows_of, width = z_ref.shape
    step = step_of(width)

    def one(start, carry):
        plain, scaled = carry
        rows = pl.ds(start, step)
        normed = (z_ref[rows, :] - average) * inverse
        upstream = g_ref[rows, :] * slope(normed * gain + offset) * geo.mask(start, step, width)
        g_ref[rows, :] = upstream
        return plain + fold_rows(upstream), scaled + fold_rows(upstream * normed)

    zero = jnp.zeros((8, width), F32)
    plain, scaled = over_rows(rows_of, step, one, (zero, zero))
    return jnp.sum(plain, axis=0, keepdims=True), jnp.sum(scaled, axis=0, keepdims=True)


def expand_back(geo, block, two, place, counts, got, g_in, z3, mom3, wide, *rest):
    if two:
        zs, short, z2, mom2, narrow, own, other, dv, dvs, g_out, sums, sent, weight, sem = rest
    else:
        z2, mom2, narrow, own, other, dv, g_out, sums, sent, weight, sem = rest
    section = place[1]
    count = counts[section, place[0]]
    choice = Choice(section, block, own, other, weight, sem.at[0])
    choice.start()
    total = total_of(counts, section, geo.pixels)
    main = dv.shape[1]
    both = summed(got)
    plain, scaled = both[0:1, :main], both[1:2, :main]
    sums[0:1, :] = plain
    sums[1:2, :] = scaled
    g_ref = g_in.get()
    norm_grad(
        geo, geo.rows, z3.get(), g_ref, mom3[0:1, :], mom3[1:2, :], wide[0:1, :], plain, scaled, total, count, dv.ref
    )
    dv.send()
    choice.wait()
    g_out.ref[...] = dot_back(dv.ref[...], weight[...])
    send_rows(
        sent,
        (silu_back(geo, z2.get(), mom2[0:1, :], mom2[1:2, :], narrow[1:2, :], narrow[3:4, :], g_out.ref),),
    )
    sent.send()
    g_out.send()
    if two:
        scaled = jnp.concatenate([both[0:1, main:], both[1:2, main:]], axis=1)
        sums[2:3, :] = scaled
        norm_grad(
            geo, geo.rows, zs.get(), g_ref, mom3[2:3, :], mom3[3:4, :], short[0:1, :], plain, scaled, total, count,
            dvs.ref,
        )
        dvs.send()


def tap_back(geo, planes, block, place, counts, got, g_in, z2, mom2, narrow, z1, mom1, own, other, dv, g_out, sums, sent,
             wide_dv, weight, sem):
    section = place[1]
    count = counts[section, place[0]]
    choice = Choice(section, block, own, other, weight, sem.at[0])
    choice.start()
    total = total_of(counts, section, geo.pixels)
    both = summed(got)
    plain, scaled = both[0:1, :], both[1:2, :]
    sums[0:1, :] = plain
    sums[1:2, :] = scaled
    norm_grad(
        geo, geo.rows, z2.get(), g_in.get(), mom2[0:1, :], mom2[1:2, :], narrow[1:2, :], plain, scaled, total, count,
        wide_dv,
    )
    dv.ref[...] = wide_dv[...].astype(BF16)
    dv.send()
    choice.wait()
    g_ref = g_out.ref
    width = g_ref.shape[1]
    ready = {}
    totals = [None] * planes
    for tap, (plane, line, column) in enumerate(taps_of(2 if planes == 4 else 1)):
        if column not in ready:
            values = wide_dv[...]
            if column != 0:
                values = pltpu.roll(values, (column * geo.slots) % geo.rows, 0)
            ready[column] = values.astype(BF16)
        left = turned(ready[column], line * geo.line)
        product = dot_back(left, weight[tap * width : (tap + 1) * width, :])
        totals[plane] = product if totals[plane] is None else totals[plane] + product
    for plane in range(planes):
        g_ref[plane * geo.rows : (plane + 1) * geo.rows, :] = totals[plane]
    send_rows(
        sent,
        (silu_back(geo, z1.get(), mom1[0:1, :], mom1[1:2, :], narrow[0:1, :], narrow[2:3, :], g_ref),),
    )


def join_back(geo, place, counts, got, g_in, u1, mom4, narrow, weight, g3, z3, zs, mom3, wide, short, dv, g_out, sums,
              sent):
    section = place[1]
    count = counts[section, place[0]]
    total = total_of(counts, section, geo.pixels)
    both = summed(got)
    plain, scaled = both[0:1, :], both[1:2, :]
    sums[0:1, :] = plain
    sums[1:2, :] = scaled
    norm_grad(
        geo, geo.rows, u1.get(), g_in.get(), mom4[0:1, :], mom4[1:2, :], narrow[0:1, :], plain, scaled, total, count,
        dv.ref,
    )
    dv.send()
    g_ref = g_out.ref
    g_ref[...] = dot_back(dv.ref[...], weight.get()[...])
    average_c, inverse_c = mom3[0:1, :], mom3[1:2, :]
    average_s, inverse_s = mom3[2:3, :], mom3[3:4, :]
    gain_c, gain_s = wide[0:1, :], short[0:1, :]
    offset = wide[1:2, :] + short[1:2, :]
    width = g_ref.shape[1]
    g3, z3, zs = g3.get(), z3.get(), zs.get()

    def one(start, carry):
        plain, scaled_c, scaled_s = carry
        rows = pl.ds(start, 16)
        normed_c = (z3[rows, :] - average_c) * inverse_c
        normed_s = (zs[rows, :] - average_s) * inverse_s
        arrived = (g_ref[rows, :] + g3[rows, :]).astype(BF16).astype(F32)
        upstream = arrived * slope(normed_c * gain_c + normed_s * gain_s + offset) * geo.mask(start, 16, width)
        g_ref[rows, :] = upstream
        return (
            plain + fold_rows(upstream),
            scaled_c + fold_rows(upstream * normed_c),
            scaled_s + fold_rows(upstream * normed_s),
        )

    zero = jnp.zeros((8, width), F32)
    results = over_rows(geo.rows, 16, one, (zero, zero, zero))
    g_out.send()
    plain, scaled_c, scaled_s = [jnp.sum(value, axis=0, keepdims=True) for value in results]
    half = width // 2
    send_short(
        sent,
        jnp.concatenate(
            [
                jnp.concatenate([plain, scaled_s[:, :half]], axis=1),
                jnp.concatenate([scaled_c, scaled_s[:, half:]], axis=1),
            ],
            axis=0,
        ),
    )


def reduce_back(geo, place, counts, got, g_in, z1, mom1, narrow, dv, sums):
    section = place[1]
    count = counts[section, place[0]]
    total = total_of(counts, section, geo.pixels * 4)
    both = summed(got)
    plain, scaled = both[0:1, :], both[1:2, :]
    sums[0:1, :] = plain
    sums[1:2, :] = scaled
    norm_grad(
        geo, 4 * geo.rows, z1.get(), g_in.get(), mom1[0:1, :], mom1[1:2, :], narrow[0:1, :], plain, scaled, total, count,
        dv.ref,
    )


def image_kernel(geo, dv, weight, dvs, weight_s, image_grad, flat):
    dv, weight = dv.get(), weight.get()
    for plane in (1, 2, 3, 0):
        at = plane * geo.rows
        product = dot_back(dv[at : at + geo.rows, :], weight[...])
        if plane == 0:
            product = product + dot_back(dvs.get()[...], weight_s.get()[...])
        flat[at : at + geo.rows, :] = product
        for line in range(geo.side):
            for column in range(geo.side):
                row = at + line * geo.line + column * geo.slots
                image_grad.ref[0, 2 * line + plane // 2, 2 * column + plane % 2] = flat[
                    row : row + geo.slots, :
                ].astype(BF16)


def exchange(sent):
    return lax.all_to_all(sent, "dp", 0, 0)


def swapped(value):
    return lax.ppermute(value, "section", [(0, 1), (1, 0)])


def across(value, mask):
    return lax.ppermute(value, "dp", [(i, i ^ mask) for i in range(lax.axis_size("dp"))])


class Piece:
    def __init__(self, rows, columns, devices, split, width):
        self.split = split
        self.width = width
        self.rows = rows // 2 if split == "rows" else rows
        self.columns = columns if split == "rows" else columns // 2
        self.height = self.rows // devices
        self.folded = self.columns < width
        self.lines = self.height // 2 if self.folded else self.height * (self.columns // width)

    def product(self, section, left, right):
        pixels = right.shape[0]
        if self.split == "rows":
            half = pl.ds(pl.multiple_of(section * self.rows, self.rows), self.rows)
            return dot_rows(left[0:pixels, half], right[...])
        half = pl.ds(pl.multiple_of(section * self.columns, self.columns), self.columns)
        return dot_rows(left[0:pixels, :], right[:, half])

    def blocks(self):
        if self.folded:
            half = self.height // 2
            return [(0, 0, half, self.columns, 0, 0), (half, 0, half, self.columns, 0, self.columns)]
        return [
            (0, block * self.width, self.height, self.width, block * self.height, 0)
            for block in range(self.columns // self.width)
        ]


def pieces_kernel(pieces, place, *refs):
    count = len(pieces)
    inputs = refs[: 4 * count]
    send_left, keep_left, send_right, keep_right, total = refs[4 * count :]
    me, section = place[0], place[1]
    half = send_left.shape[3]
    devices = 4 * send_left.shape[1]
    line = 0
    for number, piece in enumerate(pieces):
        left, left_other, right, right_other = [
            one.get() if isinstance(one, Late) else one for one in inputs[4 * number : 4 * number + 4]
        ]
        total[0 : piece.rows, 0 : piece.columns] = piece.product(section, left, right) + piece.product(
            section, left_other, right_other
        )
        for step in range(devices):
            first, second = step & 1, (step >> 1) & 1
            for row, column, height, width, at, lane in piece.blocks():
                start = pl.multiple_of((me ^ step) * piece.height, piece.height) + row
                value = total[pl.ds(start, height), column : column + width].astype(BF16)
                to = slice(line + at, line + at + height)
                for start_lane in range(0, width, half):
                    part = value[:, start_lane : start_lane + half]
                    if lane + start_lane < half:
                        (send_left if first else keep_left).ref[second, step >> 2, to, :] = part
                    else:
                        (send_right if second else keep_right).ref[first, step >> 2, to, :] = part
        line += piece.lines


class Reduction:
    def __init__(self, place, pieces, factors, helds=None):
        devices = lax.axis_size("dp")
        helds = helds or (False,) * len(pieces)
        lines = sum(piece.lines for piece in pieces)
        shape = spec((2, devices // 4, lines, pieces[0].width // 2), BF16)
        self.pieces = pieces
        args = [place]
        for four in factors:
            args += four
        tall = max(piece.rows for piece in pieces)
        wide = max(piece.columns for piece in pieces)
        send_left, keep_left, send_right, keep_right = stage(
            lambda *refs: pieces_kernel(pieces, *refs),
            (shape,) * 4,
            "dddd",
            args,
            "s" + "".join("dddg" if held else "dddd" for held in helds),
            (pltpu.VMEM((tall, wide), F32),),
        )
        self.sent = (send_left, send_right)
        self.rest = (keep_left, keep_right)
        self.masks = (1, 2)
        self.step = 1

    def advance(self):
        self.step += 1
        if self.step == 2:
            self.sent = tuple(rest[1] + got[1] for rest, got in zip(self.rest, self.got))
            self.rest = tuple(rest[0] + got[0] for rest, got in zip(self.rest, self.got))
            self.masks = (2, 1)
        else:
            total = jnp.concatenate([rest + got for rest, got in zip(self.rest, self.got)], axis=-1)
            self.rest = (total[0],)
            self.sent = tuple(total[number] for number in range(1, total.shape[0]))
            self.masks = tuple(number << 2 for number in range(1, total.shape[0]))

    def fly(self):
        self.got = tuple(across(value, mask) for value, mask in zip(self.sent, self.masks))

    def finish(self):
        total = self.rest[0].astype(F32)
        for value in self.got:
            total = total + value.astype(F32)
        results = []
        line = 0
        for piece in self.pieces:
            blocks = [
                total[line + at : line + at + height, lane : lane + width]
                for _, _, height, width, at, lane in piece.blocks()
            ]
            results.append(
                blocks[0] if len(blocks) == 1 else jnp.concatenate(blocks, axis=0 if piece.folded else 1)
            )
            line += piece.lines
        return results


def body(
    images,
    out_grad,
    live_counts,
    w_reduce0,
    w_short,
    short_gain,
    short_bias,
    w_reduce1,
    w_mid,
    w_expand,
    gain_narrow,
    bias_narrow,
    gain_wide,
    bias_wide,
):
    section = lax.axis_index("section")
    dp_index = lax.axis_index("dp")
    devices = lax.axis_size("dp")
    slots = images.shape[1]
    side = images.shape[2] // 2
    geo = Geometry(slots, side)
    c_in = images.shape[4]
    mid = w_mid.shape[2]
    out = w_expand.shape[2]
    rows = geo.rows
    all_rows = 4 * rows
    place = jnp.stack([dp_index, section]).astype(jnp.int32)

    def bound(kernel, *fixed):
        def run(*refs):
            kernel(geo, *fixed, *refs)

        return run

    own_narrow = jnp.concatenate([gain_narrow[0], bias_narrow[0]], axis=0)
    own_wide = jnp.concatenate([gain_wide, bias_wide], axis=0)
    mid_other = swapped(w_mid)
    expand_other = swapped(w_expand)
    other_narrow = swapped(own_narrow)
    other_wide = swapped(own_wide)
    front = section == 0
    narrow0 = jnp.where(front, own_narrow, other_narrow)
    narrow1 = jnp.where(front, other_narrow, own_narrow)
    wide0 = jnp.where(front, own_wide, other_wide)
    wide1 = jnp.where(front, other_wide, own_wide)
    short = jnp.stack([short_gain, short_bias])
    counts = live_counts.T
    images = images.transpose(0, 2, 3, 1, 4)
    out_grad = out_grad.transpose(0, 2, 3, 1, 4)

    def dma(number):
        return pltpu.SemaphoreType.DMA((number,))

    piece_mid = Piece(9 * mid, mid, devices, "columns", mid)
    piece_expand = Piece(mid, out, devices, "columns", mid)
    piece_reduce1 = Piece(out, mid, devices, "rows", mid)
    piece_short = Piece(c_in, out, devices, "rows", mid)
    piece_reduce0 = Piece(c_in, mid, devices, "rows", mid)
    heights = [block[2] for piece in (piece_mid, piece_expand, piece_reduce1, piece_short, piece_reduce0) for block in piece.blocks()]
    packed = devices == 16 and all(height % 16 == 0 for height in heights)

    def partner(value, got):
        if not packed:
            return got, value
        return lax.optimization_barrier((got, swapped(value)))

    x, z1, sent = stage(
        bound(first_kernel),
        (spec((all_rows, c_in), BF16), spec((all_rows, mid)), spec((devices, 2, mid))),
        "ddd",
        (place, counts, images, w_reduce0),
        "ssad",
        (
            pltpu.VMEM((2 * side, 2 * side, slots, c_in), BF16),
            pltpu.VMEM((4, geo.line, c_in), F32),
            dma(1),
        ),
    )
    got = exchange(sent)
    zs, stats_s = stage(
        bound(short_kernel),
        (spec((rows, out)), spec((2, out))),
        "dd",
        (place, counts, x, w_short),
        "ssad",
        (pltpu.VMEM((rows, c_in), BF16), dma(1)),
    )
    tap_scratch = (pltpu.VMEM((9 * mid, mid), BF16), dma(1))
    taps0, z2, mom1, sent = stage(
        bound(tap_kernel, 4, 0),
        (spec((rows, 9 * mid), BF16), spec((rows, mid)), spec((2, mid)), spec((devices, 2, 3 * (mid + out) // 2), BF16)),
        "dddd",
        (place, counts, got, z1, narrow0, w_mid, mid_other, stats_s),
        "ssgddaad",
        (pltpu.VMEM((all_rows, mid), F32),) + tap_scratch,
    )
    got = exchange(sent)
    got, x_other = partner(x, got)
    expand_scratch = (pltpu.VMEM((mid, out), BF16), dma(1))
    a2, z3, mom2, moments_s, sent = stage(
        bound(expand_kernel, 0, True),
        (spec((rows, mid), BF16), spec((rows, out)), spec((2, mid)), spec((2, out)), spec((devices, 2, out))),
        "ddddd",
        (place, counts, got, z2, narrow0, w_expand, expand_other),
        "ssgddaa",
        expand_scratch,
    )
    got = exchange(sent)
    got, taps0_other = partner(taps0, got)
    joined, u1, mom3, sent = stage(
        bound(join_kernel),
        (spec((rows, out), BF16), spec((rows, mid)), spec((4, out)), spec((devices, 2, mid))),
        "dddd",
        (place, counts, got, z3, zs, moments_s, wide0, short, w_reduce1),
        "ssgdddddd",
    )
    got = exchange(sent)
    got, a2_other = partner(a2, got)
    taps1, u2, mom4, sent = stage(
        bound(tap_kernel, 1, 1),
        (spec((rows, 9 * mid), BF16), spec((rows, mid)), spec((2, mid)), spec((devices, 2, mid))),
        "dddd",
        (place, counts, got, u1, narrow1, w_mid, mid_other),
        "ssgddaa",
        (pltpu.VMEM((rows, mid), F32),) + tap_scratch,
    )
    got = exchange(sent)
    got, joined_other = partner(joined, got)
    c2, u3, mom5, sent = stage(
        bound(expand_kernel, 1, False),
        (spec((rows, mid), BF16), spec((rows, out)), spec((2, mid)), spec((devices, 2, out))),
        "dddd",
        (place, counts, got, u2, narrow1, w_expand, expand_other),
        "ssgddaa",
        expand_scratch,
    )
    got = exchange(sent)
    got, taps1_other = partner(taps1, got)
    block_out, g3, mom6, sent = stage(
        bound(turn_kernel),
        (
            spec((1, side, side, slots, out), BF16),
            spec((rows, out)),
            spec((2, out)),
            spec((devices, 2, out)),
        ),
        "dddd",
        (place, counts, got, u3, joined, wide1, out_grad),
        "ssgddda",
        (pltpu.VMEM((side, side, slots, out), BF16), pltpu.VMEM((rows, out), F32), dma(1)),
    )
    got = exchange(sent)
    got, c2_other = partner(c2, got)
    du3, g2, sums6, sent = stage(
        bound(expand_back, 1, False),
        (spec((rows, out), BF16), spec((rows, mid)), spec((2, out)), spec((devices, 2, mid))),
        "dddd",
        (place, counts, got, g3, u3, mom6, wide1, u2, mom5, narrow1, w_expand, expand_other),
        "ssgdddddddaa",
        expand_scratch,
    )
    got = exchange(sent)
    got, du3_other = partner(du3, got)
    tap_back_scratch = (pltpu.VMEM((rows, mid), F32),) + tap_scratch
    du2, g1, sums5, sent = stage(
        bound(tap_back, 1, 1),
        (spec((rows, mid), BF16), spec((rows, mid)), spec((2, mid)), spec((devices, 2, mid))),
        "dddd",
        (place, counts, got, g2, u2, mom5, narrow1, u1, mom4, w_mid, mid_other),
        "ssgddddddaa",
        tap_back_scratch,
    )
    got = exchange(sent)
    def tied(value, starting=(), arrived=()):
        values = lax.optimization_barrier(
            (value, tuple(one.sent for one in starting), tuple(one.got for one in arrived))
        )
        for one, sent in zip(starting, values[1]):
            one.sent = sent
            one.fly()
        for one, got in zip(arrived, values[2]):
            one.got = got
        return values[0]

    if packed:
        first = Reduction(
            place,
            (piece_expand, piece_mid),
            ((c2, c2_other, du3, du3_other), (taps1, taps1_other, du2, swapped(du2))),
            (False, True),
        )
        got = tied(got, (first,))
    du1, gj, sums4, sent = stage(
        bound(join_back),
        (spec((rows, mid), BF16), spec((rows, out)), spec((2, mid)), spec((devices, 2, out + out // 2), BF16)),
        "dddd",
        (place, counts, got, g1, u1, mom4, narrow1, w_reduce1, g3, z3, zs, mom3, wide0, short),
        "ssgddddddddddd",
    )
    got = exchange(sent)
    got, du1_other = partner(du1, got)
    if packed:
        first.advance()
        got = tied(got, (first,))
    dz3, dzs, g2, sums3, sent = stage(
        bound(expand_back, 0, True),
        (
            spec((rows, out), BF16),
            spec((rows, out), BF16),
            spec((rows, mid)),
            spec((3, out)),
            spec((devices, 2, mid)),
        ),
        "ddddd",
        (place, counts, got, gj, z3, mom3, wide0, zs, short, z2, mom2, narrow0, w_expand, expand_other),
        "ssgdddddddddaa",
        expand_scratch,
    )
    got = exchange(sent)
    if packed:
        second = Reduction(
            place,
            (piece_reduce1, piece_expand, piece_short),
            (
                (joined, joined_other, du1, du1_other),
                (a2, a2_other, dz3, swapped(dz3)),
                (x, x_other, dzs, swapped(dzs)),
            ),
            (False, True, True),
        )
        got = tied(got, (second,), (first,))
    dz2, g1, sums2, sent = stage(
        bound(tap_back, 4, 0),
        (spec((rows, mid), BF16), spec((all_rows, mid)), spec((2, mid)), spec((devices, 2, mid))),
        "dddd",
        (place, counts, got, g2, z2, mom2, narrow0, z1, mom1, w_mid, mid_other),
        "ssgddddddaa",
        tap_back_scratch,
    )
    got = exchange(sent)
    got, dz2_other = partner(dz2, got)
    if packed:
        second.advance()
        first.advance()
        got = tied(got, (second, first))
    dz1, sums1 = stage(
        bound(reduce_back),
        (spec((all_rows, mid), BF16), spec((2, mid))),
        "dd",
        (place, counts, got, g1, z1, mom1, narrow0),
        "ssgdddd",
    )
    if packed:
        third = Reduction(
            place,
            (piece_mid, piece_reduce0),
            ((taps0, taps0_other, dz2, dz2_other), (x, x_other, dz1, swapped(dz1))),
        )
        dz1 = tied(dz1, (third,), (second,))
        second.advance()
        dz1 = tied(dz1, (second,), (first,))
    wide_front = sums3[:2]
    wide_sent = jnp.concatenate([jnp.where(front, sums6, wide_front), sums3[0:1], sums3[2:3]], axis=0)
    front_narrow = jnp.stack([sums1, sums2])
    back_narrow = jnp.stack([sums4, sums5])
    narrow_sent = jnp.where(front, back_narrow, front_narrow)
    dz1, wide_sent, narrow_sent = lax.optimization_barrier((dz1, wide_sent, narrow_sent))
    wide_got = swapped(wide_sent)
    narrow_got = swapped(narrow_sent)
    (image_grad,) = stage(
        bound(image_kernel),
        (spec((1, 2 * side, 2 * side, slots, c_in), BF16),),
        "d",
        (dz1, w_reduce0, dzs, w_short),
        "dddd",
        (pltpu.VMEM((all_rows, c_in), F32),),
    )
    block_out = block_out.transpose(0, 3, 1, 2, 4)
    image_grad, wide_got, narrow_got = lax.optimization_barrier((image_grad, wide_got, narrow_got))
    wide_sums = jnp.where(front, wide_front, sums6) + wide_got[:2]
    width = out // (2 * devices)
    both_short = jnp.stack([sums3[2] + wide_got[3], sums3[0] + wide_got[2]])
    short_norm = lax.dynamic_slice_in_dim(both_short, (section * devices + dp_index) * width, width, 1)
    narrow_sums = jnp.where(front, front_narrow, back_narrow) + narrow_got
    if packed:
        expand1, mid1 = first.finish()
        image_grad = tied(image_grad, (), (third,))
        third.advance()
        image_grad = tied(image_grad, (third,))
        image_grad = tied(image_grad, (), (third,))
        third.advance()
        image_grad = tied(image_grad, (third,))
        reduce1, expand0, short_grad = second.finish()
        image_grad = tied(image_grad, (), (third,))
        mid0, reduce0 = third.finish()

        def to_owner(front_half, back_half, axis):
            mine = jnp.where(front, front_half, back_half)
            other = swapped(jnp.where(front, back_half, front_half))
            first_half = jnp.where(front, mine, other)
            second_half = jnp.where(front, other, mine)
            return jnp.concatenate([first_half, second_half], axis=axis)

        grad_mid = to_owner(mid0, mid1, 1)
        grad_expand = to_owner(expand0, expand1, 1)
    else:

        def product(left, right):
            return dot_rows(left, right).astype(BF16)

        def of_block(front_grad, back_grad):
            mine = jnp.where(front, front_grad, back_grad)
            both = mine + swapped(jnp.where(front, back_grad, front_grad))
            return lax.psum_scatter(both, "dp", scatter_dimension=0, tiled=True).astype(F32)

        def of_both(grad):
            return lax.psum_scatter(grad, ("section", "dp"), scatter_dimension=0, tiled=True).astype(F32)

        grad_mid = of_block(product(taps0, dz2), product(taps1, du2))
        grad_expand = of_block(product(a2, dz3), product(c2, du3))
        reduce1 = of_both(product(joined, du1))
        short_grad = of_both(product(x[:rows], dzs))
        reduce0 = of_both(product(x, dz1))
    return (
        block_out,
        image_grad.transpose(0, 3, 1, 2, 4),
        reduce0,
        short_grad,
        short_norm,
        reduce1,
        grad_mid[None],
        grad_expand[None],
        narrow_sums[None, :, 1],
        narrow_sums[None, :, 0],
        wide_sums[None, 1],
        wide_sums[None, 0],
    )


def solution(mesh):
    return jax.shard_map(
        body,
        mesh=mesh,
        in_specs=(
            P(None, "dp", None, None, None),
            P(None, "dp", None, None, None),
            P(),
            P(),
            P(),
            P(),
            P(),
            P(),
            P("section", None, None),
            P("section", None, None),
            P("section", None, None),
            P("section", None, None),
            P("section", None),
            P("section", None),
        ),
        out_specs=(
            P("section", "dp", None, None, None),
            P("section", "dp", None, None, None),
            P(("section", "dp"), None),
            P(("section", "dp"), None),
            P(None, ("section", "dp")),
            P(("section", "dp"), None),
            P("section", "dp", None),
            P("section", "dp", None),
            P("section", None, None),
            P("section", None, None),
            P("section", None),
            P("section", None),
        ),
        check_vma=False,
    )
```

profile of v0, /device:TPU:9, one launch (start us, length us, event | category | flops | bytes accessed | tf_op | source)
XLA Modules:
  0.0 339.9 jit_solution(3027060176128629513)
XLA Ops:
  2.0 6.3 %shard_map.229 = (bf16[1024,1024]{1,0:T(8,128)(2,1)}, f32[1024,512]{1,0:T(8,128)}, f32[16,2,512]{2,1,0:T(2,128)}) custom-call(s32[2]{0:T(128)} %pad_add_fusion.refs_0_, s32[2,16]{1,0:T(2,128)} %bitcast.91, bf16[2,14,14,4,1024]{4,3,2,1,0:T(4,128)(2,1)} %bitcast.88, bf16[1024,512]{1,0:T(8,128)(2,1)} %refs_1_.1), custom_call_target="tpu_custom_call" | custom-call | tf_op jit(solution)/shard_map/pallas_call | solution.py:87
  9.1 6.7 %all-to-all-start = ((f32[16,2,512]{2,1,0:T(2,128)}), f32[16,2,512]{2,1,0:T(2,128)S(1)}, u32[]{:S(2)}, u32[]{:S(2)}) async-start(f32[16,2,512]{2,1,0:T(2,128)} %get-tuple-element.147), calls=%async_computation | async-start | bytes 131072 | tf_op jit(solution)/shard_map/all_to_all | solution.py:690
  15.7 5.7 %shard_map.230 = (f32[256,2048]{1,0:T(8,128)}, f32[2,2048]{1,0:T(2,128)}) custom-call(s32[2]{0:T(128)} %pad_add_fusion.refs_0_, s32[2,16]{1,0:T(2,128)} %bitcast.92, bf16[1024,1024]{1,0:T(8,128)(2,1)} %get-tuple-element.149.refs_2_.refs_9_.refs_5_, bf16[1024,2048]{1,0:T(8,128)(2,1)} %refs_3_.5), custom_call_target="tpu_custom_call" | custom-call | tf_op jit(solution)/shard_map/pallas_call | solution.py:87
  22.1 6.3 %shard_map.231 = (bf16[256,4608]{1,0:T(8,128)(2,1)}, f32[256,512]{1,0:T(8,128)}, f32[2,512]{1,0:T(2,128)}, bf16[16,2,3840]{2,1,0:T(2,128)(2,1)}) custom-call(s32[2]{0:T(128)} %pad_add_fusion.refs_0_, s32[2,16]{1,0:T(2,128)} %bitcast.93, f32[16,2,512]{2,1,0:T(2,128)S(1)} %all-to-all-done.refs_2_, f32[1024,512]{1,0:T(8,128)} %get-tuple-element.148.refs_3_.refs_7_.refs_4_, ...), custom_call_target="tpu_custom_call" | custom-call | tf_op jit(solution)/shard_map/pallas_call | solution.py:87
  29.5 6.4 %all-to-all-start.1 = ((bf16[16,2,3840]{2,1,0:T(2,128)(2,1)}), bf16[16,2,3840]{2,1,0:T(2,128)(2,1)S(1)}, u32[]{:S(2)}, u32[]{:S(2)}) async-start(bf16[16,2,3840]{2,1,0:T(2,128)(2,1)} %get-tuple-element.151), calls=%async_computation.1 | async-start | bytes 491520 | tf_op jit(solution)/shard_map/all_to_all | solution.py:690
  36.5 6.7 %all-to-all-done.1.refs_2_ = bf16[16,2,3840]{2,1,0:T(2,128)(2,1)S(1)} async-done(((bf16[16,2,3840]{2,1,0:T(2,128)(2,1)}), bf16[16,2,3840]{2,1,0:T(2,128)(2,1)S(1)}, u32[]{:S(2)}, u32[]{:S(2)}) %all-to-all-start.1) | async-done | bytes 245792 | tf_op jit(solution)/shard_map/all_to_all | solution.py:690
  43.2 5.1 %shard_map.232 = (bf16[256,512]{1,0:T(8,128)(2,1)}, f32[256,2048]{1,0:T(8,128)}, f32[2,512]{1,0:T(2,128)}, f32[2,2048]{1,0:T(2,128)}, f32[16,2,2048]{2,1,0:T(2,128)}) custom-call(s32[2]{0:T(128)} %pad_add_fusion.refs_0_, s32[2,16]{1,0:T(2,128)} %bitcast.94, bf16[16,2,3840]{2,1,0:T(2,128)(2,1)S(1)} %all-to-all-done.1.refs_2_, ...), custom_call_target="tpu_custom_call" | custom-call | tf_op jit(solution)/shard_map/pallas_call | solution.py:87
  48.2 5.4 %all-to-all-start.2 = ((f32[16,2,2048]{2,1,0:T(2,128)}), f32[16,2,2048]{2,1,0:T(2,128)S(1)}, u32[]{:S(2)}, u32[]{:S(2)}) async-start(f32[16,2,2048]{2,1,0:T(2,128)} %get-tuple-element.154), calls=%async_computation.2 | async-start | bytes 524288 | tf_op jit(solution)/shard_map/all_to_all | solution.py:690
  54.2 1.6 collective-permute-start.6
  56.4 4.0 %all-to-all-done.2.refs_2_ = f32[16,2,2048]{2,1,0:T(2,128)S(1)} async-done(((f32[16,2,2048]{2,1,0:T(2,128)}), f32[16,2,2048]{2,1,0:T(2,128)S(1)}, u32[]{:S(2)}, u32[]{:S(2)}) %all-to-all-start.2) | async-done | bytes 262176 | tf_op jit(solution)/shard_map/all_to_all | solution.py:690
  60.5 6.1 %shard_map.233 = (bf16[256,2048]{1,0:T(8,128)(2,1)}, f32[256,512]{1,0:T(8,128)}, f32[4,2048]{1,0:T(4,128)}, f32[16,2,512]{2,1,0:T(2,128)}) custom-call(s32[2]{0:T(128)} %pad_add_fusion.refs_0_, s32[2,16]{1,0:T(2,128)} %bitcast.95, f32[16,2,2048]{2,1,0:T(2,128)S(1)} %all-to-all-done.2.refs_2_, f32[256,2048]{1,0:T(8,128)} %get-tuple-element.157.refs_3_.refs_9_.refs_4_, ...), custom_call_target="tpu_custom_call" | custom-call | tf_op jit(solution)/shard_map/pallas_call | solution.py:87
  66.6 5.9 %all-to-all-start.3 = ((f32[16,2,512]{2,1,0:T(2,128)}), f32[16,2,512]{2,1,0:T(2,128)S(1)}, u32[]{:S(2)}, u32[]{:S(2)}) async-start(f32[16,2,512]{2,1,0:T(2,128)} %get-tuple-element.160), calls=%async_computation.3 | async-start | bytes 131072 | tf_op jit(solution)/shard_map/all_to_all | solution.py:690
  72.5 5.4 %all-to-all-done.3.refs_2_ = f32[16,2,512]{2,1,0:T(2,128)S(1)} async-done(((f32[16,2,512]{2,1,0:T(2,128)}), f32[16,2,512]{2,1,0:T(2,128)S(1)}, u32[]{:S(2)}, u32[]{:S(2)}) %all-to-all-start.3) | async-done | bytes 65568 | tf_op jit(solution)/shard_map/all_to_all | solution.py:690
  77.9 5.9 %shard_map.234 = (bf16[256,4608]{1,0:T(8,128)(2,1)}, f32[256,512]{1,0:T(8,128)}, f32[2,512]{1,0:T(2,128)}, f32[16,2,512]{2,1,0:T(2,128)}) custom-call(s32[2]{0:T(128)} %pad_add_fusion.refs_0_, s32[2,16]{1,0:T(2,128)} %bitcast.96, f32[16,2,512]{2,1,0:T(2,128)S(1)} %all-to-all-done.3.refs_2_, f32[256,512]{1,0:T(8,128)} %get-tuple-element.163.refs_3_.refs_7_.refs_4_, ...), custom_call_target="tpu_custom_call" | custom-call | tf_op jit(solution)/shard_map/pallas_call | solution.py:87
  83.9 2.8 collective-permute-start.8
  86.8 9.9 %all_to_all.60.refs_2_ = f32[16,2,512]{2,1,0:T(2,128)S(1)} all-to-all(f32[16,2,512]{2,1,0:T(2,128)} %get-tuple-element.164), channel_id=1, replica_groups=mesh['section'=2,'dp'=16] {'dp'}, dimensions={0} | all-to-all | bytes 131072 | tf_op jit(solution)/shard_map/all_to_all | solution.py:690
  96.6 4.8 %shard_map.235 = (bf16[256,512]{1,0:T(8,128)(2,1)}, f32[256,2048]{1,0:T(8,128)}, f32[2,512]{1,0:T(2,128)}, f32[16,2,2048]{2,1,0:T(2,128)}) custom-call(s32[2]{0:T(128)} %pad_add_fusion.refs_0_, s32[2,16]{1,0:T(2,128)} %bitcast.97, f32[16,2,512]{2,1,0:T(2,128)S(1)} %all_to_all.60.refs_2_, f32[256,512]{1,0:T(8,128)} %get-tuple-element.167.refs_3_.refs_7_.refs_4_, ...), custom_call_target="tpu_custom_call" | custom-call | tf_op jit(solution)/shard_map/pallas_call | solution.py:87
  101.5 11.3 %all_to_all.61.refs_2_ = f32[16,2,2048]{2,1,0:T(2,128)S(1)} all-to-all(f32[16,2,2048]{2,1,0:T(2,128)} %get-tuple-element.168), channel_id=1, replica_groups=mesh['section'=2,'dp'=16] {'dp'}, dimensions={0} | all-to-all | bytes 524288 | tf_op jit(solution)/shard_map/all_to_all | solution.py:690
  112.7 6.9 %shard_map.236 = (bf16[1,7,7,4,2048]{4,3,2,1,0:T(4,128)(2,1)}, f32[256,2048]{1,0:T(8,128)}, f32[2,2048]{1,0:T(2,128)}, f32[16,2,2048]{2,1,0:T(2,128)}) custom-call(s32[2]{0:T(128)} %pad_add_fusion.refs_0_, s32[2,16]{1,0:T(2,128)} %bitcast.98, f32[16,2,2048]{2,1,0:T(2,128)S(1)} %all_to_all.61.refs_2_, f32[256,2048]{1,0:T(8,128)} %get-tuple-element.171.refs_3_.refs_4_, ...), custom_call_target="tpu_custom_call" | custom-call | tf_op jit(solution)/shard_map/pallas_call | solution.py:87
  119.7 5.8 %all-to-all-start.6 = ((f32[16,2,2048]{2,1,0:T(2,128)}), f32[16,2,2048]{2,1,0:T(2,128)S(1)}, u32[]{:S(2)}, u32[]{:S(2)}) async-start(f32[16,2,2048]{2,1,0:T(2,128)} %get-tuple-element.173), calls=%async_computation.6 | async-start | bytes 524288 | tf_op jit(solution)/shard_map/all_to_all | solution.py:690
  125.5 2.1 collective-permute-start.9
  128.7 3.5 %all-to-all-done.6.refs_2_ = f32[16,2,2048]{2,1,0:T(2,128)S(1)} async-done(((f32[16,2,2048]{2,1,0:T(2,128)}), f32[16,2,2048]{2,1,0:T(2,128)S(1)}, u32[]{:S(2)}, u32[]{:S(2)}) %all-to-all-start.6) | async-done | bytes 262176 | tf_op jit(solution)/shard_map/all_to_all | solution.py:690
  132.2 5.9 %shard_map.237 = (bf16[256,2048]{1,0:T(8,128)(2,1)}, f32[256,512]{1,0:T(8,128)}, f32[2,2048]{1,0:T(2,128)}, f32[16,2,512]{2,1,0:T(2,128)}) custom-call(s32[2]{0:T(128)} %pad_add_fusion.refs_0_, s32[2,16]{1,0:T(2,128)} %bitcast.99, f32[16,2,2048]{2,1,0:T(2,128)S(1)} %all-to-all-done.6.refs_2_, f32[256,2048]{1,0:T(8,128)} %get-tuple-element.176.refs_3_.refs_8_, ...), custom_call_target="tpu_custom_call" | custom-call | tf_op jit(solution)/shard_map/pallas_call | solution.py:87
  138.2 3.6 %collective-permute-start.10 = (bf16[256,2048]{1,0:T(8,128)(2,1)}, bf16[256,2048]{1,0:T(8,128)(2,1)S(1)}, u32[]{:S(2)}, u32[]{:S(2)}) collective-permute-start(bf16[256,2048]{1,0:T(8,128)(2,1)} %get-tuple-element.180.refs_3_), channel_id=1, source_target_pairs={{0,16},{16,0},{1,17},{17,1},{2,18},{18,2},{3,19},{19,3},{4,20},{20... | collective-permute-start | bytes 3145736 | tf_op jit(solution)/shard_map/ppermute | solution.py:694
  141.8 9.6 %all_to_all.62.refs_2_ = f32[16,2,512]{2,1,0:T(2,128)S(1)} all-to-all(f32[16,2,512]{2,1,0:T(2,128)} %get-tuple-element.179), channel_id=1, replica_groups=mesh['section'=2,'dp'=16] {'dp'}, dimensions={0} | all-to-all | bytes 131072 | tf_op jit(solution)/shard_map/all_to_all | solution.py:690
  151.4 6.4 %shard_map.238 = (bf16[256,512]{1,0:T(8,128)(2,1)}, f32[256,512]{1,0:T(8,128)}, f32[2,512]{1,0:T(2,128)}, f32[16,2,512]{2,1,0:T(2,128)}) custom-call(s32[2]{0:T(128)} %pad_add_fusion.refs_0_, s32[2,16]{1,0:T(2,128)} %bitcast.100, f32[16,2,512]{2,1,0:T(2,128)S(1)} %all_to_all.62.refs_2_, f32[256,512]{1,0:T(8,128)} %get-tuple-element.182.refs_3_, ...), custom_call_target="tpu_custom_call" | custom-call | tf_op jit(solution)/shard_map/pallas_call | solution.py:87
  157.8 1.3 collective-permute-start.11
  159.1 4.4 %all-to-all-start.8 = ((f32[16,2,512]{2,1,0:T(2,128)}), f32[16,2,512]{2,1,0:T(2,128)S(1)}, u32[]{:S(2)}, u32[]{:S(2)}) async-start(f32[16,2,512]{2,1,0:T(2,128)} %get-tuple-element.184), calls=%async_computation.8 | async-start | bytes 131072 | tf_op jit(solution)/shard_map/all_to_all | solution.py:690
  163.5 7.2 %shard_map.239 = (bf16[2,4,208,256]{3,2,1,0:T(8,128)(2,1)}, bf16[2,4,208,256]{3,2,1,0:T(8,128)(2,1)}, bf16[2,4,208,256]{3,2,1,0:T(8,128)(2,1)}, bf16[2,4,208,256]{3,2,1,0:T(8,128)(2,1)}) custom-call(s32[2]{0:T(128)} %pad_add_fusion.refs_0_, bf16[256,512]{1,0:T(8,128)(2,1)} %get-tuple-element.174.refs_1_, bf16[256,512]{1,0:T(8,128)(2,1)} %copy-done.17, ...), custom_call_target="tpu_custom_call" | custom-call | tf_op jit(solution)/shard_map/pallas_call | solution.py:87
  170.7 1.3 collective-permute-start.13
  173.2 8.8 %shard_map.240 = (bf16[256,512]{1,0:T(8,128)(2,1)}, f32[256,2048]{1,0:T(8,128)}, f32[2,512]{1,0:T(2,128)}, bf16[16,2,3072]{2,1,0:T(2,128)(2,1)}) custom-call(s32[2]{0:T(128)} %pad_add_fusion.refs_0_, s32[2,16]{1,0:T(2,128)} %bitcast.101, f32[16,2,512]{2,1,0:T(2,128)S(1)} %all-to-all-done.8.refs_2_, f32[256,512]{1,0:T(8,128)} %get-tuple-element.192.refs_3_, ...), custom_call_target="tpu_custom_call" | custom-call | tf_op jit(solution)/shard_map/pallas_call | solution.py:87
  182.0 4.6 %all-to-all-start.9 = ((bf16[16,2,3072]{2,1,0:T(2,128)(2,1)}), bf16[16,2,3072]{2,1,0:T(2,128)(2,1)S(1)}, u32[]{:S(2)}, u32[]{:S(2)}) async-start(bf16[16,2,3072]{2,1,0:T(2,128)(2,1)} %get-tuple-element.194), calls=%async_computation.9 | async-start | bytes 393216 | tf_op jit(solution)/shard_map/all_to_all | solution.py:690
  186.7 1.4 collective-permute-start.12
  188.1 1.4 collective-permute-done.12.refs_4_
  189.5 4.5 %all-to-all-done.9.refs_2_ = bf16[16,2,3072]{2,1,0:T(2,128)(2,1)S(1)} async-done(((bf16[16,2,3072]{2,1,0:T(2,128)(2,1)}), bf16[16,2,3072]{2,1,0:T(2,128)(2,1)S(1)}, u32[]{:S(2)}, u32[]{:S(2)}) %all-to-all-start.9) | async-done | bytes 196640 | tf_op jit(solution)/shard_map/all_to_all | solution.py:690
  194.0 2.1 fusion.12
  196.1 7.5 %shard_map.241 = (bf16[256,2048]{1,0:T(8,128)(2,1)}, bf16[256,2048]{1,0:T(8,128)(2,1)}, f32[256,512]{1,0:T(8,128)}, f32[3,2048]{1,0:T(4,128)}, f32[16,2,512]{2,1,0:T(2,128)}) custom-call(s32[2]{0:T(128)} %pad_add_fusion.refs_0_, s32[2,16]{1,0:T(2,128)} %bitcast.102, bf16[16,2,3072]{2,1,0:T(2,128)(2,1)S(1)} %all-to-all-done.9.refs_2_, ...), custom_call_target="tpu_custom_call" | custom-call | tf_op jit(solution)/shard_map/pallas_call | solution.py:87
  203.6 1.8 collective-permute-start.15
  207.0 5.5 %all-to-all-start.10 = ((f32[16,2,512]{2,1,0:T(2,128)}), f32[16,2,512]{2,1,0:T(2,128)S(1)}, u32[]{:S(2)}, u32[]{:S(2)}) async-start(f32[16,2,512]{2,1,0:T(2,128)} %get-tuple-element.204), calls=%async_computation.10 | async-start | bytes 131072 | tf_op jit(solution)/shard_map/all_to_all | solution.py:690
  212.5 7.9 %shard_map.242 = (bf16[2,4,256,256]{3,2,1,0:T(8,128)(2,1)}, bf16[2,4,256,256]{3,2,1,0:T(8,128)(2,1)}, bf16[2,4,256,256]{3,2,1,0:T(8,128)(2,1)}, bf16[2,4,256,256]{3,2,1,0:T(8,128)(2,1)}) custom-call(s32[2]{0:T(128)} %pad_add_fusion.refs_0_, bf16[256,2048]{1,0:T(8,128)(2,1)} %get-tuple-element.165.refs_4_.refs_1_, bf16[256,2048]{1,0:T(8,128)(2,1)} %copy-done.3, ...), custom_call_target="tpu_custom_call" | custom-call | tf_op jit(solution)/shard_map/pallas_call | solution.py:87
  220.4 1.3 collective-permute-start.20
  222.9 8.8 %shard_map.243 = (bf16[256,512]{1,0:T(8,128)(2,1)}, f32[1024,512]{1,0:T(8,128)}, f32[2,512]{1,0:T(2,128)}, f32[16,2,512]{2,1,0:T(2,128)}) custom-call(s32[2]{0:T(128)} %pad_add_fusion.refs_0_, s32[2,16]{1,0:T(2,128)} %bitcast.103, f32[16,2,512]{2,1,0:T(2,128)S(1)} %all-to-all-done.10.refs_2_, f32[256,512]{1,0:T(8,128)} %get-tuple-element.216.refs_3_, ...), custom_call_target="tpu_custom_call" | custom-call | tf_op jit(solution)/shard_map/pallas_call | solution.py:87
  231.7 4.6 %all-to-all-start.11 = ((f32[16,2,512]{2,1,0:T(2,128)}), f32[16,2,512]{2,1,0:T(2,128)S(1)}, u32[]{:S(2)}, u32[]{:S(2)}) async-start(f32[16,2,512]{2,1,0:T(2,128)} %get-tuple-element.218), calls=%async_computation.11 | async-start | bytes 131072 | tf_op jit(solution)/shard_map/all_to_all | solution.py:690
  236.3 2.7 collective-permute-start.19
  239.0 1.6 fusion.9
  241.5 4.0 %all-to-all-done.11.refs_2_ = f32[16,2,512]{2,1,0:T(2,128)S(1)} async-done(((f32[16,2,512]{2,1,0:T(2,128)}), f32[16,2,512]{2,1,0:T(2,128)S(1)}, u32[]{:S(2)}, u32[]{:S(2)}) %all-to-all-start.11) | async-done | bytes 65568 | tf_op jit(solution)/shard_map/all_to_all | solution.py:690
  247.9 4.9 %shard_map.244 = (bf16[1024,512]{1,0:T(8,128)(2,1)}, f32[2,512]{1,0:T(2,128)}) custom-call(s32[2]{0:T(128)} %pad_add_fusion.refs_0_, s32[2,16]{1,0:T(2,128)} %bitcast.104, f32[16,2,512]{2,1,0:T(2,128)S(1)} %all-to-all-done.11.refs_2_, f32[1024,512]{1,0:T(8,128)} %get-tuple-element.228.refs_3_, f32[1024,512]{1,0:T(8,128)} %get-tuple-element.148.refs_3_.refs_7_.refs_4_, ...), custom_call_target="tpu_custom_call" | custom-call | tf_op jit(solution)/shard_map/pallas_call | solution.py:87
  252.8 2.8 collective-permute-start.22
  255.6 1.2 collective-permute-start.23
  258.1 2.1 collective-permute-start.26
  260.1 1.3 broadcast_select_fusion.7
  262.4 9.9 %shard_map.245 = (bf16[2,4,176,256]{3,2,1,0:T(8,128)(2,1)}, bf16[2,4,176,256]{3,2,1,0:T(8,128)(2,1)}, bf16[2,4,176,256]{3,2,1,0:T(8,128)(2,1)}, bf16[2,4,176,256]{3,2,1,0:T(8,128)(2,1)}) custom-call(s32[2]{0:T(128)} %pad_add_fusion.refs_0_, bf16[256,4608]{1,0:T(8,128)(2,1)} %get-tuple-element.155.refs_1_, bf16[256,4608]{1,0:T(8,128)(2,1)} %collective-permute-done.4.refs_2_, ...), custom_call_target="tpu_custom_call" | custom-call | tf_op jit(solution)/shard_map/pallas_call | solution.py:87
  274.7 4.2 %collective-permute-done.27 = bf16[208,512]{1,0:T(8,128)(2,1)} collective-permute-done((bf16[208,512]{1,0:T(8,128)(2,1)}, bf16[208,512]{1,0:T(8,128)(2,1)}, u32[]{:S(2)}, u32[]{:S(2)}) %collective-permute-start.27) | collective-permute-done | bytes 213024 | tf_op jit(solution)/shard_map/ppermute | solution.py:698
  279.0 1.7 collective-permute-start.29
  282.1 1.2 collective-permute-start.30
  283.6 5.9 %shard_map.246 = bf16[1,14,14,4,1024]{4,3,2,1,0:T(4,128)(2,1)} custom-call(bf16[1024,512]{1,0:T(8,128)(2,1)} %get-tuple-element.249.refs_7_.refs_0_, bf16[1024,512]{1,0:T(8,128)(2,1)} %refs_1_.1, bf16[256,2048]{1,0:T(8,128)(2,1)} %get-tuple-element.210.refs_11_.refs_2_, bf16[1024,2048]{1,0:T(8,128)(2,1)} %refs_3_.5), custom_call_target="tpu_custom_call" | custom-call | tf_op jit(solution)/shard_map/pallas_call | solution.py:87
  289.6 2.3 collective-permute-start.38
  294.8 4.7 %collective-permute-done.30 = bf16[2,4,176,256]{3,2,1,0:T(8,128)(2,1)S(1)} collective-permute-done((bf16[2,4,176,256]{3,2,1,0:T(8,128)(2,1)}, bf16[2,4,176,256]{3,2,1,0:T(8,128)(2,1)S(1)}, u32[]{:S(2)}, u32[]{:S(2)}) %collective-permute-start.30) | collective-permute-done | bytes 720928 | tf_op jit(solution)/shard_map/ppermute | solution.py:698
  302.9 11.3 %collective-permute-done.39 = bf16[256,512]{1,0:T(8,128)(2,1)S(1)} collective-permute-done((bf16[256,512]{1,0:T(8,128)(2,1)S(1)}, bf16[256,512]{1,0:T(8,128)(2,1)S(1)}, u32[]{:S(2)}, u32[]{:S(2)}) %collective-permute-start.39) | collective-permute-done | bytes 262176 | tf_op jit(solution)/shard_map/ppermute | solution.py:698
  315.0 2.3 collective-permute-start.41
  317.6 2.4 collective-permute-start.35
  320.9 4.0 %collective-permute-done.34 = bf16[176,512]{1,0:T(8,128)(2,1)S(1)} collective-permute-done((bf16[176,512]{1,0:T(8,128)(2,1)S(1)}, bf16[176,512]{1,0:T(8,128)(2,1)S(1)}, u32[]{:S(2)}, u32[]{:S(2)}) %collective-permute-start.34) | collective-permute-done | bytes 180256 | tf_op jit(solution)/shard_map/ppermute | solution.py:698
  325.0 6.2 %collective-permute-done.35 = bf16[176,512]{1,0:T(8,128)(2,1)S(1)} collective-permute-done((bf16[176,512]{1,0:T(8,128)(2,1)S(1)}, bf16[176,512]{1,0:T(8,128)(2,1)S(1)}, u32[]{:S(2)}, u32[]{:S(2)}) %collective-permute-start.35) | collective-permute-done | bytes 180256 | tf_op jit(solution)/shard_map/ppermute | solution.py:698
  331.2 5.0 %collective-permute-done.36 = bf16[176,512]{1,0:T(8,128)(2,1)S(1)} collective-permute-done((bf16[176,512]{1,0:T(8,128)(2,1)S(1)}, bf16[176,512]{1,0:T(8,128)(2,1)S(1)}, u32[]{:S(2)}, u32[]{:S(2)}) %collective-permute-start.36) | collective-permute-done | bytes 180256 | tf_op jit(solution)/shard_map/ppermute | solution.py:698
  (169 shorter events, 32.2 us)
Async XLA Ops:
  0.6 21.5 %collective-permute-start.1 = (bf16[1,4608,512]{2,1,0:T(8,128)(2,1)}, bf16[1,4608,512]{2,1,0:T(8,128)(2,1)}, u32[]{:S(2)}, u32[]{:S(2)}) collective-permute-start(bf16[1,4608,512]{2,1,0:T(8,128)(2,1)} %refs_9_.3), channel_id=1, source_target_pairs={{0,16},{16,0},{1,17},{17,1},{2,18},{18,2},{3,19},{19,3},{4,20},{20... | collective-permute-start | bytes 14155784 | tf_op jit(solution)/shard_map/ppermute | solution.py:694
  8.3 28.2 %collective-permute-start.2 = (bf16[1024,1024]{1,0:T(8,128)(2,1)}, bf16[1024,1024]{1,0:T(8,128)(2,1)}, u32[]{:S(2)}, u32[]{:S(2)}) collective-permute-start(bf16[1024,1024]{1,0:T(8,128)(2,1)} %get-tuple-element.149.refs_2_.refs_9_.refs_5_), channel_id=1, source_target_pairs={{0,16},{16,0},{1,17},{17,1},{2,18},{18,2},{3,19},{19,3},{4,20},{20... | collective-permute-start | bytes 6291464 | tf_op jit(solution)/shard_map/ppermute | solution.py:694
  8.4 34.8 %collective-permute-start.3 = (bf16[1,512,2048]{2,1,0:T(8,128)(2,1)S(1)}, bf16[1,512,2048]{2,1,0:T(8,128)(2,1)}, u32[]{:S(2)}, u32[]{:S(2)}) collective-permute-start(bf16[1,512,2048]{2,1,0:T(8,128)(2,1)S(1)} %copy-done), channel_id=1, source_target_pairs={{0,16},{16,0},{1,17},{17,1},{2,18},{18,2},{3,19},{19,3},{4,20},{20... | collective-permute-start | bytes 6291464 | tf_op jit(solution)/shard_map/ppermute | solution.py:694
  8.9 12.6 %collective-permute-start = (f32[4,512]{1,0:T(4,128)S(1)}, f32[4,512]{1,0:T(4,128)S(1)}, u32[]{:S(2)}, u32[]{:S(2)}) collective-permute-start(f32[4,512]{1,0:T(4,128)S(1)} %pad_maximum_fusion.11), channel_id=1, source_target_pairs={{0,16},{16,0},{1,17},{17,1},{2,18},{18,2},{3,19},{19,3},{4,20},{20... | collective-permute-start | bytes 24584 | tf_op jit(solution)/shard_map/ppermute | solution.py:694
  9.1 13.0 %all-to-all-start = ((f32[16,2,512]{2,1,0:T(2,128)}), f32[16,2,512]{2,1,0:T(2,128)S(1)}, u32[]{:S(2)}, u32[]{:S(2)}) async-start(f32[16,2,512]{2,1,0:T(2,128)} %get-tuple-element.147), calls=%async_computation | async-start | bytes 131072 | tf_op jit(solution)/shard_map/all_to_all | solution.py:690
  22.1 13.7 %copy-start.21 = (f32[1,2048]{1,0:T(1,128)S(1)}, f32[1,2048]{1,0:T(1,128)}, u32[]{:S(2)}) copy-start(f32[1,2048]{1,0:T(1,128)} %param.27) | copy-start | bytes 24580
  22.1 13.7 %copy-start.22 = (f32[1,2048]{1,0:T(1,128)S(1)}, f32[1,2048]{1,0:T(1,128)}, u32[]{:S(2)}) copy-start(f32[1,2048]{1,0:T(1,128)} %param.26) | copy-start | bytes 24580
  28.4 32.0 %collective-permute-start.4 = (bf16[256,4608]{1,0:T(8,128)(2,1)}, bf16[256,4608]{1,0:T(8,128)(2,1)}, u32[]{:S(2)}, u32[]{:S(2)}) collective-permute-start(bf16[256,4608]{1,0:T(8,128)(2,1)} %get-tuple-element.155.refs_1_), channel_id=1, source_target_pairs={{0,16},{16,0},{1,17},{17,1},{2,18},{18,2},{3,19},{19,3},{4,20},{20... | collective-permute-start | bytes 7077896 | tf_op jit(solution)/shard_map/ppermute | solution.py:694
  29.5 13.7 %all-to-all-start.1 = ((bf16[16,2,3840]{2,1,0:T(2,128)(2,1)}), bf16[16,2,3840]{2,1,0:T(2,128)(2,1)S(1)}, u32[]{:S(2)}, u32[]{:S(2)}) async-start(bf16[16,2,3840]{2,1,0:T(2,128)(2,1)} %get-tuple-element.151), calls=%async_computation.1 | async-start | bytes 491520 | tf_op jit(solution)/shard_map/all_to_all | solution.py:690
  35.8 20.0 %collective-permute-start.5 = (f32[2,2048]{1,0:T(2,128)S(1)}, f32[2,2048]{1,0:T(2,128)S(1)}, u32[]{:S(2)}, u32[]{:S(2)}) collective-permute-start(f32[2,2048]{1,0:T(2,128)S(1)} %pad_maximum_fusion.9), channel_id=1, source_target_pairs={{0,16},{16,0},{1,17},{17,1},{2,18},{18,2},{3,19},{19,3},{4,20},{20... | collective-permute-start | bytes 49160 | tf_op jit(solution)/shard_map/ppermute | solution.py:694
  43.2 10.5 %copy-start.29 = (f32[2048]{0:T(1024)S(1)}, f32[2048]{0:T(1024)}, u32[]{:S(2)}) copy-start(f32[2048]{0:T(1024)} %param.20) | copy-start | bytes 24580
  43.2 10.5 %copy-start.30 = (f32[2048]{0:T(1024)S(1)}, f32[2048]{0:T(1024)}, u32[]{:S(2)}) copy-start(f32[2048]{0:T(1024)} %param.19) | copy-start | bytes 24580
  48.2 12.2 %all-to-all-start.2 = ((f32[16,2,2048]{2,1,0:T(2,128)}), f32[16,2,2048]{2,1,0:T(2,128)S(1)}, u32[]{:S(2)}, u32[]{:S(2)}) async-start(f32[16,2,2048]{2,1,0:T(2,128)} %get-tuple-element.154), calls=%async_computation.2 | async-start | bytes 524288 | tf_op jit(solution)/shard_map/all_to_all | solution.py:690
  54.2 18.2 %collective-permute-start.6 = (bf16[256,512]{1,0:T(8,128)(2,1)}, bf16[256,512]{1,0:T(8,128)(2,1)S(1)}, u32[]{:S(2)}, u32[]{:S(2)}) collective-permute-start(bf16[256,512]{1,0:T(8,128)(2,1)} %get-tuple-element.161.refs_5_), channel_id=1, source_target_pairs={{0,16},{16,0},{1,17},{17,1},{2,18},{18,2},{3,19},{19,3},{4,20},{20... | collective-permute-start | bytes 786440 | tf_op jit(solution)/shard_map/ppermute | solution.py:694
  66.6 11.4 %all-to-all-start.3 = ((f32[16,2,512]{2,1,0:T(2,128)}), f32[16,2,512]{2,1,0:T(2,128)S(1)}, u32[]{:S(2)}, u32[]{:S(2)}) async-start(f32[16,2,512]{2,1,0:T(2,128)} %get-tuple-element.160), calls=%async_computation.3 | async-start | bytes 131072 | tf_op jit(solution)/shard_map/all_to_all | solution.py:690
  72.5 11.4 %copy-start.13 = (bf16[256,512]{1,0:T(8,128)(2,1)}, bf16[256,512]{1,0:T(8,128)(2,1)S(1)}, u32[]{:S(2)}) copy-start(bf16[256,512]{1,0:T(8,128)(2,1)S(1)} %collective-permute-done.6.refs_6_) | copy-start | bytes 786436
  83.9 28.8 %collective-permute-start.8 = (bf16[256,4608]{1,0:T(8,128)(2,1)}, bf16[256,4608]{1,0:T(8,128)(2,1)S(1)}, u32[]{:S(2)}, u32[]{:S(2)}) collective-permute-start(bf16[256,4608]{1,0:T(8,128)(2,1)} %get-tuple-element.169.refs_5_), channel_id=1, source_target_pairs={{0,16},{16,0},{1,17},{17,1},{2,18},{18,2},{3,19},{19,3},{4,20},{20... | collective-permute-start | bytes 7077896 | tf_op jit(solution)/shard_map/ppermute | solution.py:694
  86.7 10.0 %collective-permute-start.7 = (bf16[256,2048]{1,0:T(8,128)(2,1)S(1)}, bf16[256,2048]{1,0:T(8,128)(2,1)S(1)}, u32[]{:S(2)}, u32[]{:S(2)}) collective-permute-start(bf16[256,2048]{1,0:T(8,128)(2,1)S(1)} %copy-done.1), channel_id=1, source_target_pairs={{0,16},{16,0},{1,17},{17,1},{2,18},{18,2},{3,19},{19,3},{4,20},{20... | collective-permute-start | bytes 3145736 | tf_op jit(solution)/shard_map/ppermute | solution.py:694
  112.7 12.8 %copy-start.15 = (bf16[256,512]{1,0:T(8,128)(2,1)S(1)}, bf16[256,512]{1,0:T(8,128)(2,1)}, u32[]{:S(2)}) copy-start(bf16[256,512]{1,0:T(8,128)(2,1)} %get-tuple-element.174.refs_1_) | copy-start | bytes 786436
  119.7 12.5 %all-to-all-start.6 = ((f32[16,2,2048]{2,1,0:T(2,128)}), f32[16,2,2048]{2,1,0:T(2,128)S(1)}, u32[]{:S(2)}, u32[]{:S(2)}) async-start(f32[16,2,2048]{2,1,0:T(2,128)} %get-tuple-element.173), calls=%async_computation.6 | async-start | bytes 524288 | tf_op jit(solution)/shard_map/all_to_all | solution.py:690
  125.5 3.2 collective-permute-start.9
  138.2 13.2 %collective-permute-start.10 = (bf16[256,2048]{1,0:T(8,128)(2,1)}, bf16[256,2048]{1,0:T(8,128)(2,1)S(1)}, u32[]{:S(2)}, u32[]{:S(2)}) collective-permute-start(bf16[256,2048]{1,0:T(8,128)(2,1)} %get-tuple-element.180.refs_3_), channel_id=1, source_target_pairs={{0,16},{16,0},{1,17},{17,1},{2,18},{18,2},{3,19},{19,3},{4,20},{20... | collective-permute-start | bytes 3145736 | tf_op jit(solution)/shard_map/ppermute | solution.py:694
  157.8 5.7 %collective-permute-start.11 = (bf16[256,512]{1,0:T(8,128)(2,1)}, bf16[256,512]{1,0:T(8,128)(2,1)S(1)}, u32[]{:S(2)}, u32[]{:S(2)}) collective-permute-start(bf16[256,512]{1,0:T(8,128)(2,1)} %get-tuple-element.188.refs_7_), channel_id=1, source_target_pairs={{0,16},{16,0},{1,17},{17,1},{2,18},{18,2},{3,19},{19,3},{4,20},{20... | collective-permute-start | bytes 786440 | tf_op jit(solution)/shard_map/ppermute | solution.py:694
  159.1 11.6 %all-to-all-start.8 = ((f32[16,2,512]{2,1,0:T(2,128)}), f32[16,2,512]{2,1,0:T(2,128)S(1)}, u32[]{:S(2)}, u32[]{:S(2)}) async-start(f32[16,2,512]{2,1,0:T(2,128)} %get-tuple-element.184), calls=%async_computation.8 | async-start | bytes 131072 | tf_op jit(solution)/shard_map/all_to_all | solution.py:690
  170.7 23.2 %collective-permute-start.13 = (bf16[2,4,208,256]{3,2,1,0:T(8,128)(2,1)}, bf16[2,4,208,256]{3,2,1,0:T(8,128)(2,1)S(1)}, u32[]{:S(2)}, u32[]{:S(2)}) collective-permute-start(bf16[2,4,208,256]{3,2,1,0:T(8,128)(2,1)} %get-tuple-element.198), channel_id=1, source_target_pairs={{0,1},{1,0},{2,3},{3,2},{4,5},{5,4},{6,7},{7,6},{8,9},{9,8},{10,11... | collective-permute-start | bytes 2555912 | tf_op jit(solution)/shard_map/ppermute | solution.py:698
  172.0 22.0 %collective-permute-start.14 = (bf16[2,4,208,256]{3,2,1,0:T(8,128)(2,1)}, bf16[2,4,208,256]{3,2,1,0:T(8,128)(2,1)}, u32[]{:S(2)}, u32[]{:S(2)}) collective-permute-start(bf16[2,4,208,256]{3,2,1,0:T(8,128)(2,1)} %get-tuple-element.200), channel_id=1, source_target_pairs={{0,2},{1,3},{2,0},{3,1},{4,6},{5,7},{6,4},{7,5},{8,10},{9,11},{10,... | collective-permute-start | bytes 2555912 | tf_op jit(solution)/shard_map/ppermute | solution.py:698
  173.2 20.8 %copy-start.8 = (bf16[2,4,208,256]{3,2,1,0:T(8,128)(2,1)S(1)}, bf16[2,4,208,256]{3,2,1,0:T(8,128)(2,1)}, u32[]{:S(2)}) copy-start(bf16[2,4,208,256]{3,2,1,0:T(8,128)(2,1)} %get-tuple-element.197) | copy-start | bytes 2555908
  173.2 20.8 %copy-start.9 = (bf16[2,4,208,256]{3,2,1,0:T(8,128)(2,1)S(1)}, bf16[2,4,208,256]{3,2,1,0:T(8,128)(2,1)}, u32[]{:S(2)}) copy-start(bf16[2,4,208,256]{3,2,1,0:T(8,128)(2,1)} %get-tuple-element.199) | copy-start | bytes 2555908
  182.0 11.9 %all-to-all-start.9 = ((bf16[16,2,3072]{2,1,0:T(2,128)(2,1)}), bf16[16,2,3072]{2,1,0:T(2,128)(2,1)S(1)}, u32[]{:S(2)}, u32[]{:S(2)}) async-start(bf16[16,2,3072]{2,1,0:T(2,128)(2,1)} %get-tuple-element.194), calls=%async_computation.9 | async-start | bytes 393216 | tf_op jit(solution)/shard_map/all_to_all | solution.py:690
  186.7 2.8 collective-permute-start.12
  189.5 14.1 %copy-start.16 = (bf16[256,512]{1,0:T(8,128)(2,1)}, bf16[256,512]{1,0:T(8,128)(2,1)S(1)}, u32[]{:S(2)}) copy-start(bf16[256,512]{1,0:T(8,128)(2,1)S(1)} %collective-permute-done.12.refs_4_) | copy-start | bytes 786436
  203.6 8.9 %collective-permute-start.15 = (bf16[256,2048]{1,0:T(8,128)(2,1)}, bf16[256,2048]{1,0:T(8,128)(2,1)S(1)}, u32[]{:S(2)}, u32[]{:S(2)}) collective-permute-start(bf16[256,2048]{1,0:T(8,128)(2,1)} %get-tuple-element.208.refs_7_), channel_id=1, source_target_pairs={{0,16},{16,0},{1,17},{17,1},{2,18},{18,2},{3,19},{19,3},{4,20},{20... | collective-permute-start | bytes 3145736 | tf_op jit(solution)/shard_map/ppermute | solution.py:694
  205.4 7.1 %collective-permute-start.16 = (bf16[256,2048]{1,0:T(8,128)(2,1)}, bf16[256,2048]{1,0:T(8,128)(2,1)S(1)}, u32[]{:S(2)}, u32[]{:S(2)}) collective-permute-start(bf16[256,2048]{1,0:T(8,128)(2,1)} %get-tuple-element.210.refs_11_.refs_2_), channel_id=1, source_target_pairs={{0,16},{16,0},{1,17},{17,1},{2,18},{18,2},{3,19},{19,3},{4,20},{20... | collective-permute-start | bytes 3145736 | tf_op jit(solution)/shard_map/ppermute | solution.py:694
  205.5 14.9 %collective-permute-start.17 = (bf16[4,208,256]{2,1,0:T(8,128)(2,1)S(1)}, bf16[4,208,256]{2,1,0:T(8,128)(2,1)}, u32[]{:S(2)}, u32[]{:S(2)}) collective-permute-start(bf16[4,208,256]{2,1,0:T(8,128)(2,1)S(1)} %fusion.13), channel_id=1, source_target_pairs={{0,2},{1,3},{2,0},{3,1},{4,6},{5,7},{6,4},{7,5},{8,10},{9,11},{10,... | collective-permute-start | bytes 1277960 | tf_op jit(solution)/shard_map/ppermute | solution.py:698
  206.7 13.7 %collective-permute-start.18 = (bf16[4,208,256]{2,1,0:T(8,128)(2,1)}, bf16[4,208,256]{2,1,0:T(8,128)(2,1)}, u32[]{:S(2)}, u32[]{:S(2)}) collective-permute-start(bf16[4,208,256]{2,1,0:T(8,128)(2,1)} %fusion.12), channel_id=1, source_target_pairs={{0,1},{1,0},{2,3},{3,2},{4,5},{5,4},{6,7},{7,6},{8,9},{9,8},{10,11... | collective-permute-start | bytes 1277960 | tf_op jit(solution)/shard_map/ppermute | solution.py:698
  207.0 13.4 %all-to-all-start.10 = ((f32[16,2,512]{2,1,0:T(2,128)}), f32[16,2,512]{2,1,0:T(2,128)S(1)}, u32[]{:S(2)}, u32[]{:S(2)}) async-start(f32[16,2,512]{2,1,0:T(2,128)} %get-tuple-element.204), calls=%async_computation.10 | async-start | bytes 131072 | tf_op jit(solution)/shard_map/all_to_all | solution.py:690
  220.4 25.1 %collective-permute-start.20 = (bf16[2,4,256,256]{3,2,1,0:T(8,128)(2,1)}, bf16[2,4,256,256]{3,2,1,0:T(8,128)(2,1)}, u32[]{:S(2)}, u32[]{:S(2)}) collective-permute-start(bf16[2,4,256,256]{3,2,1,0:T(8,128)(2,1)} %get-tuple-element.222), channel_id=1, source_target_pairs={{0,1},{1,0},{2,3},{3,2},{4,5},{5,4},{6,7},{7,6},{8,9},{9,8},{10,11... | collective-permute-start | bytes 3145736 | tf_op jit(solution)/shard_map/ppermute | solution.py:698
  221.7 25.0 %collective-permute-start.21 = (bf16[2,4,256,256]{3,2,1,0:T(8,128)(2,1)}, bf16[2,4,256,256]{3,2,1,0:T(8,128)(2,1)}, u32[]{:S(2)}, u32[]{:S(2)}) collective-permute-start(bf16[2,4,256,256]{3,2,1,0:T(8,128)(2,1)} %get-tuple-element.224), channel_id=1, source_target_pairs={{0,2},{1,3},{2,0},{3,1},{4,6},{5,7},{6,4},{7,5},{8,10},{9,11},{10,... | collective-permute-start | bytes 3145736 | tf_op jit(solution)/shard_map/ppermute | solution.py:698
  231.7 13.8 %all-to-all-start.11 = ((f32[16,2,512]{2,1,0:T(2,128)}), f32[16,2,512]{2,1,0:T(2,128)S(1)}, u32[]{:S(2)}, u32[]{:S(2)}) async-start(f32[16,2,512]{2,1,0:T(2,128)} %get-tuple-element.218), calls=%async_computation.11 | async-start | bytes 131072 | tf_op jit(solution)/shard_map/all_to_all | solution.py:690
  236.3 9.2 %collective-permute-start.19 = (bf16[256,512]{1,0:T(8,128)(2,1)}, bf16[256,512]{1,0:T(8,128)(2,1)S(1)}, u32[]{:S(2)}, u32[]{:S(2)}) collective-permute-start(bf16[256,512]{1,0:T(8,128)(2,1)} %get-tuple-element.219.refs_3_), channel_id=1, source_target_pairs={{0,16},{16,0},{1,17},{17,1},{2,18},{18,2},{3,19},{19,3},{4,20},{20... | collective-permute-start | bytes 786440 | tf_op jit(solution)/shard_map/ppermute | solution.py:694
  252.8 8.7 %collective-permute-start.22 = (bf16[1024,512]{1,0:T(8,128)(2,1)}, bf16[1024,512]{1,0:T(8,128)(2,1)S(1)}, u32[]{:S(2)}, u32[]{:S(2)}) collective-permute-start(bf16[1024,512]{1,0:T(8,128)(2,1)} %get-tuple-element.249.refs_7_.refs_0_), channel_id=1, source_target_pairs={{0,16},{16,0},{1,17},{17,1},{2,18},{18,2},{3,19},{19,3},{4,20},{20... | collective-permute-start | bytes 3145736 | tf_op jit(solution)/shard_map/ppermute | solution.py:694
  255.6 16.8 %collective-permute-start.23 = (bf16[4,256,256]{2,1,0:T(8,128)(2,1)S(1)}, bf16[4,256,256]{2,1,0:T(8,128)(2,1)S(1)}, u32[]{:S(2)}, u32[]{:S(2)}) collective-permute-start(bf16[4,256,256]{2,1,0:T(8,128)(2,1)S(1)} %fusion.5), channel_id=1, source_target_pairs={{0,2},{1,3},{2,0},{3,1},{4,6},{5,7},{6,4},{7,5},{8,10},{9,11},{10,... | collective-permute-start | bytes 1572872 | tf_op jit(solution)/shard_map/ppermute | solution.py:698
  256.8 15.6 %collective-permute-start.24 = (bf16[4,256,256]{2,1,0:T(8,128)(2,1)S(1)}, bf16[4,256,256]{2,1,0:T(8,128)(2,1)S(1)}, u32[]{:S(2)}, u32[]{:S(2)}) collective-permute-start(bf16[4,256,256]{2,1,0:T(8,128)(2,1)S(1)} %fusion.4), channel_id=1, source_target_pairs={{0,1},{1,0},{2,3},{3,2},{4,5},{5,4},{6,7},{7,6},{8,9},{9,8},{10,11... | collective-permute-start | bytes 1572872 | tf_op jit(solution)/shard_map/ppermute | solution.py:698
  257.8 16.9 %collective-permute-start.25 = (bf16[208,512]{1,0:T(8,128)(2,1)}, bf16[208,512]{1,0:T(8,128)(2,1)}, u32[]{:S(2)}, u32[]{:S(2)}) collective-permute-start(bf16[208,512]{1,0:T(8,128)(2,1)} %get-tuple-element.239), channel_id=1, source_target_pairs={{0,4},{1,5},{2,6},{3,7},{4,0},{5,1},{6,2},{7,3},{8,12},{9,13},{10,... | collective-permute-start | bytes 638984 | tf_op jit(solution)/shard_map/ppermute | solution.py:698
  258.1 16.7 %collective-permute-start.26 = (bf16[208,512]{1,0:T(8,128)(2,1)}, bf16[208,512]{1,0:T(8,128)(2,1)}, u32[]{:S(2)}, u32[]{:S(2)}) collective-permute-start(bf16[208,512]{1,0:T(8,128)(2,1)} %get-tuple-element.240), channel_id=1, source_target_pairs={{0,8},{1,9},{2,10},{3,11},{4,12},{5,13},{6,14},{7,15},{8,0},{9,1},... | collective-permute-start | bytes 638984 | tf_op jit(solution)/shard_map/ppermute | solution.py:698
  261.5 17.5 %collective-permute-start.27 = (bf16[208,512]{1,0:T(8,128)(2,1)}, bf16[208,512]{1,0:T(8,128)(2,1)}, u32[]{:S(2)}, u32[]{:S(2)}) collective-permute-start(bf16[208,512]{1,0:T(8,128)(2,1)} %get-tuple-element.241), channel_id=1, source_target_pairs={{0,12},{1,13},{2,14},{3,15},{4,8},{5,9},{6,10},{7,11},{8,4},{9,5},... | collective-permute-start | bytes 638984 | tf_op jit(solution)/shard_map/ppermute | solution.py:698
  279.0 10.7 %collective-permute-start.29 = (f32[2,2,512]{2,1,0:T(2,128)}, f32[2,2,512]{2,1,0:T(2,128)S(1)}, u32[]{:S(2)}, u32[]{:S(2)}) collective-permute-start(f32[2,2,512]{2,1,0:T(2,128)} %broadcast_select_fusion.7), channel_id=1, source_target_pairs={{0,16},{16,0},{1,17},{17,1},{2,18},{18,2},{3,19},{19,3},{4,20},{20... | collective-permute-start | bytes 24584 | tf_op jit(solution)/shard_map/ppermute | solution.py:694
  280.7 11.3 %collective-permute-start.28 = (f32[4,2048]{1,0:T(4,128)}, f32[4,2048]{1,0:T(4,128)S(1)}, u32[]{:S(2)}, u32[]{:S(2)}) collective-permute-start(f32[4,2048]{1,0:T(4,128)} %pad_maximum_fusion.8), channel_id=1, source_target_pairs={{0,16},{16,0},{1,17},{17,1},{2,18},{18,2},{3,19},{19,3},{4,20},{20... | collective-permute-start | bytes 98312 | tf_op jit(solution)/shard_map/ppermute | solution.py:694
  282.0 10.3 %copy-start.23 = (f32[2,512]{1,0:T(2,128)S(1)}, f32[2,512]{1,0:T(2,128)}, u32[]{:S(2)}) copy-start(f32[2,512]{1,0:T(2,128)} %get-tuple-element.246) | copy-start | bytes 12292
  282.0 10.3 %copy-start.24 = (f32[2,512]{1,0:T(2,128)S(1)}, f32[2,512]{1,0:T(2,128)}, u32[]{:S(2)}) copy-start(f32[2,512]{1,0:T(2,128)} %get-tuple-element.245) | copy-start | bytes 12292
  282.0 18.4 %copy-start.11 = (bf16[2,4,176,256]{3,2,1,0:T(8,128)(2,1)S(1)}, bf16[2,4,176,256]{3,2,1,0:T(8,128)(2,1)}, u32[]{:S(2)}) copy-start(bf16[2,4,176,256]{3,2,1,0:T(8,128)(2,1)} %get-tuple-element.256) | copy-start | bytes 2162692
  282.0 18.4 %copy-start.12 = (bf16[2,4,176,256]{3,2,1,0:T(8,128)(2,1)S(1)}, bf16[2,4,176,256]{3,2,1,0:T(8,128)(2,1)}, u32[]{:S(2)}) copy-start(bf16[2,4,176,256]{3,2,1,0:T(8,128)(2,1)} %get-tuple-element.258) | copy-start | bytes 2162692
  282.1 17.5 %collective-permute-start.30 = (bf16[2,4,176,256]{3,2,1,0:T(8,128)(2,1)}, bf16[2,4,176,256]{3,2,1,0:T(8,128)(2,1)S(1)}, u32[]{:S(2)}, u32[]{:S(2)}) collective-permute-start(bf16[2,4,176,256]{3,2,1,0:T(8,128)(2,1)} %get-tuple-element.253), channel_id=1, source_target_pairs={{0,1},{1,0},{2,3},{3,2},{4,5},{5,4},{6,7},{7,6},{8,9},{9,8},{10,11... | collective-permute-start | bytes 2162696 | tf_op jit(solution)/shard_map/ppermute | solution.py:698
  283.3 17.1 %collective-permute-start.31 = (bf16[2,4,176,256]{3,2,1,0:T(8,128)(2,1)}, bf16[2,4,176,256]{3,2,1,0:T(8,128)(2,1)S(1)}, u32[]{:S(2)}, u32[]{:S(2)}) collective-permute-start(bf16[2,4,176,256]{3,2,1,0:T(8,128)(2,1)} %get-tuple-element.254), channel_id=1, source_target_pairs={{0,2},{1,3},{2,0},{3,1},{4,6},{5,7},{6,4},{7,5},{8,10},{9,11},{10,... | collective-permute-start | bytes 2162696 | tf_op jit(solution)/shard_map/ppermute | solution.py:698
  289.5 12.1 %collective-permute-start.37 = (bf16[256,512]{1,0:T(8,128)(2,1)S(1)}, bf16[256,512]{1,0:T(8,128)(2,1)S(1)}, u32[]{:S(2)}, u32[]{:S(2)}) collective-permute-start(bf16[256,512]{1,0:T(8,128)(2,1)S(1)} %get-tuple-element.274), channel_id=1, source_target_pairs={{0,4},{1,5},{2,6},{3,7},{4,0},{5,1},{6,2},{7,3},{8,12},{9,13},{10,... | collective-permute-start | bytes 786440 | tf_op jit(solution)/shard_map/ppermute | solution.py:698
  289.6 13.3 %collective-permute-start.38 = (bf16[256,512]{1,0:T(8,128)(2,1)S(1)}, bf16[256,512]{1,0:T(8,128)(2,1)S(1)}, u32[]{:S(2)}, u32[]{:S(2)}) collective-permute-start(bf16[256,512]{1,0:T(8,128)(2,1)S(1)} %get-tuple-element.275), channel_id=1, source_target_pairs={{0,8},{1,9},{2,10},{3,11},{4,12},{5,13},{6,14},{7,15},{8,0},{9,1},... | collective-permute-start | bytes 786440 | tf_op jit(solution)/shard_map/ppermute | solution.py:698
  292.0 22.2 %collective-permute-start.39 = (bf16[256,512]{1,0:T(8,128)(2,1)S(1)}, bf16[256,512]{1,0:T(8,128)(2,1)S(1)}, u32[]{:S(2)}, u32[]{:S(2)}) collective-permute-start(bf16[256,512]{1,0:T(8,128)(2,1)S(1)} %get-tuple-element.276), channel_id=1, source_target_pairs={{0,12},{1,13},{2,14},{3,15},{4,8},{5,9},{6,10},{7,11},{8,4},{9,5},... | collective-permute-start | bytes 786440 | tf_op jit(solution)/shard_map/ppermute | solution.py:698
  300.5 16.8 %collective-permute-start.32 = (bf16[4,176,256]{2,1,0:T(8,128)(2,1)S(1)}, bf16[4,176,256]{2,1,0:T(8,128)(2,1)S(1)}, u32[]{:S(2)}, u32[]{:S(2)}) collective-permute-start(bf16[4,176,256]{2,1,0:T(8,128)(2,1)S(1)} %add_bitcast_fusion.1), channel_id=1, source_target_pairs={{0,2},{1,3},{2,0},{3,1},{4,6},{5,7},{6,4},{7,5},{8,10},{9,11},{10,... | collective-permute-start | bytes 1081352 | tf_op jit(solution)/shard_map/ppermute | solution.py:698
  300.8 16.5 %collective-permute-start.33 = (bf16[4,176,256]{2,1,0:T(8,128)(2,1)S(1)}, bf16[4,176,256]{2,1,0:T(8,128)(2,1)S(1)}, u32[]{:S(2)}, u32[]{:S(2)}) collective-permute-start(bf16[4,176,256]{2,1,0:T(8,128)(2,1)S(1)} %add_bitcast_fusion), channel_id=1, source_target_pairs={{0,1},{1,0},{2,3},{3,2},{4,5},{5,4},{6,7},{7,6},{8,9},{9,8},{10,11... | collective-permute-start | bytes 1081352 | tf_op jit(solution)/shard_map/ppermute | solution.py:698
  315.0 22.6 %collective-permute-start.41 = (f32[32,1024]{1,0:T(8,128)S(1)}, f32[32,1024]{1,0:T(8,128)S(1)}, u32[]{:S(2)}, u32[]{:S(2)}) collective-permute-start(f32[32,1024]{1,0:T(8,128)S(1)} %fusion.41), channel_id=1, source_target_pairs={{0,16},{16,0},{1,17},{17,1},{2,18},{18,2},{3,19},{19,3},{4,20},{20... | collective-permute-start | bytes 393224 | tf_op jit(solution)/shard_map/ppermute | solution.py:694
  317.5 7.5 %collective-permute-start.34 = (bf16[176,512]{1,0:T(8,128)(2,1)S(1)}, bf16[176,512]{1,0:T(8,128)(2,1)S(1)}, u32[]{:S(2)}, u32[]{:S(2)}) collective-permute-start(bf16[176,512]{1,0:T(8,128)(2,1)S(1)} %get-tuple-element.267), channel_id=1, source_target_pairs={{0,4},{1,5},{2,6},{3,7},{4,0},{5,1},{6,2},{7,3},{8,12},{9,13},{10,... | collective-permute-start | bytes 540680 | tf_op jit(solution)/shard_map/ppermute | solution.py:698
  317.6 13.6 %collective-permute-start.35 = (bf16[176,512]{1,0:T(8,128)(2,1)S(1)}, bf16[176,512]{1,0:T(8,128)(2,1)S(1)}, u32[]{:S(2)}, u32[]{:S(2)}) collective-permute-start(bf16[176,512]{1,0:T(8,128)(2,1)S(1)} %get-tuple-element.268), channel_id=1, source_target_pairs={{0,8},{1,9},{2,10},{3,11},{4,12},{5,13},{6,14},{7,15},{8,0},{9,1},... | collective-permute-start | bytes 540680 | tf_op jit(solution)/shard_map/ppermute | solution.py:698
  319.9 16.3 %collective-permute-start.36 = (bf16[176,512]{1,0:T(8,128)(2,1)S(1)}, bf16[176,512]{1,0:T(8,128)(2,1)S(1)}, u32[]{:S(2)}, u32[]{:S(2)}) collective-permute-start(bf16[176,512]{1,0:T(8,128)(2,1)S(1)} %get-tuple-element.269), channel_id=1, source_target_pairs={{0,12},{1,13},{2,14},{3,15},{4,8},{5,9},{6,10},{7,11},{8,4},{9,5},... | collective-permute-start | bytes 540680 | tf_op jit(solution)/shard_map/ppermute | solution.py:698
  336.4 2.6 collective-permute-start.40
  (18 other events, 135.9 us)
where the time goes:
time: 342 us; the launch traced here: 340 us
  Pallas kernels  121 us (35%)
  starting transfers between devices  96.5 us (28%)
  waiting for transfers between devices  68.2 us (20%)
  blocking collectives  30.7 us (9%)
  other arithmetic  18.5 us (5%)
  local copies, waits for them, and re-layouts  4.01 us (1%)
    pallas_call x18, Pallas kernels, stage(): pl.pallas_call(run, out_shape=list(outs), in_specs=[kinds[kind] for kind...  121 us
    all_to_all x9, starting transfers between devices, exchange(): return lax.all_to_all(sent, 'dp', 0, 0)  49.3 us
    ppermute x21, waiting for transfers between devices, across(): lax.ppermute(value, 'dp', [(i, i ^ mask) for i in range(lax.axis_size('dp...  37.6 us
    all_to_all x3, blocking collectives, exchange(): return lax.all_to_all(sent, 'dp', 0, 0)  30.7 us
    ppermute x21, starting transfers between devices, swapped(): return lax.ppermute(value, 'section', [(0, 1), (1, 0)])  28.6 us
    all_to_all x9, waiting for transfers between devices, exchange(): return lax.all_to_all(sent, 'dp', 0, 0)  28 us
    ppermute x21, starting transfers between devices, across(): lax.ppermute(value, 'dp', [(i, i ^ mask) for i in range(lax.axis_size('dp...  18.6 us
  transfers between devices with their start and end apart: 51, of which 16 were waited for; matrix products, arithmetic and copies ran while one was open for 5% of the time, Pallas kernels for 24%

commit v1 on v0

--- a/solution.py
+++ b/solution.py
@@ -143,13 +143,13 @@
     total = (count * (geo.pixels * planes)).astype(F32)
 
     def plain(start, acc):
-        return acc + fold_rows(z_ref[pl.ds(start, step), :] * geo.mask(start, step, width, count))
+        return acc + fold_rows(z_ref[pl.ds(start, step), :].astype(F32) * geo.mask(start, step, width, count))
 
     zero = jnp.zeros((8, width), F32)
     average = jnp.sum(over_rows(rows, step, plain, zero), axis=0, keepdims=True) / total
 
     def squared(start, acc):
-        centered = z_ref[pl.ds(start, step), :] - average
+        centered = z_ref[pl.ds(start, step), :].astype(F32) - average
         return acc + fold_rows(centered * centered * geo.mask(start, step, width, count))
 
     spread = jnp.sum(over_rows(rows, step, squared, zero), axis=0, keepdims=True)
@@ -324,7 +324,7 @@
     z_ref = z_out.ref
     for plane in range(4):
         at = plane * geo.rows
-        z_ref[at : at + geo.rows, :] = dot(x_ref[at : at + geo.rows, :], weight[...])
+        z_ref[at : at + geo.rows, :] = dot(x_ref[at : at + geo.rows, :], weight[...]).astype(z_ref.dtype)
     z_out.send()
     send_rows(sent, (local_stats(z_ref, geo, count, 4),))
 
@@ -335,7 +335,7 @@
     load.start()
     load.wait()
     z_ref = z_out.ref
-    z_ref[...] = dot(x_vmem[...], weight.get()[...])
+    z_ref[...] = dot(x_vmem[...], weight.get()[...]).astype(BF16)
     z_out.send()
     average, spread = local_stats(z_ref, geo, count, 1)
     stats[0:1, :] = average
@@ -360,7 +360,7 @@
     rows_of, width = z_ref.shape
 
     def activate(start, carry):
-        pre = (z_ref[pl.ds(start, 64), :] - average) * gain + offset
+        pre = (z_ref[pl.ds(start, 64), :].astype(F32) - average) * gain + offset
         active[pl.ds(start, 64), :] = pre * sigmoid(pre) * geo.mask(start, 64, width)
         return carry
 
@@ -410,7 +410,7 @@
     over_rows(geo.rows, 64, activate, 0)
     a_out.send()
     choice.wait()
-    z_out.ref[...] = dot(a_out.ref[...], weight[...])
+    z_out.ref[...] = dot(a_out.ref[...], weight[...]).astype(BF16)
     z_out.send()
     send_rows(sent, (local_stats(z_out.ref, geo, count, 1),))
     sent.send()
@@ -434,7 +434,11 @@
 
     def activate(start, carry):
         rows = pl.ds(start, 16)
-        pre = (z3[rows, :] - average_c) * gain_c + (zs[rows, :] - average_s) * gain_s + offset
+        pre = (
+            (z3[rows, :].astype(F32) - average_c) * gain_c
+            + (zs[rows, :].astype(F32) - average_s) * gain_s
+            + offset
+        )
         joined.ref[rows, :] = (pre * sigmoid(pre)).astype(BF16)
         return carry
 
@@ -453,7 +457,7 @@
     average, inverse = combined(got, slice(None), counts, section, geo.pixels)
     moments[0:1, :] = average
     moments[1:2, :] = inverse
-    g_ref = g_out.ref
+    g_ref = flat
     width = g_ref.shape[1]
     empty = jnp.zeros((geo.slots, width), F32)
     for line in range(geo.side):
@@ -472,12 +476,12 @@
     def activate(start, carry):
         plain, scaled = carry
         rows = pl.ds(start, 16)
-        normed = (u3[rows, :] - average) * inverse
+        normed = (u3[rows, :].astype(F32) - average) * inverse
         pre = normed * weight + offset + joined[rows, :].astype(F32)
         part = sigmoid(pre)
+        upstream = g_ref[rows, :] * geo.mask(start, 16, width, count) * (part * (1.0 + pre * (1.0 - part)))
         flat[rows, :] = pre * part
-        upstream = g_ref[rows, :] * geo.mask(start, 16, width, count) * (part * (1.0 + pre * (1.0 - part)))
-        g_ref[rows, :] = upstream
+        g_out.ref[rows, :] = upstream.astype(BF16)
         return plain + fold_rows(upstream), scaled + fold_rows(upstream * normed)
 
     zero = jnp.zeros((8, width), F32)
@@ -500,24 +504,24 @@
 
     def one(start, carry):
         rows = pl.ds(start, step)
-        centered = z_ref[rows, :] - average
-        value = factor * (g_ref[rows, :] - plain_part - centered * scaled_part)
+        centered = z_ref[rows, :].astype(F32) - average
+        value = factor * (g_ref[rows, :].astype(F32) - plain_part - centered * scaled_part)
         out_ref[rows, :] = (value * geo.mask(start, step, width, count)).astype(out_ref.dtype)
         return carry
 
     over_rows(rows_of, step, one, 0)
 
 
-def silu_back(geo, z_ref, average, inverse, gain, offset, g_ref):
+def silu_back(geo, z_ref, average, inverse, gain, offset, g_ref, out_ref):
     rows_of, width = z_ref.shape
     step = step_of(width)
 
     def one(start, carry):
         plain, scaled = carry
         rows = pl.ds(start, step)
-        normed = (z_ref[rows, :] - average) * inverse
+        normed = (z_ref[rows, :].astype(F32) - average) * inverse
         upstream = g_ref[rows, :] * slope(normed * gain + offset) * geo.mask(start, step, width)
-        g_ref[rows, :] = upstream
+        out_ref[rows, :] = upstream.astype(out_ref.dtype)
         return plain + fold_rows(upstream), scaled + fold_rows(upstream * normed)
 
     zero = jnp.zeros((8, width), F32)
@@ -549,7 +553,11 @@
     g_out.ref[...] = dot_back(dv.ref[...], weight[...])
     send_rows(
         sent,
-        (silu_back(geo, z2.get(), mom2[0:1, :], mom2[1:2, :], narrow[1:2, :], narrow[3:4, :], g_out.ref),),
+        (
+            silu_back(
+                geo, z2.get(), mom2[0:1, :], mom2[1:2, :], narrow[1:2, :], narrow[3:4, :], g_out.ref, g_out.ref
+            ),
+        ),
     )
     sent.send()
     g_out.send()
@@ -564,7 +572,7 @@
 
 
 def tap_back(geo, planes, block, place, counts, got, g_in, z2, mom2, narrow, z1, mom1, own, other, dv, g_out, sums, sent,
-             wide_dv, weight, sem):
+             work, wide_dv, weight, sem):
     section = place[1]
     count = counts[section, place[0]]
     choice = Choice(section, block, own, other, weight, sem.at[0])
@@ -581,8 +589,7 @@
     dv.ref[...] = wide_dv[...].astype(BF16)
     dv.send()
     choice.wait()
-    g_ref = g_out.ref
-    width = g_ref.shape[1]
+    width = work.shape[1]
     ready = {}
     totals = [None] * planes
     for tap, (plane, line, column) in enumerate(taps_of(2 if planes == 4 else 1)):
@@ -595,15 +602,19 @@
         product = dot_back(left, weight[tap * width : (tap + 1) * width, :])
         totals[plane] = product if totals[plane] is None else totals[plane] + product
     for plane in range(planes):
-        g_ref[plane * geo.rows : (plane + 1) * geo.rows, :] = totals[plane]
+        work[plane * geo.rows : (plane + 1) * geo.rows, :] = totals[plane]
     send_rows(
         sent,
-        (silu_back(geo, z1.get(), mom1[0:1, :], mom1[1:2, :], narrow[0:1, :], narrow[2:3, :], g_ref),),
+        (
+            silu_back(
+                geo, z1.get(), mom1[0:1, :], mom1[1:2, :], narrow[0:1, :], narrow[2:3, :], work, g_out.ref
+            ),
+        ),
     )
 
 
 def join_back(geo, place, counts, got, g_in, u1, mom4, narrow, weight, g3, z3, zs, mom3, wide, short, dv, g_out, sums,
-              sent):
+              sent, flat):
     section = place[1]
     count = counts[section, place[0]]
     total = total_of(counts, section, geo.pixels)
@@ -616,23 +627,22 @@
         dv.ref,
     )
     dv.send()
-    g_ref = g_out.ref
-    g_ref[...] = dot_back(dv.ref[...], weight.get()[...])
+    flat[...] = dot_back(dv.ref[...], weight.get()[...])
     average_c, inverse_c = mom3[0:1, :], mom3[1:2, :]
     average_s, inverse_s = mom3[2:3, :], mom3[3:4, :]
     gain_c, gain_s = wide[0:1, :], short[0:1, :]
     offset = wide[1:2, :] + short[1:2, :]
-    width = g_ref.shape[1]
+    width = flat.shape[1]
     g3, z3, zs = g3.get(), z3.get(), zs.get()
 
     def one(start, carry):
         plain, scaled_c, scaled_s = carry
         rows = pl.ds(start, 16)
-        normed_c = (z3[rows, :] - average_c) * inverse_c
-        normed_s = (zs[rows, :] - average_s) * inverse_s
-        arrived = (g_ref[rows, :] + g3[rows, :]).astype(BF16).astype(F32)
+        normed_c = (z3[rows, :].astype(F32) - average_c) * inverse_c
+        normed_s = (zs[rows, :].astype(F32) - average_s) * inverse_s
+        arrived = (flat[rows, :] + g3[rows, :].astype(F32)).astype(BF16).astype(F32)
         upstream = arrived * slope(normed_c * gain_c + normed_s * gain_s + offset) * geo.mask(start, 16, width)
-        g_ref[rows, :] = upstream
+        g_out.ref[rows, :] = upstream.astype(BF16)
         return (
             plain + fold_rows(upstream),
             scaled_c + fold_rows(upstream * normed_c),
@@ -883,7 +893,7 @@
 
     x, z1, sent = stage(
         bound(first_kernel),
-        (spec((all_rows, c_in), BF16), spec((all_rows, mid)), spec((devices, 2, mid))),
+        (spec((all_rows, c_in), BF16), spec((all_rows, mid), BF16), spec((devices, 2, mid))),
         "ddd",
         (place, counts, images, w_reduce0),
         "ssad",
@@ -896,7 +906,7 @@
     got = exchange(sent)
     zs, stats_s = stage(
         bound(short_kernel),
-        (spec((rows, out)), spec((2, out))),
+        (spec((rows, out), BF16), spec((2, out))),
         "dd",
         (place, counts, x, w_short),
         "ssad",
@@ -916,7 +926,7 @@
     expand_scratch = (pltpu.VMEM((mid, out), BF16), dma(1))
     a2, z3, mom2, moments_s, sent = stage(
         bound(expand_kernel, 0, True),
-        (spec((rows, mid), BF16), spec((rows, out)), spec((2, mid)), spec((2, out)), spec((devices, 2, out))),
+        (spec((rows, mid), BF16), spec((rows, out), BF16), spec((2, mid)), spec((2, out)), spec((devices, 2, out))),
         "ddddd",
         (place, counts, got, z2, narrow0, w_expand, expand_other),
         "ssgddaa",
@@ -945,7 +955,7 @@
     got, joined_other = partner(joined, got)
     c2, u3, mom5, sent = stage(
         bound(expand_kernel, 1, False),
-        (spec((rows, mid), BF16), spec((rows, out)), spec((2, mid)), spec((devices, 2, out))),
+        (spec((rows, mid), BF16), spec((rows, out), BF16), spec((2, mid)), spec((devices, 2, out))),
         "dddd",
         (place, counts, got, u2, narrow1, w_expand, expand_other),
         "ssgddaa",
@@ -957,7 +967,7 @@
         bound(turn_kernel),
         (
             spec((1, side, side, slots, out), BF16),
-            spec((rows, out)),
+            spec((rows, out), BF16),
             spec((2, out)),
             spec((devices, 2, out)),
         ),
@@ -985,7 +995,7 @@
         "dddd",
         (place, counts, got, g2, u2, mom5, narrow1, u1, mom4, w_mid, mid_other),
         "ssgddddddaa",
-        tap_back_scratch,
+        (pltpu.VMEM((rows, mid), F32),) + tap_back_scratch,
     )
     got = exchange(sent)
     def tied(value, starting=(), arrived=()):
@@ -1009,10 +1019,11 @@
         got = tied(got, (first,))
     du1, gj, sums4, sent = stage(
         bound(join_back),
-        (spec((rows, mid), BF16), spec((rows, out)), spec((2, mid)), spec((devices, 2, out + out // 2), BF16)),
+        (spec((rows, mid), BF16), spec((rows, out), BF16), spec((2, mid)), spec((devices, 2, out + out // 2), BF16)),
         "dddd",
         (place, counts, got, g1, u1, mom4, narrow1, w_reduce1, g3, z3, zs, mom3, wide0, short),
         "ssgddddddddddd",
+        (pltpu.VMEM((rows, out), F32),),
     )
     got = exchange(sent)
     got, du1_other = partner(du1, got)
@@ -1048,11 +1059,11 @@
         got = tied(got, (second,), (first,))
     dz2, g1, sums2, sent = stage(
         bound(tap_back, 4, 0),
-        (spec((rows, mid), BF16), spec((all_rows, mid)), spec((2, mid)), spec((devices, 2, mid))),
+        (spec((rows, mid), BF16), spec((all_rows, mid), BF16), spec((2, mid)), spec((devices, 2, mid))),
         "dddd",
         (place, counts, got, g2, z2, mom2, narrow0, z1, mom1, w_mid, mid_other),
         "ssgddddddaa",
-        tap_back_scratch,
+        (pltpu.VMEM((all_rows, mid), F32),) + tap_back_scratch,
     )
     got = exchange(sent)
     got, dz2_other = partner(dz2, got)

time: 342 us -> 339 us (level)
  Pallas kernels: 121 us -> 116 us
    pallas_call x18, Pallas kernels: 121 us -> 116 us  [stage(): pl.pallas_call(run, out_shape=list(outs), in_specs=[kinds[kind] for kind...]
where the time goes in v1:
time: 339 us; the launch traced here: 337 us
  Pallas kernels  116 us (34%)
  starting transfers between devices  96.5 us (28%)
  waiting for transfers between devices  69.8 us (21%)
  blocking collectives  30.7 us (9%)
  other arithmetic  18.5 us (5%)
  local copies, waits for them, and re-layouts  4.02 us (1%)
    pallas_call x18, Pallas kernels, stage(): pl.pallas_call(run, out_shape=list(outs), in_specs=[kinds[kind] for kind...  116 us
    all_to_all x9, starting transfers between devices, exchange(): return lax.all_to_all(sent, 'dp', 0, 0)  49.3 us
    ppermute x21, waiting for transfers between devices, across(): lax.ppermute(value, 'dp', [(i, i ^ mask) for i in range(lax.axis_size('dp...  37.6 us
    all_to_all x3, blocking collectives, exchange(): return lax.all_to_all(sent, 'dp', 0, 0)  30.7 us
    all_to_all x9, waiting for transfers between devices, exchange(): return lax.all_to_all(sent, 'dp', 0, 0)  29.6 us
    ppermute x21, starting transfers between devices, swapped(): return lax.ppermute(value, 'section', [(0, 1), (1, 0)])  28.5 us
    ppermute x21, starting transfers between devices, across(): lax.ppermute(value, 'dp', [(i, i ^ mask) for i in range(lax.axis_size('dp...  18.7 us
  transfers between devices with their start and end apart: 51, of which 16 were waited for; matrix products, arithmetic and copies ran while one was open for 5% of the time, Pallas kernels for 24%

profile of v1, /device:TPU:9, one launch (start us, length us, event | category | flops | bytes accessed | tf_op | source)
XLA Modules:
  0.0 336.9 jit_solution(11123498497539731825)
XLA Ops:
  2.1 6.2 %shard_map.229 = (bf16[1024,1024]{1,0:T(8,128)(2,1)}, bf16[1024,512]{1,0:T(8,128)(2,1)}, f32[16,2,512]{2,1,0:T(2,128)}) custom-call(s32[2]{0:T(128)} %pad_add_fusion.refs_0_, s32[2,16]{1,0:T(2,128)} %bitcast.91, bf16[2,14,14,4,1024]{4,3,2,1,0:T(4,128)(2,1)} %bitcast.88, bf16[1024,512]{1,0:T(8,128)(2,1)} %refs_1_.1), custom_call_target="tpu_custom_call" | custom-call | tf_op jit(solution)/shard_map/pallas_call | solution.py:87
  9.1 6.7 %all-to-all-start = ((f32[16,2,512]{2,1,0:T(2,128)}), f32[16,2,512]{2,1,0:T(2,128)S(1)}, u32[]{:S(2)}, u32[]{:S(2)}) async-start(f32[16,2,512]{2,1,0:T(2,128)} %get-tuple-element.147), calls=%async_computation | async-start | bytes 131072 | tf_op jit(solution)/shard_map/all_to_all | solution.py:700
  15.7 5.8 %shard_map.230 = (bf16[256,2048]{1,0:T(8,128)(2,1)}, f32[2,2048]{1,0:T(2,128)}) custom-call(s32[2]{0:T(128)} %pad_add_fusion.refs_0_, s32[2,16]{1,0:T(2,128)} %bitcast.92, bf16[1024,1024]{1,0:T(8,128)(2,1)} %get-tuple-element.149.refs_2_.refs_9_.refs_5_, bf16[1024,2048]{1,0:T(8,128)(2,1)} %refs_3_.5), custom_call_target="tpu_custom_call" | custom-call | tf_op jit(solution)/shard_map/pallas_call | solution.py:87
  22.2 6.0 %shard_map.231 = (bf16[256,4608]{1,0:T(8,128)(2,1)}, f32[256,512]{1,0:T(8,128)}, f32[2,512]{1,0:T(2,128)}, bf16[16,2,3840]{2,1,0:T(2,128)(2,1)}) custom-call(s32[2]{0:T(128)} %pad_add_fusion.refs_0_, s32[2,16]{1,0:T(2,128)} %bitcast.93, f32[16,2,512]{2,1,0:T(2,128)S(1)} %all-to-all-done.refs_2_, ...), custom_call_target="tpu_custom_call" | custom-call | tf_op jit(solution)/shard_map/pallas_call | solution.py:87
  29.2 6.4 %all-to-all-start.1 = ((bf16[16,2,3840]{2,1,0:T(2,128)(2,1)}), bf16[16,2,3840]{2,1,0:T(2,128)(2,1)S(1)}, u32[]{:S(2)}, u32[]{:S(2)}) async-start(bf16[16,2,3840]{2,1,0:T(2,128)(2,1)} %get-tuple-element.151), calls=%async_computation.1 | async-start | bytes 491520 | tf_op jit(solution)/shard_map/all_to_all | solution.py:700
  36.3 6.7 %all-to-all-done.1.refs_2_ = bf16[16,2,3840]{2,1,0:T(2,128)(2,1)S(1)} async-done(((bf16[16,2,3840]{2,1,0:T(2,128)(2,1)}), bf16[16,2,3840]{2,1,0:T(2,128)(2,1)S(1)}, u32[]{:S(2)}, u32[]{:S(2)}) %all-to-all-start.1) | async-done | bytes 245792 | tf_op jit(solution)/shard_map/all_to_all | solution.py:700
  43.0 5.2 %shard_map.232 = (bf16[256,512]{1,0:T(8,128)(2,1)}, bf16[256,2048]{1,0:T(8,128)(2,1)}, f32[2,512]{1,0:T(2,128)}, f32[2,2048]{1,0:T(2,128)}, f32[16,2,2048]{2,1,0:T(2,128)}) custom-call(s32[2]{0:T(128)} %pad_add_fusion.refs_0_, s32[2,16]{1,0:T(2,128)} %bitcast.94, bf16[16,2,3840]{2,1,0:T(2,128)(2,1)S(1)} %all-to-all-done.1.refs_2_, ...), custom_call_target="tpu_custom_call" | custom-call | tf_op jit(solution)/shard_map/pallas_call | solution.py:87
  48.1 5.4 %all-to-all-start.2 = ((f32[16,2,2048]{2,1,0:T(2,128)}), f32[16,2,2048]{2,1,0:T(2,128)S(1)}, u32[]{:S(2)}, u32[]{:S(2)}) async-start(f32[16,2,2048]{2,1,0:T(2,128)} %get-tuple-element.154), calls=%async_computation.2 | async-start | bytes 524288 | tf_op jit(solution)/shard_map/all_to_all | solution.py:700
  54.1 1.6 collective-permute-start.6
  56.3 4.0 %all-to-all-done.2.refs_2_ = f32[16,2,2048]{2,1,0:T(2,128)S(1)} async-done(((f32[16,2,2048]{2,1,0:T(2,128)}), f32[16,2,2048]{2,1,0:T(2,128)S(1)}, u32[]{:S(2)}, u32[]{:S(2)}) %all-to-all-start.2) | async-done | bytes 262176 | tf_op jit(solution)/shard_map/all_to_all | solution.py:700
  60.3 5.5 %shard_map.233 = (bf16[256,2048]{1,0:T(8,128)(2,1)}, f32[256,512]{1,0:T(8,128)}, f32[4,2048]{1,0:T(4,128)}, f32[16,2,512]{2,1,0:T(2,128)}) custom-call(s32[2]{0:T(128)} %pad_add_fusion.refs_0_, s32[2,16]{1,0:T(2,128)} %bitcast.95, f32[16,2,2048]{2,1,0:T(2,128)S(1)} %all-to-all-done.2.refs_2_, bf16[256,2048]{1,0:T(8,128)(2,1)} %get-tuple-element.157.refs_3_.refs_9_.refs_4_, ...), custom_call_target="tpu_custom_call" | custom-call | tf_op jit(solution)/shard_map/pallas_call | solution.py:87
  65.9 5.9 %all-to-all-start.3 = ((f32[16,2,512]{2,1,0:T(2,128)}), f32[16,2,512]{2,1,0:T(2,128)S(1)}, u32[]{:S(2)}, u32[]{:S(2)}) async-start(f32[16,2,512]{2,1,0:T(2,128)} %get-tuple-element.160), calls=%async_computation.3 | async-start | bytes 131072 | tf_op jit(solution)/shard_map/all_to_all | solution.py:700
  71.8 5.4 %all-to-all-done.3.refs_2_ = f32[16,2,512]{2,1,0:T(2,128)S(1)} async-done(((f32[16,2,512]{2,1,0:T(2,128)}), f32[16,2,512]{2,1,0:T(2,128)S(1)}, u32[]{:S(2)}, u32[]{:S(2)}) %all-to-all-start.3) | async-done | bytes 65568 | tf_op jit(solution)/shard_map/all_to_all | solution.py:700
  77.3 5.9 %shard_map.234 = (bf16[256,4608]{1,0:T(8,128)(2,1)}, f32[256,512]{1,0:T(8,128)}, f32[2,512]{1,0:T(2,128)}, f32[16,2,512]{2,1,0:T(2,128)}) custom-call(s32[2]{0:T(128)} %pad_add_fusion.refs_0_, s32[2,16]{1,0:T(2,128)} %bitcast.96, f32[16,2,512]{2,1,0:T(2,128)S(1)} %all-to-all-done.3.refs_2_, f32[256,512]{1,0:T(8,128)} %get-tuple-element.163.refs_3_.refs_7_.refs_4_, ...), custom_call_target="tpu_custom_call" | custom-call | tf_op jit(solution)/shard_map/pallas_call | solution.py:87
  83.2 2.8 collective-permute-start.8
  86.1 9.9 %all_to_all.60.refs_2_ = f32[16,2,512]{2,1,0:T(2,128)S(1)} all-to-all(f32[16,2,512]{2,1,0:T(2,128)} %get-tuple-element.164), channel_id=1, replica_groups=mesh['section'=2,'dp'=16] {'dp'}, dimensions={0} | all-to-all | bytes 131072 | tf_op jit(solution)/shard_map/all_to_all | solution.py:700
  96.0 4.9 %shard_map.235 = (bf16[256,512]{1,0:T(8,128)(2,1)}, bf16[256,2048]{1,0:T(8,128)(2,1)}, f32[2,512]{1,0:T(2,128)}, f32[16,2,2048]{2,1,0:T(2,128)}) custom-call(s32[2]{0:T(128)} %pad_add_fusion.refs_0_, s32[2,16]{1,0:T(2,128)} %bitcast.97, f32[16,2,512]{2,1,0:T(2,128)S(1)} %all_to_all.60.refs_2_, f32[256,512]{1,0:T(8,128)} %get-tuple-element.167.refs_3_.refs_7_.refs_4_, ...), custom_call_target="tpu_custom_call" | custom-call | tf_op jit(solution)/shard_map/pallas_call | solution.py:87
  100.9 11.3 %all_to_all.61.refs_2_ = f32[16,2,2048]{2,1,0:T(2,128)S(1)} all-to-all(f32[16,2,2048]{2,1,0:T(2,128)} %get-tuple-element.168), channel_id=1, replica_groups=mesh['section'=2,'dp'=16] {'dp'}, dimensions={0} | all-to-all | bytes 524288 | tf_op jit(solution)/shard_map/all_to_all | solution.py:700
  112.1 6.4 %shard_map.236 = (bf16[1,7,7,4,2048]{4,3,2,1,0:T(4,128)(2,1)}, bf16[256,2048]{1,0:T(8,128)(2,1)}, f32[2,2048]{1,0:T(2,128)}, f32[16,2,2048]{2,1,0:T(2,128)}) custom-call(s32[2]{0:T(128)} %pad_add_fusion.refs_0_, s32[2,16]{1,0:T(2,128)} %bitcast.98, f32[16,2,2048]{2,1,0:T(2,128)S(1)} %all_to_all.61.refs_2_, ...), custom_call_target="tpu_custom_call" | custom-call | tf_op jit(solution)/shard_map/pallas_call | solution.py:87
  118.6 5.8 %all-to-all-start.6 = ((f32[16,2,2048]{2,1,0:T(2,128)}), f32[16,2,2048]{2,1,0:T(2,128)S(1)}, u32[]{:S(2)}, u32[]{:S(2)}) async-start(f32[16,2,2048]{2,1,0:T(2,128)} %get-tuple-element.173), calls=%async_computation.6 | async-start | bytes 524288 | tf_op jit(solution)/shard_map/all_to_all | solution.py:700
  124.4 2.1 collective-permute-start.9
  127.6 3.5 %all-to-all-done.6.refs_2_ = f32[16,2,2048]{2,1,0:T(2,128)S(1)} async-done(((f32[16,2,2048]{2,1,0:T(2,128)}), f32[16,2,2048]{2,1,0:T(2,128)S(1)}, u32[]{:S(2)}, u32[]{:S(2)}) %all-to-all-start.6) | async-done | bytes 262176 | tf_op jit(solution)/shard_map/all_to_all | solution.py:700
  131.1 5.4 %shard_map.237 = (bf16[256,2048]{1,0:T(8,128)(2,1)}, f32[256,512]{1,0:T(8,128)}, f32[2,2048]{1,0:T(2,128)}, f32[16,2,512]{2,1,0:T(2,128)}) custom-call(s32[2]{0:T(128)} %pad_add_fusion.refs_0_, s32[2,16]{1,0:T(2,128)} %bitcast.99, f32[16,2,2048]{2,1,0:T(2,128)S(1)} %all-to-all-done.6.refs_2_, bf16[256,2048]{1,0:T(8,128)(2,1)} %get-tuple-element.176.refs_3_.refs_8_, ...), custom_call_target="tpu_custom_call" | custom-call | tf_op jit(solution)/shard_map/pallas_call | solution.py:87
  136.5 3.6 %collective-permute-start.10 = (bf16[256,2048]{1,0:T(8,128)(2,1)}, bf16[256,2048]{1,0:T(8,128)(2,1)S(1)}, u32[]{:S(2)}, u32[]{:S(2)}) collective-permute-start(bf16[256,2048]{1,0:T(8,128)(2,1)} %get-tuple-element.180.refs_3_), channel_id=1, source_target_pairs={{0,16},{16,0},{1,17},{17,1},{2,18},{18,2},{3,19},{19,3},{4,20},{20... | collective-permute-start | bytes 3145736 | tf_op jit(solution)/shard_map/ppermute | solution.py:704
  140.1 9.6 %all_to_all.62.refs_2_ = f32[16,2,512]{2,1,0:T(2,128)S(1)} all-to-all(f32[16,2,512]{2,1,0:T(2,128)} %get-tuple-element.179), channel_id=1, replica_groups=mesh['section'=2,'dp'=16] {'dp'}, dimensions={0} | all-to-all | bytes 131072 | tf_op jit(solution)/shard_map/all_to_all | solution.py:700
  149.7 6.4 %shard_map.238 = (bf16[256,512]{1,0:T(8,128)(2,1)}, f32[256,512]{1,0:T(8,128)}, f32[2,512]{1,0:T(2,128)}, f32[16,2,512]{2,1,0:T(2,128)}) custom-call(s32[2]{0:T(128)} %pad_add_fusion.refs_0_, s32[2,16]{1,0:T(2,128)} %bitcast.100, f32[16,2,512]{2,1,0:T(2,128)S(1)} %all_to_all.62.refs_2_, f32[256,512]{1,0:T(8,128)} %get-tuple-element.182.refs_3_, ...), custom_call_target="tpu_custom_call" | custom-call | tf_op jit(solution)/shard_map/pallas_call | solution.py:87
  156.2 1.3 collective-permute-start.11
  157.5 4.4 %all-to-all-start.8 = ((f32[16,2,512]{2,1,0:T(2,128)}), f32[16,2,512]{2,1,0:T(2,128)S(1)}, u32[]{:S(2)}, u32[]{:S(2)}) async-start(f32[16,2,512]{2,1,0:T(2,128)} %get-tuple-element.184), calls=%async_computation.8 | async-start | bytes 131072 | tf_op jit(solution)/shard_map/all_to_all | solution.py:700
  161.9 7.2 %shard_map.239 = (bf16[2,4,208,256]{3,2,1,0:T(8,128)(2,1)}, bf16[2,4,208,256]{3,2,1,0:T(8,128)(2,1)}, bf16[2,4,208,256]{3,2,1,0:T(8,128)(2,1)}, bf16[2,4,208,256]{3,2,1,0:T(8,128)(2,1)}) custom-call(s32[2]{0:T(128)} %pad_add_fusion.refs_0_, bf16[256,512]{1,0:T(8,128)(2,1)} %get-tuple-element.174.refs_1_, bf16[256,512]{1,0:T(8,128)(2,1)} %copy-done.17, ...), custom_call_target="tpu_custom_call" | custom-call | tf_op jit(solution)/shard_map/pallas_call | solution.py:87
  169.2 1.3 collective-permute-start.13
  171.6 8.0 %shard_map.240 = (bf16[256,512]{1,0:T(8,128)(2,1)}, bf16[256,2048]{1,0:T(8,128)(2,1)}, f32[2,512]{1,0:T(2,128)}, bf16[16,2,3072]{2,1,0:T(2,128)(2,1)}) custom-call(s32[2]{0:T(128)} %pad_add_fusion.refs_0_, s32[2,16]{1,0:T(2,128)} %bitcast.101, f32[16,2,512]{2,1,0:T(2,128)S(1)} %all-to-all-done.8.refs_2_, f32[256,512]{1,0:T(8,128)} %get-tuple-element.192.refs_3_, ...), custom_call_target="tpu_custom_call" | custom-call | tf_op jit(solution)/shard_map/pallas_call | solution.py:87
  179.6 4.6 %all-to-all-start.9 = ((bf16[16,2,3072]{2,1,0:T(2,128)(2,1)}), bf16[16,2,3072]{2,1,0:T(2,128)(2,1)S(1)}, u32[]{:S(2)}, u32[]{:S(2)}) async-start(bf16[16,2,3072]{2,1,0:T(2,128)(2,1)} %get-tuple-element.194), calls=%async_computation.9 | async-start | bytes 393216 | tf_op jit(solution)/shard_map/all_to_all | solution.py:700
  184.2 1.4 collective-permute-start.12
  185.6 1.4 collective-permute-done.12.refs_4_
  187.0 5.5 %all-to-all-done.9.refs_2_ = bf16[16,2,3072]{2,1,0:T(2,128)(2,1)S(1)} async-done(((bf16[16,2,3072]{2,1,0:T(2,128)(2,1)}), bf16[16,2,3072]{2,1,0:T(2,128)(2,1)S(1)}, u32[]{:S(2)}, u32[]{:S(2)}) %all-to-all-start.9) | async-done | bytes 196640 | tf_op jit(solution)/shard_map/all_to_all | solution.py:700
  192.6 2.1 fusion.12
  194.6 6.7 %shard_map.241 = (bf16[256,2048]{1,0:T(8,128)(2,1)}, bf16[256,2048]{1,0:T(8,128)(2,1)}, f32[256,512]{1,0:T(8,128)}, f32[3,2048]{1,0:T(4,128)}, f32[16,2,512]{2,1,0:T(2,128)}) custom-call(s32[2]{0:T(128)} %pad_add_fusion.refs_0_, s32[2,16]{1,0:T(2,128)} %bitcast.102, bf16[16,2,3072]{2,1,0:T(2,128)(2,1)S(1)} %all-to-all-done.9.refs_2_, ...), custom_call_target="tpu_custom_call" | custom-call | tf_op jit(solution)/shard_map/pallas_call | solution.py:87
  201.4 1.7 collective-permute-start.15
  204.6 5.5 %all-to-all-start.10 = ((f32[16,2,512]{2,1,0:T(2,128)}), f32[16,2,512]{2,1,0:T(2,128)S(1)}, u32[]{:S(2)}, u32[]{:S(2)}) async-start(f32[16,2,512]{2,1,0:T(2,128)} %get-tuple-element.204), calls=%async_computation.10 | async-start | bytes 131072 | tf_op jit(solution)/shard_map/all_to_all | solution.py:700
  210.1 7.9 %shard_map.242 = (bf16[2,4,256,256]{3,2,1,0:T(8,128)(2,1)}, bf16[2,4,256,256]{3,2,1,0:T(8,128)(2,1)}, bf16[2,4,256,256]{3,2,1,0:T(8,128)(2,1)}, bf16[2,4,256,256]{3,2,1,0:T(8,128)(2,1)}) custom-call(s32[2]{0:T(128)} %pad_add_fusion.refs_0_, bf16[256,2048]{1,0:T(8,128)(2,1)} %get-tuple-element.165.refs_4_.refs_1_, bf16[256,2048]{1,0:T(8,128)(2,1)} %copy-done.3, ...), custom_call_target="tpu_custom_call" | custom-call | tf_op jit(solution)/shard_map/pallas_call | solution.py:87
  218.0 1.2 collective-permute-start.20
  220.5 8.2 %shard_map.243 = (bf16[256,512]{1,0:T(8,128)(2,1)}, bf16[1024,512]{1,0:T(8,128)(2,1)}, f32[2,512]{1,0:T(2,128)}, f32[16,2,512]{2,1,0:T(2,128)}) custom-call(s32[2]{0:T(128)} %pad_add_fusion.refs_0_, s32[2,16]{1,0:T(2,128)} %bitcast.103, f32[16,2,512]{2,1,0:T(2,128)S(1)} %all-to-all-done.10.refs_2_, f32[256,512]{1,0:T(8,128)} %get-tuple-element.216.refs_3_, ...), custom_call_target="tpu_custom_call" | custom-call | tf_op jit(solution)/shard_map/pallas_call | solution.py:87
  228.7 4.6 %all-to-all-start.11 = ((f32[16,2,512]{2,1,0:T(2,128)}), f32[16,2,512]{2,1,0:T(2,128)S(1)}, u32[]{:S(2)}, u32[]{:S(2)}) async-start(f32[16,2,512]{2,1,0:T(2,128)} %get-tuple-element.218), calls=%async_computation.11 | async-start | bytes 131072 | tf_op jit(solution)/shard_map/all_to_all | solution.py:700
  233.3 2.7 collective-permute-start.19
  236.0 1.6 fusion.9
  238.5 4.6 %all-to-all-done.11.refs_2_ = f32[16,2,512]{2,1,0:T(2,128)S(1)} async-done(((f32[16,2,512]{2,1,0:T(2,128)}), f32[16,2,512]{2,1,0:T(2,128)S(1)}, u32[]{:S(2)}, u32[]{:S(2)}) %all-to-all-start.11) | async-done | bytes 65568 | tf_op jit(solution)/shard_map/all_to_all | solution.py:700
  245.5 4.2 %shard_map.244 = (bf16[1024,512]{1,0:T(8,128)(2,1)}, f32[2,512]{1,0:T(2,128)}) custom-call(s32[2]{0:T(128)} %pad_add_fusion.refs_0_, s32[2,16]{1,0:T(2,128)} %bitcast.104, f32[16,2,512]{2,1,0:T(2,128)S(1)} %all-to-all-done.11.refs_2_, bf16[1024,512]{1,0:T(8,128)(2,1)} %get-tuple-element.228.refs_3_, ...), custom_call_target="tpu_custom_call" | custom-call | tf_op jit(solution)/shard_map/pallas_call | solution.py:87
  249.7 2.8 collective-permute-start.22
  252.5 1.2 collective-permute-start.23
  255.0 2.1 collective-permute-start.26
  257.1 1.3 broadcast_select_fusion.7
  259.4 9.9 %shard_map.245 = (bf16[2,4,176,256]{3,2,1,0:T(8,128)(2,1)}, bf16[2,4,176,256]{3,2,1,0:T(8,128)(2,1)}, bf16[2,4,176,256]{3,2,1,0:T(8,128)(2,1)}, bf16[2,4,176,256]{3,2,1,0:T(8,128)(2,1)}) custom-call(s32[2]{0:T(128)} %pad_add_fusion.refs_0_, bf16[256,4608]{1,0:T(8,128)(2,1)} %get-tuple-element.155.refs_1_, bf16[256,4608]{1,0:T(8,128)(2,1)} %collective-permute-done.4.refs_2_, ...), custom_call_target="tpu_custom_call" | custom-call | tf_op jit(solution)/shard_map/pallas_call | solution.py:87
  271.7 4.2 %collective-permute-done.27 = bf16[208,512]{1,0:T(8,128)(2,1)} collective-permute-done((bf16[208,512]{1,0:T(8,128)(2,1)}, bf16[208,512]{1,0:T(8,128)(2,1)}, u32[]{:S(2)}, u32[]{:S(2)}) %collective-permute-start.27) | collective-permute-done | bytes 213024 | tf_op jit(solution)/shard_map/ppermute | solution.py:708
  275.9 1.7 collective-permute-start.29
  279.0 1.2 collective-permute-start.30
  280.5 5.9 %shard_map.246 = bf16[1,14,14,4,1024]{4,3,2,1,0:T(4,128)(2,1)} custom-call(bf16[1024,512]{1,0:T(8,128)(2,1)} %get-tuple-element.249.refs_7_.refs_0_, bf16[1024,512]{1,0:T(8,128)(2,1)} %refs_1_.1, bf16[256,2048]{1,0:T(8,128)(2,1)} %get-tuple-element.210.refs_11_.refs_2_, bf16[1024,2048]{1,0:T(8,128)(2,1)} %refs_3_.5), custom_call_target="tpu_custom_call" | custom-call | tf_op jit(solution)/shard_map/pallas_call | solution.py:87
  286.6 2.3 collective-permute-start.38
  291.8 4.7 %collective-permute-done.30 = bf16[2,4,176,256]{3,2,1,0:T(8,128)(2,1)S(1)} collective-permute-done((bf16[2,4,176,256]{3,2,1,0:T(8,128)(2,1)}, bf16[2,4,176,256]{3,2,1,0:T(8,128)(2,1)S(1)}, u32[]{:S(2)}, u32[]{:S(2)}) %collective-permute-start.30) | collective-permute-done | bytes 720928 | tf_op jit(solution)/shard_map/ppermute | solution.py:708
  299.8 11.3 %collective-permute-done.39 = bf16[256,512]{1,0:T(8,128)(2,1)S(1)} collective-permute-done((bf16[256,512]{1,0:T(8,128)(2,1)S(1)}, bf16[256,512]{1,0:T(8,128)(2,1)S(1)}, u32[]{:S(2)}, u32[]{:S(2)}) %collective-permute-start.39) | collective-permute-done | bytes 262176 | tf_op jit(solution)/shard_map/ppermute | solution.py:708
  312.0 2.3 collective-permute-start.41
  314.5 2.3 collective-permute-start.35
  317.9 4.0 %collective-permute-done.34 = bf16[176,512]{1,0:T(8,128)(2,1)S(1)} collective-permute-done((bf16[176,512]{1,0:T(8,128)(2,1)S(1)}, bf16[176,512]{1,0:T(8,128)(2,1)S(1)}, u32[]{:S(2)}, u32[]{:S(2)}) %collective-permute-start.34) | collective-permute-done | bytes 180256 | tf_op jit(solution)/shard_map/ppermute | solution.py:708
  321.9 6.2 %collective-permute-done.35 = bf16[176,512]{1,0:T(8,128)(2,1)S(1)} collective-permute-done((bf16[176,512]{1,0:T(8,128)(2,1)S(1)}, bf16[176,512]{1,0:T(8,128)(2,1)S(1)}, u32[]{:S(2)}, u32[]{:S(2)}) %collective-permute-start.35) | collective-permute-done | bytes 180256 | tf_op jit(solution)/shard_map/ppermute | solution.py:708
  328.1 5.0 %collective-permute-done.36 = bf16[176,512]{1,0:T(8,128)(2,1)S(1)} collective-permute-done((bf16[176,512]{1,0:T(8,128)(2,1)S(1)}, bf16[176,512]{1,0:T(8,128)(2,1)S(1)}, u32[]{:S(2)}, u32[]{:S(2)}) %collective-permute-start.36) | collective-permute-done | bytes 180256 | tf_op jit(solution)/shard_map/ppermute | solution.py:708
  (169 shorter events, 32.3 us)
Async XLA Ops:
  0.7 21.5 %collective-permute-start.1 = (bf16[1,4608,512]{2,1,0:T(8,128)(2,1)}, bf16[1,4608,512]{2,1,0:T(8,128)(2,1)}, u32[]{:S(2)}, u32[]{:S(2)}) collective-permute-start(bf16[1,4608,512]{2,1,0:T(8,128)(2,1)} %refs_9_.3), channel_id=1, source_target_pairs={{0,16},{16,0},{1,17},{17,1},{2,18},{18,2},{3,19},{19,3},{4,20},{20... | collective-permute-start | bytes 14155784 | tf_op jit(solution)/shard_map/ppermute | solution.py:704
  8.3 28.0 %collective-permute-start.2 = (bf16[1024,1024]{1,0:T(8,128)(2,1)}, bf16[1024,1024]{1,0:T(8,128)(2,1)}, u32[]{:S(2)}, u32[]{:S(2)}) collective-permute-start(bf16[1024,1024]{1,0:T(8,128)(2,1)} %get-tuple-element.149.refs_2_.refs_9_.refs_5_), channel_id=1, source_target_pairs={{0,16},{16,0},{1,17},{17,1},{2,18},{18,2},{3,19},{19,3},{4,20},{20... | collective-permute-start | bytes 6291464 | tf_op jit(solution)/shard_map/ppermute | solution.py:704
  8.4 34.5 %collective-permute-start.3 = (bf16[1,512,2048]{2,1,0:T(8,128)(2,1)S(1)}, bf16[1,512,2048]{2,1,0:T(8,128)(2,1)}, u32[]{:S(2)}, u32[]{:S(2)}) collective-permute-start(bf16[1,512,2048]{2,1,0:T(8,128)(2,1)S(1)} %copy-done), channel_id=1, source_target_pairs={{0,16},{16,0},{1,17},{17,1},{2,18},{18,2},{3,19},{19,3},{4,20},{20... | collective-permute-start | bytes 6291464 | tf_op jit(solution)/shard_map/ppermute | solution.py:704
  8.9 12.7 %collective-permute-start = (f32[4,512]{1,0:T(4,128)S(1)}, f32[4,512]{1,0:T(4,128)S(1)}, u32[]{:S(2)}, u32[]{:S(2)}) collective-permute-start(f32[4,512]{1,0:T(4,128)S(1)} %pad_maximum_fusion.11), channel_id=1, source_target_pairs={{0,16},{16,0},{1,17},{17,1},{2,18},{18,2},{3,19},{19,3},{4,20},{20... | collective-permute-start | bytes 24584 | tf_op jit(solution)/shard_map/ppermute | solution.py:704
  9.1 13.1 %all-to-all-start = ((f32[16,2,512]{2,1,0:T(2,128)}), f32[16,2,512]{2,1,0:T(2,128)S(1)}, u32[]{:S(2)}, u32[]{:S(2)}) async-start(f32[16,2,512]{2,1,0:T(2,128)} %get-tuple-element.147), calls=%async_computation | async-start | bytes 131072 | tf_op jit(solution)/shard_map/all_to_all | solution.py:700
  22.2 13.4 %copy-start.21 = (f32[1,2048]{1,0:T(1,128)S(1)}, f32[1,2048]{1,0:T(1,128)}, u32[]{:S(2)}) copy-start(f32[1,2048]{1,0:T(1,128)} %param.27) | copy-start | bytes 24580
  22.2 13.4 %copy-start.22 = (f32[1,2048]{1,0:T(1,128)S(1)}, f32[1,2048]{1,0:T(1,128)}, u32[]{:S(2)}) copy-start(f32[1,2048]{1,0:T(1,128)} %param.26) | copy-start | bytes 24580
  28.2 32.1 %collective-permute-start.4 = (bf16[256,4608]{1,0:T(8,128)(2,1)}, bf16[256,4608]{1,0:T(8,128)(2,1)}, u32[]{:S(2)}, u32[]{:S(2)}) collective-permute-start(bf16[256,4608]{1,0:T(8,128)(2,1)} %get-tuple-element.155.refs_1_), channel_id=1, source_target_pairs={{0,16},{16,0},{1,17},{17,1},{2,18},{18,2},{3,19},{19,3},{4,20},{20... | collective-permute-start | bytes 7077896 | tf_op jit(solution)/shard_map/ppermute | solution.py:704
  29.2 13.7 %all-to-all-start.1 = ((bf16[16,2,3840]{2,1,0:T(2,128)(2,1)}), bf16[16,2,3840]{2,1,0:T(2,128)(2,1)S(1)}, u32[]{:S(2)}, u32[]{:S(2)}) async-start(bf16[16,2,3840]{2,1,0:T(2,128)(2,1)} %get-tuple-element.151), calls=%async_computation.1 | async-start | bytes 491520 | tf_op jit(solution)/shard_map/all_to_all | solution.py:700
  35.6 20.1 %collective-permute-start.5 = (f32[2,2048]{1,0:T(2,128)S(1)}, f32[2,2048]{1,0:T(2,128)S(1)}, u32[]{:S(2)}, u32[]{:S(2)}) collective-permute-start(f32[2,2048]{1,0:T(2,128)S(1)} %pad_maximum_fusion.9), channel_id=1, source_target_pairs={{0,16},{16,0},{1,17},{17,1},{2,18},{18,2},{3,19},{19,3},{4,20},{20... | collective-permute-start | bytes 49160 | tf_op jit(solution)/shard_map/ppermute | solution.py:704
  43.0 10.5 %copy-start.29 = (f32[2048]{0:T(1024)S(1)}, f32[2048]{0:T(1024)}, u32[]{:S(2)}) copy-start(f32[2048]{0:T(1024)} %param.20) | copy-start | bytes 24580
  43.0 10.5 %copy-start.30 = (f32[2048]{0:T(1024)S(1)}, f32[2048]{0:T(1024)}, u32[]{:S(2)}) copy-start(f32[2048]{0:T(1024)} %param.19) | copy-start | bytes 24580
  48.1 12.2 %all-to-all-start.2 = ((f32[16,2,2048]{2,1,0:T(2,128)}), f32[16,2,2048]{2,1,0:T(2,128)S(1)}, u32[]{:S(2)}, u32[]{:S(2)}) async-start(f32[16,2,2048]{2,1,0:T(2,128)} %get-tuple-element.154), calls=%async_computation.2 | async-start | bytes 524288 | tf_op jit(solution)/shard_map/all_to_all | solution.py:700
  54.1 17.7 %collective-permute-start.6 = (bf16[256,512]{1,0:T(8,128)(2,1)}, bf16[256,512]{1,0:T(8,128)(2,1)S(1)}, u32[]{:S(2)}, u32[]{:S(2)}) collective-permute-start(bf16[256,512]{1,0:T(8,128)(2,1)} %get-tuple-element.161.refs_5_), channel_id=1, source_target_pairs={{0,16},{16,0},{1,17},{17,1},{2,18},{18,2},{3,19},{19,3},{4,20},{20... | collective-permute-start | bytes 786440 | tf_op jit(solution)/shard_map/ppermute | solution.py:704
  65.9 11.4 %all-to-all-start.3 = ((f32[16,2,512]{2,1,0:T(2,128)}), f32[16,2,512]{2,1,0:T(2,128)S(1)}, u32[]{:S(2)}, u32[]{:S(2)}) async-start(f32[16,2,512]{2,1,0:T(2,128)} %get-tuple-element.160), calls=%async_computation.3 | async-start | bytes 131072 | tf_op jit(solution)/shard_map/all_to_all | solution.py:700
  71.8 11.4 %copy-start.13 = (bf16[256,512]{1,0:T(8,128)(2,1)}, bf16[256,512]{1,0:T(8,128)(2,1)S(1)}, u32[]{:S(2)}) copy-start(bf16[256,512]{1,0:T(8,128)(2,1)S(1)} %collective-permute-done.6.refs_6_) | copy-start | bytes 786436
  83.2 28.9 %collective-permute-start.8 = (bf16[256,4608]{1,0:T(8,128)(2,1)}, bf16[256,4608]{1,0:T(8,128)(2,1)S(1)}, u32[]{:S(2)}, u32[]{:S(2)}) collective-permute-start(bf16[256,4608]{1,0:T(8,128)(2,1)} %get-tuple-element.169.refs_5_), channel_id=1, source_target_pairs={{0,16},{16,0},{1,17},{17,1},{2,18},{18,2},{3,19},{19,3},{4,20},{20... | collective-permute-start | bytes 7077896 | tf_op jit(solution)/shard_map/ppermute | solution.py:704
  86.0 10.0 %collective-permute-start.7 = (bf16[256,2048]{1,0:T(8,128)(2,1)S(1)}, bf16[256,2048]{1,0:T(8,128)(2,1)S(1)}, u32[]{:S(2)}, u32[]{:S(2)}) collective-permute-start(bf16[256,2048]{1,0:T(8,128)(2,1)S(1)} %copy-done.1), channel_id=1, source_target_pairs={{0,16},{16,0},{1,17},{17,1},{2,18},{18,2},{3,19},{19,3},{4,20},{20... | collective-permute-start | bytes 3145736 | tf_op jit(solution)/shard_map/ppermute | solution.py:704
  112.1 12.3 %copy-start.15 = (bf16[256,512]{1,0:T(8,128)(2,1)S(1)}, bf16[256,512]{1,0:T(8,128)(2,1)}, u32[]{:S(2)}) copy-start(bf16[256,512]{1,0:T(8,128)(2,1)} %get-tuple-element.174.refs_1_) | copy-start | bytes 786436
  118.6 12.5 %all-to-all-start.6 = ((f32[16,2,2048]{2,1,0:T(2,128)}), f32[16,2,2048]{2,1,0:T(2,128)S(1)}, u32[]{:S(2)}, u32[]{:S(2)}) async-start(f32[16,2,2048]{2,1,0:T(2,128)} %get-tuple-element.173), calls=%async_computation.6 | async-start | bytes 524288 | tf_op jit(solution)/shard_map/all_to_all | solution.py:700
  124.4 3.2 collective-permute-start.9
  136.5 13.2 %collective-permute-start.10 = (bf16[256,2048]{1,0:T(8,128)(2,1)}, bf16[256,2048]{1,0:T(8,128)(2,1)S(1)}, u32[]{:S(2)}, u32[]{:S(2)}) collective-permute-start(bf16[256,2048]{1,0:T(8,128)(2,1)} %get-tuple-element.180.refs_3_), channel_id=1, source_target_pairs={{0,16},{16,0},{1,17},{17,1},{2,18},{18,2},{3,19},{19,3},{4,20},{20... | collective-permute-start | bytes 3145736 | tf_op jit(solution)/shard_map/ppermute | solution.py:704
  156.2 5.7 %collective-permute-start.11 = (bf16[256,512]{1,0:T(8,128)(2,1)}, bf16[256,512]{1,0:T(8,128)(2,1)S(1)}, u32[]{:S(2)}, u32[]{:S(2)}) collective-permute-start(bf16[256,512]{1,0:T(8,128)(2,1)} %get-tuple-element.188.refs_7_), channel_id=1, source_target_pairs={{0,16},{16,0},{1,17},{17,1},{2,18},{18,2},{3,19},{19,3},{4,20},{20... | collective-permute-start | bytes 786440 | tf_op jit(solution)/shard_map/ppermute | solution.py:704
  157.5 11.7 %all-to-all-start.8 = ((f32[16,2,512]{2,1,0:T(2,128)}), f32[16,2,512]{2,1,0:T(2,128)S(1)}, u32[]{:S(2)}, u32[]{:S(2)}) async-start(f32[16,2,512]{2,1,0:T(2,128)} %get-tuple-element.184), calls=%async_computation.8 | async-start | bytes 131072 | tf_op jit(solution)/shard_map/all_to_all | solution.py:700
  169.2 23.3 %collective-permute-start.13 = (bf16[2,4,208,256]{3,2,1,0:T(8,128)(2,1)}, bf16[2,4,208,256]{3,2,1,0:T(8,128)(2,1)S(1)}, u32[]{:S(2)}, u32[]{:S(2)}) collective-permute-start(bf16[2,4,208,256]{3,2,1,0:T(8,128)(2,1)} %get-tuple-element.198), channel_id=1, source_target_pairs={{0,1},{1,0},{2,3},{3,2},{4,5},{5,4},{6,7},{7,6},{8,9},{9,8},{10,11... | collective-permute-start | bytes 2555912 | tf_op jit(solution)/shard_map/ppermute | solution.py:708
  170.4 22.1 %collective-permute-start.14 = (bf16[2,4,208,256]{3,2,1,0:T(8,128)(2,1)}, bf16[2,4,208,256]{3,2,1,0:T(8,128)(2,1)}, u32[]{:S(2)}, u32[]{:S(2)}) collective-permute-start(bf16[2,4,208,256]{3,2,1,0:T(8,128)(2,1)} %get-tuple-element.200), channel_id=1, source_target_pairs={{0,2},{1,3},{2,0},{3,1},{4,6},{5,7},{6,4},{7,5},{8,10},{9,11},{10,... | collective-permute-start | bytes 2555912 | tf_op jit(solution)/shard_map/ppermute | solution.py:708
  171.6 20.9 %copy-start.8 = (bf16[2,4,208,256]{3,2,1,0:T(8,128)(2,1)S(1)}, bf16[2,4,208,256]{3,2,1,0:T(8,128)(2,1)}, u32[]{:S(2)}) copy-start(bf16[2,4,208,256]{3,2,1,0:T(8,128)(2,1)} %get-tuple-element.197) | copy-start | bytes 2555908
  171.6 21.0 %copy-start.9 = (bf16[2,4,208,256]{3,2,1,0:T(8,128)(2,1)S(1)}, bf16[2,4,208,256]{3,2,1,0:T(8,128)(2,1)}, u32[]{:S(2)}) copy-start(bf16[2,4,208,256]{3,2,1,0:T(8,128)(2,1)} %get-tuple-element.199) | copy-start | bytes 2555908
  179.6 12.9 %all-to-all-start.9 = ((bf16[16,2,3072]{2,1,0:T(2,128)(2,1)}), bf16[16,2,3072]{2,1,0:T(2,128)(2,1)S(1)}, u32[]{:S(2)}, u32[]{:S(2)}) async-start(bf16[16,2,3072]{2,1,0:T(2,128)(2,1)} %get-tuple-element.194), calls=%async_computation.9 | async-start | bytes 393216 | tf_op jit(solution)/shard_map/all_to_all | solution.py:700
  184.2 2.8 collective-permute-start.12
  187.0 14.3 %copy-start.16 = (bf16[256,512]{1,0:T(8,128)(2,1)}, bf16[256,512]{1,0:T(8,128)(2,1)S(1)}, u32[]{:S(2)}) copy-start(bf16[256,512]{1,0:T(8,128)(2,1)S(1)} %collective-permute-done.12.refs_4_) | copy-start | bytes 786436
  192.5 10.6 %copy-start.10 = (bf16[2,4,208,256]{3,2,1,0:T(8,128)(2,1)}, bf16[2,4,208,256]{3,2,1,0:T(8,128)(2,1)S(1)}, u32[]{:S(2)}) copy-start(bf16[2,4,208,256]{3,2,1,0:T(8,128)(2,1)S(1)} %collective-permute-done.13) | copy-start | bytes 2555908
  201.4 8.8 %collective-permute-start.15 = (bf16[256,2048]{1,0:T(8,128)(2,1)}, bf16[256,2048]{1,0:T(8,128)(2,1)S(1)}, u32[]{:S(2)}, u32[]{:S(2)}) collective-permute-start(bf16[256,2048]{1,0:T(8,128)(2,1)} %get-tuple-element.208.refs_7_), channel_id=1, source_target_pairs={{0,16},{16,0},{1,17},{17,1},{2,18},{18,2},{3,19},{19,3},{4,20},{20... | collective-permute-start | bytes 3145736 | tf_op jit(solution)/shard_map/ppermute | solution.py:704
  203.0 7.1 %collective-permute-start.16 = (bf16[256,2048]{1,0:T(8,128)(2,1)}, bf16[256,2048]{1,0:T(8,128)(2,1)S(1)}, u32[]{:S(2)}, u32[]{:S(2)}) collective-permute-start(bf16[256,2048]{1,0:T(8,128)(2,1)} %get-tuple-element.210.refs_11_.refs_2_), channel_id=1, source_target_pairs={{0,16},{16,0},{1,17},{17,1},{2,18},{18,2},{3,19},{19,3},{4,20},{20... | collective-permute-start | bytes 3145736 | tf_op jit(solution)/shard_map/ppermute | solution.py:704
  203.1 14.9 %collective-permute-start.17 = (bf16[4,208,256]{2,1,0:T(8,128)(2,1)S(1)}, bf16[4,208,256]{2,1,0:T(8,128)(2,1)}, u32[]{:S(2)}, u32[]{:S(2)}) collective-permute-start(bf16[4,208,256]{2,1,0:T(8,128)(2,1)S(1)} %fusion.13), channel_id=1, source_target_pairs={{0,2},{1,3},{2,0},{3,1},{4,6},{5,7},{6,4},{7,5},{8,10},{9,11},{10,... | collective-permute-start | bytes 1277960 | tf_op jit(solution)/shard_map/ppermute | solution.py:708
  204.3 13.7 %collective-permute-start.18 = (bf16[4,208,256]{2,1,0:T(8,128)(2,1)}, bf16[4,208,256]{2,1,0:T(8,128)(2,1)}, u32[]{:S(2)}, u32[]{:S(2)}) collective-permute-start(bf16[4,208,256]{2,1,0:T(8,128)(2,1)} %fusion.12), channel_id=1, source_target_pairs={{0,1},{1,0},{2,3},{3,2},{4,5},{5,4},{6,7},{7,6},{8,9},{9,8},{10,11... | collective-permute-start | bytes 1277960 | tf_op jit(solution)/shard_map/ppermute | solution.py:708
  204.6 13.4 %all-to-all-start.10 = ((f32[16,2,512]{2,1,0:T(2,128)}), f32[16,2,512]{2,1,0:T(2,128)S(1)}, u32[]{:S(2)}, u32[]{:S(2)}) async-start(f32[16,2,512]{2,1,0:T(2,128)} %get-tuple-element.204), calls=%async_computation.10 | async-start | bytes 131072 | tf_op jit(solution)/shard_map/all_to_all | solution.py:700
  218.0 25.1 %collective-permute-start.20 = (bf16[2,4,256,256]{3,2,1,0:T(8,128)(2,1)}, bf16[2,4,256,256]{3,2,1,0:T(8,128)(2,1)}, u32[]{:S(2)}, u32[]{:S(2)}) collective-permute-start(bf16[2,4,256,256]{3,2,1,0:T(8,128)(2,1)} %get-tuple-element.222), channel_id=1, source_target_pairs={{0,1},{1,0},{2,3},{3,2},{4,5},{5,4},{6,7},{7,6},{8,9},{9,8},{10,11... | collective-permute-start | bytes 3145736 | tf_op jit(solution)/shard_map/ppermute | solution.py:708
  219.3 25.1 %collective-permute-start.21 = (bf16[2,4,256,256]{3,2,1,0:T(8,128)(2,1)}, bf16[2,4,256,256]{3,2,1,0:T(8,128)(2,1)}, u32[]{:S(2)}, u32[]{:S(2)}) collective-permute-start(bf16[2,4,256,256]{3,2,1,0:T(8,128)(2,1)} %get-tuple-element.224), channel_id=1, source_target_pairs={{0,2},{1,3},{2,0},{3,1},{4,6},{5,7},{6,4},{7,5},{8,10},{9,11},{10,... | collective-permute-start | bytes 3145736 | tf_op jit(solution)/shard_map/ppermute | solution.py:708
  228.7 14.4 %all-to-all-start.11 = ((f32[16,2,512]{2,1,0:T(2,128)}), f32[16,2,512]{2,1,0:T(2,128)S(1)}, u32[]{:S(2)}, u32[]{:S(2)}) async-start(f32[16,2,512]{2,1,0:T(2,128)} %get-tuple-element.218), calls=%async_computation.11 | async-start | bytes 131072 | tf_op jit(solution)/shard_map/all_to_all | solution.py:700
  233.3 9.9 %collective-permute-start.19 = (bf16[256,512]{1,0:T(8,128)(2,1)}, bf16[256,512]{1,0:T(8,128)(2,1)S(1)}, u32[]{:S(2)}, u32[]{:S(2)}) collective-permute-start(bf16[256,512]{1,0:T(8,128)(2,1)} %get-tuple-element.219.refs_3_), channel_id=1, source_target_pairs={{0,16},{16,0},{1,17},{17,1},{2,18},{18,2},{3,19},{19,3},{4,20},{20... | collective-permute-start | bytes 786440 | tf_op jit(solution)/shard_map/ppermute | solution.py:704
  249.7 8.7 %collective-permute-start.22 = (bf16[1024,512]{1,0:T(8,128)(2,1)}, bf16[1024,512]{1,0:T(8,128)(2,1)S(1)}, u32[]{:S(2)}, u32[]{:S(2)}) collective-permute-start(bf16[1024,512]{1,0:T(8,128)(2,1)} %get-tuple-element.249.refs_7_.refs_0_), channel_id=1, source_target_pairs={{0,16},{16,0},{1,17},{17,1},{2,18},{18,2},{3,19},{19,3},{4,20},{20... | collective-permute-start | bytes 3145736 | tf_op jit(solution)/shard_map/ppermute | solution.py:704
  252.5 16.8 %collective-permute-start.23 = (bf16[4,256,256]{2,1,0:T(8,128)(2,1)S(1)}, bf16[4,256,256]{2,1,0:T(8,128)(2,1)S(1)}, u32[]{:S(2)}, u32[]{:S(2)}) collective-permute-start(bf16[4,256,256]{2,1,0:T(8,128)(2,1)S(1)} %fusion.5), channel_id=1, source_target_pairs={{0,2},{1,3},{2,0},{3,1},{4,6},{5,7},{6,4},{7,5},{8,10},{9,11},{10,... | collective-permute-start | bytes 1572872 | tf_op jit(solution)/shard_map/ppermute | solution.py:708
  253.8 15.6 %collective-permute-start.24 = (bf16[4,256,256]{2,1,0:T(8,128)(2,1)S(1)}, bf16[4,256,256]{2,1,0:T(8,128)(2,1)S(1)}, u32[]{:S(2)}, u32[]{:S(2)}) collective-permute-start(bf16[4,256,256]{2,1,0:T(8,128)(2,1)S(1)} %fusion.4), channel_id=1, source_target_pairs={{0,1},{1,0},{2,3},{3,2},{4,5},{5,4},{6,7},{7,6},{8,9},{9,8},{10,11... | collective-permute-start | bytes 1572872 | tf_op jit(solution)/shard_map/ppermute | solution.py:708
  254.7 17.0 %collective-permute-start.25 = (bf16[208,512]{1,0:T(8,128)(2,1)}, bf16[208,512]{1,0:T(8,128)(2,1)}, u32[]{:S(2)}, u32[]{:S(2)}) collective-permute-start(bf16[208,512]{1,0:T(8,128)(2,1)} %get-tuple-element.239), channel_id=1, source_target_pairs={{0,4},{1,5},{2,6},{3,7},{4,0},{5,1},{6,2},{7,3},{8,12},{9,13},{10,... | collective-permute-start | bytes 638984 | tf_op jit(solution)/shard_map/ppermute | solution.py:708
  255.0 16.7 %collective-permute-start.26 = (bf16[208,512]{1,0:T(8,128)(2,1)}, bf16[208,512]{1,0:T(8,128)(2,1)}, u32[]{:S(2)}, u32[]{:S(2)}) collective-permute-start(bf16[208,512]{1,0:T(8,128)(2,1)} %get-tuple-element.240), channel_id=1, source_target_pairs={{0,8},{1,9},{2,10},{3,11},{4,12},{5,13},{6,14},{7,15},{8,0},{9,1},... | collective-permute-start | bytes 638984 | tf_op jit(solution)/shard_map/ppermute | solution.py:708
  258.4 17.5 %collective-permute-start.27 = (bf16[208,512]{1,0:T(8,128)(2,1)}, bf16[208,512]{1,0:T(8,128)(2,1)}, u32[]{:S(2)}, u32[]{:S(2)}) collective-permute-start(bf16[208,512]{1,0:T(8,128)(2,1)} %get-tuple-element.241), channel_id=1, source_target_pairs={{0,12},{1,13},{2,14},{3,15},{4,8},{5,9},{6,10},{7,11},{8,4},{9,5},... | collective-permute-start | bytes 638984 | tf_op jit(solution)/shard_map/ppermute | solution.py:708
  275.9 10.7 %collective-permute-start.29 = (f32[2,2,512]{2,1,0:T(2,128)}, f32[2,2,512]{2,1,0:T(2,128)S(1)}, u32[]{:S(2)}, u32[]{:S(2)}) collective-permute-start(f32[2,2,512]{2,1,0:T(2,128)} %broadcast_select_fusion.7), channel_id=1, source_target_pairs={{0,16},{16,0},{1,17},{17,1},{2,18},{18,2},{3,19},{19,3},{4,20},{20... | collective-permute-start | bytes 24584 | tf_op jit(solution)/shard_map/ppermute | solution.py:704
  277.6 11.3 %collective-permute-start.28 = (f32[4,2048]{1,0:T(4,128)}, f32[4,2048]{1,0:T(4,128)S(1)}, u32[]{:S(2)}, u32[]{:S(2)}) collective-permute-start(f32[4,2048]{1,0:T(4,128)} %pad_maximum_fusion.8), channel_id=1, source_target_pairs={{0,16},{16,0},{1,17},{17,1},{2,18},{18,2},{3,19},{19,3},{4,20},{20... | collective-permute-start | bytes 98312 | tf_op jit(solution)/shard_map/ppermute | solution.py:704
  278.9 10.3 %copy-start.23 = (f32[2,512]{1,0:T(2,128)S(1)}, f32[2,512]{1,0:T(2,128)}, u32[]{:S(2)}) copy-start(f32[2,512]{1,0:T(2,128)} %get-tuple-element.246) | copy-start | bytes 12292
  278.9 18.4 %copy-start.11 = (bf16[2,4,176,256]{3,2,1,0:T(8,128)(2,1)S(1)}, bf16[2,4,176,256]{3,2,1,0:T(8,128)(2,1)}, u32[]{:S(2)}) copy-start(bf16[2,4,176,256]{3,2,1,0:T(8,128)(2,1)} %get-tuple-element.256) | copy-start | bytes 2162692
  279.0 18.4 %copy-start.12 = (bf16[2,4,176,256]{3,2,1,0:T(8,128)(2,1)S(1)}, bf16[2,4,176,256]{3,2,1,0:T(8,128)(2,1)}, u32[]{:S(2)}) copy-start(bf16[2,4,176,256]{3,2,1,0:T(8,128)(2,1)} %get-tuple-element.258) | copy-start | bytes 2162692
  279.0 17.5 %collective-permute-start.30 = (bf16[2,4,176,256]{3,2,1,0:T(8,128)(2,1)}, bf16[2,4,176,256]{3,2,1,0:T(8,128)(2,1)S(1)}, u32[]{:S(2)}, u32[]{:S(2)}) collective-permute-start(bf16[2,4,176,256]{3,2,1,0:T(8,128)(2,1)} %get-tuple-element.253), channel_id=1, source_target_pairs={{0,1},{1,0},{2,3},{3,2},{4,5},{5,4},{6,7},{7,6},{8,9},{9,8},{10,11... | collective-permute-start | bytes 2162696 | tf_op jit(solution)/shard_map/ppermute | solution.py:708
  280.2 17.1 %collective-permute-start.31 = (bf16[2,4,176,256]{3,2,1,0:T(8,128)(2,1)}, bf16[2,4,176,256]{3,2,1,0:T(8,128)(2,1)S(1)}, u32[]{:S(2)}, u32[]{:S(2)}) collective-permute-start(bf16[2,4,176,256]{3,2,1,0:T(8,128)(2,1)} %get-tuple-element.254), channel_id=1, source_target_pairs={{0,2},{1,3},{2,0},{3,1},{4,6},{5,7},{6,4},{7,5},{8,10},{9,11},{10,... | collective-permute-start | bytes 2162696 | tf_op jit(solution)/shard_map/ppermute | solution.py:708
  286.5 12.1 %collective-permute-start.37 = (bf16[256,512]{1,0:T(8,128)(2,1)S(1)}, bf16[256,512]{1,0:T(8,128)(2,1)S(1)}, u32[]{:S(2)}, u32[]{:S(2)}) collective-permute-start(bf16[256,512]{1,0:T(8,128)(2,1)S(1)} %get-tuple-element.274), channel_id=1, source_target_pairs={{0,4},{1,5},{2,6},{3,7},{4,0},{5,1},{6,2},{7,3},{8,12},{9,13},{10,... | collective-permute-start | bytes 786440 | tf_op jit(solution)/shard_map/ppermute | solution.py:708
  286.6 13.3 %collective-permute-start.38 = (bf16[256,512]{1,0:T(8,128)(2,1)S(1)}, bf16[256,512]{1,0:T(8,128)(2,1)S(1)}, u32[]{:S(2)}, u32[]{:S(2)}) collective-permute-start(bf16[256,512]{1,0:T(8,128)(2,1)S(1)} %get-tuple-element.275), channel_id=1, source_target_pairs={{0,8},{1,9},{2,10},{3,11},{4,12},{5,13},{6,14},{7,15},{8,0},{9,1},... | collective-permute-start | bytes 786440 | tf_op jit(solution)/shard_map/ppermute | solution.py:708
  288.9 22.2 %collective-permute-start.39 = (bf16[256,512]{1,0:T(8,128)(2,1)S(1)}, bf16[256,512]{1,0:T(8,128)(2,1)S(1)}, u32[]{:S(2)}, u32[]{:S(2)}) collective-permute-start(bf16[256,512]{1,0:T(8,128)(2,1)S(1)} %get-tuple-element.276), channel_id=1, source_target_pairs={{0,12},{1,13},{2,14},{3,15},{4,8},{5,9},{6,10},{7,11},{8,4},{9,5},... | collective-permute-start | bytes 786440 | tf_op jit(solution)/shard_map/ppermute | solution.py:708
  297.4 16.8 %collective-permute-start.32 = (bf16[4,176,256]{2,1,0:T(8,128)(2,1)S(1)}, bf16[4,176,256]{2,1,0:T(8,128)(2,1)S(1)}, u32[]{:S(2)}, u32[]{:S(2)}) collective-permute-start(bf16[4,176,256]{2,1,0:T(8,128)(2,1)S(1)} %add_bitcast_fusion.1), channel_id=1, source_target_pairs={{0,2},{1,3},{2,0},{3,1},{4,6},{5,7},{6,4},{7,5},{8,10},{9,11},{10,... | collective-permute-start | bytes 1081352 | tf_op jit(solution)/shard_map/ppermute | solution.py:708
  297.8 16.5 %collective-permute-start.33 = (bf16[4,176,256]{2,1,0:T(8,128)(2,1)S(1)}, bf16[4,176,256]{2,1,0:T(8,128)(2,1)S(1)}, u32[]{:S(2)}, u32[]{:S(2)}) collective-permute-start(bf16[4,176,256]{2,1,0:T(8,128)(2,1)S(1)} %add_bitcast_fusion), channel_id=1, source_target_pairs={{0,1},{1,0},{2,3},{3,2},{4,5},{5,4},{6,7},{7,6},{8,9},{9,8},{10,11... | collective-permute-start | bytes 1081352 | tf_op jit(solution)/shard_map/ppermute | solution.py:708
  312.0 22.6 %collective-permute-start.41 = (f32[32,1024]{1,0:T(8,128)S(1)}, f32[32,1024]{1,0:T(8,128)S(1)}, u32[]{:S(2)}, u32[]{:S(2)}) collective-permute-start(f32[32,1024]{1,0:T(8,128)S(1)} %fusion.41), channel_id=1, source_target_pairs={{0,16},{16,0},{1,17},{17,1},{2,18},{18,2},{3,19},{19,3},{4,20},{20... | collective-permute-start | bytes 393224 | tf_op jit(solution)/shard_map/ppermute | solution.py:704
  314.4 7.5 %collective-permute-start.34 = (bf16[176,512]{1,0:T(8,128)(2,1)S(1)}, bf16[176,512]{1,0:T(8,128)(2,1)S(1)}, u32[]{:S(2)}, u32[]{:S(2)}) collective-permute-start(bf16[176,512]{1,0:T(8,128)(2,1)S(1)} %get-tuple-element.267), channel_id=1, source_target_pairs={{0,4},{1,5},{2,6},{3,7},{4,0},{5,1},{6,2},{7,3},{8,12},{9,13},{10,... | collective-permute-start | bytes 540680 | tf_op jit(solution)/shard_map/ppermute | solution.py:708
  314.5 13.6 %collective-permute-start.35 = (bf16[176,512]{1,0:T(8,128)(2,1)S(1)}, bf16[176,512]{1,0:T(8,128)(2,1)S(1)}, u32[]{:S(2)}, u32[]{:S(2)}) collective-permute-start(bf16[176,512]{1,0:T(8,128)(2,1)S(1)} %get-tuple-element.268), channel_id=1, source_target_pairs={{0,8},{1,9},{2,10},{3,11},{4,12},{5,13},{6,14},{7,15},{8,0},{9,1},... | collective-permute-start | bytes 540680 | tf_op jit(solution)/shard_map/ppermute | solution.py:708
  316.9 16.3 %collective-permute-start.36 = (bf16[176,512]{1,0:T(8,128)(2,1)S(1)}, bf16[176,512]{1,0:T(8,128)(2,1)S(1)}, u32[]{:S(2)}, u32[]{:S(2)}) collective-permute-start(bf16[176,512]{1,0:T(8,128)(2,1)S(1)} %get-tuple-element.269), channel_id=1, source_target_pairs={{0,12},{1,13},{2,14},{3,15},{4,8},{5,9},{6,10},{7,11},{8,4},{9,5},... | collective-permute-start | bytes 540680 | tf_op jit(solution)/shard_map/ppermute | solution.py:708
  333.3 2.6 collective-permute-start.40
  (18 other events, 143.8 us)

commit v2 on v1

--- a/solution.py
+++ b/solution.py
@@ -487,7 +487,8 @@
     zero = jnp.zeros((8, width), F32)
     plain, scaled = over_rows(geo.rows, 16, activate, (zero, zero))
     g_out.send()
-    send_rows(sent, ((jnp.sum(plain, axis=0, keepdims=True), jnp.sum(scaled, axis=0, keepdims=True)),))
+    sums = (jnp.sum(plain, axis=0, keepdims=True), jnp.sum(scaled, axis=0, keepdims=True))
+    send_short(sent, jnp.concatenate(sums, axis=0))
     sent.send()
     for line in range(geo.side):
         for column in range(geo.side):
@@ -969,7 +970,7 @@
             spec((1, side, side, slots, out), BF16),
             spec((rows, out), BF16),
             spec((2, out)),
-            spec((devices, 2, out)),
+            spec((devices, 2, out), BF16),
         ),
         "dddd",
         (place, counts, got, u3, joined, wide1, out_grad),

time: 339 us -> 337 us (level)
  blocking collectives: 30.7 us -> 19.8 us
  waiting for transfers between devices: 69.8 us -> 75.9 us
  starting transfers between devices: 96.5 us -> 100 us
    all_to_all x3 -> x2, blocking collectives: 30.7 us -> 19.8 us  [exchange(): return lax.all_to_all(sent, 'dp', 0, 0)]
    all_to_all x9 -> x10, waiting for transfers between devices: 29.6 us -> 36.9 us  [exchange(): return lax.all_to_all(sent, 'dp', 0, 0)]
    all_to_all x9 -> x10, starting transfers between devices: 49.3 us -> 53.7 us  [exchange(): return lax.all_to_all(sent, 'dp', 0, 0)]
  transfers between devices with their start and end apart: 51 -> 52, of which waited for: 16 -> 16; matrix products, arithmetic and copies ran while one was open for 5% -> 5% of each run, Pallas kernels for 24% -> 26%
where the time goes in v2:
time: 337 us; the launch traced here: 335 us
  Pallas kernels  116 us (34%)
  starting transfers between devices  100 us (30%)
  waiting for transfers between devices  75.9 us (23%)
  blocking collectives  19.8 us (6%)
  other arithmetic  18.5 us (5%)
  local copies, waits for them, and re-layouts  4.02 us (1%)
    pallas_call x18, Pallas kernels, stage(): pl.pallas_call(run, out_shape=list(outs), in_specs=[kinds[kind] for kind...  116 us
    all_to_all x10, starting transfers between devices, exchange(): return lax.all_to_all(sent, 'dp', 0, 0)  53.7 us
    ppermute x21, waiting for transfers between devices, across(): lax.ppermute(value, 'dp', [(i, i ^ mask) for i in range(lax.axis_size('dp...  37.6 us
    all_to_all x10, waiting for transfers between devices, exchange(): return lax.all_to_all(sent, 'dp', 0, 0)  36.9 us
    ppermute x21, starting transfers between devices, swapped(): return lax.ppermute(value, 'section', [(0, 1), (1, 0)])  27.6 us
    all_to_all x2, blocking collectives, exchange(): return lax.all_to_all(sent, 'dp', 0, 0)  19.8 us
    ppermute x21, starting transfers between devices, across(): lax.ppermute(value, 'dp', [(i, i ^ mask) for i in range(lax.axis_size('dp...  18.7 us
  transfers between devices with their start and end apart: 52, of which 16 were waited for; matrix products, arithmetic and copies ran while one was open for 5% of the time, Pallas kernels for 26%

profile of v2, /device:TPU:9, one launch (start us, length us, event | category | flops | bytes accessed | tf_op | source)
XLA Modules:
  0.0 335.3 jit_solution(1110039974283324633)
XLA Ops:
  2.1 6.2 %shard_map.229 = (bf16[1024,1024]{1,0:T(8,128)(2,1)}, bf16[1024,512]{1,0:T(8,128)(2,1)}, f32[16,2,512]{2,1,0:T(2,128)}) custom-call(s32[2]{0:T(128)} %pad_add_fusion.refs_0_, s32[2,16]{1,0:T(2,128)} %bitcast.91, bf16[2,14,14,4,1024]{4,3,2,1,0:T(4,128)(2,1)} %bitcast.88, bf16[1024,512]{1,0:T(8,128)(2,1)} %refs_1_.1), custom_call_target="tpu_custom_call" | custom-call | tf_op jit(solution)/shard_map/pallas_call | solution.py:87
  9.1 6.7 %all-to-all-start = ((f32[16,2,512]{2,1,0:T(2,128)}), f32[16,2,512]{2,1,0:T(2,128)S(1)}, u32[]{:S(2)}, u32[]{:S(2)}) async-start(f32[16,2,512]{2,1,0:T(2,128)} %get-tuple-element.147), calls=%async_computation | async-start | bytes 131072 | tf_op jit(solution)/shard_map/all_to_all | solution.py:701
  15.7 5.8 %shard_map.230 = (bf16[256,2048]{1,0:T(8,128)(2,1)}, f32[2,2048]{1,0:T(2,128)}) custom-call(s32[2]{0:T(128)} %pad_add_fusion.refs_0_, s32[2,16]{1,0:T(2,128)} %bitcast.92, bf16[1024,1024]{1,0:T(8,128)(2,1)} %get-tuple-element.149.refs_2_.refs_9_.refs_5_, bf16[1024,2048]{1,0:T(8,128)(2,1)} %refs_3_.5), custom_call_target="tpu_custom_call" | custom-call | tf_op jit(solution)/shard_map/pallas_call | solution.py:87
  22.2 6.0 %shard_map.231 = (bf16[256,4608]{1,0:T(8,128)(2,1)}, f32[256,512]{1,0:T(8,128)}, f32[2,512]{1,0:T(2,128)}, bf16[16,2,3840]{2,1,0:T(2,128)(2,1)}) custom-call(s32[2]{0:T(128)} %pad_add_fusion.refs_0_, s32[2,16]{1,0:T(2,128)} %bitcast.93, f32[16,2,512]{2,1,0:T(2,128)S(1)} %all-to-all-done.refs_2_, ...), custom_call_target="tpu_custom_call" | custom-call | tf_op jit(solution)/shard_map/pallas_call | solution.py:87
  29.2 6.4 %all-to-all-start.1 = ((bf16[16,2,3840]{2,1,0:T(2,128)(2,1)}), bf16[16,2,3840]{2,1,0:T(2,128)(2,1)S(1)}, u32[]{:S(2)}, u32[]{:S(2)}) async-start(bf16[16,2,3840]{2,1,0:T(2,128)(2,1)} %get-tuple-element.151), calls=%async_computation.1 | async-start | bytes 491520 | tf_op jit(solution)/shard_map/all_to_all | solution.py:701
  36.3 6.7 %all-to-all-done.1.refs_2_ = bf16[16,2,3840]{2,1,0:T(2,128)(2,1)S(1)} async-done(((bf16[16,2,3840]{2,1,0:T(2,128)(2,1)}), bf16[16,2,3840]{2,1,0:T(2,128)(2,1)S(1)}, u32[]{:S(2)}, u32[]{:S(2)}) %all-to-all-start.1) | async-done | bytes 245792 | tf_op jit(solution)/shard_map/all_to_all | solution.py:701
  43.0 5.2 %shard_map.232 = (bf16[256,512]{1,0:T(8,128)(2,1)}, bf16[256,2048]{1,0:T(8,128)(2,1)}, f32[2,512]{1,0:T(2,128)}, f32[2,2048]{1,0:T(2,128)}, f32[16,2,2048]{2,1,0:T(2,128)}) custom-call(s32[2]{0:T(128)} %pad_add_fusion.refs_0_, s32[2,16]{1,0:T(2,128)} %bitcast.94, bf16[16,2,3840]{2,1,0:T(2,128)(2,1)S(1)} %all-to-all-done.1.refs_2_, ...), custom_call_target="tpu_custom_call" | custom-call | tf_op jit(solution)/shard_map/pallas_call | solution.py:87
  48.1 5.4 %all-to-all-start.2 = ((f32[16,2,2048]{2,1,0:T(2,128)}), f32[16,2,2048]{2,1,0:T(2,128)S(1)}, u32[]{:S(2)}, u32[]{:S(2)}) async-start(f32[16,2,2048]{2,1,0:T(2,128)} %get-tuple-element.154), calls=%async_computation.2 | async-start | bytes 524288 | tf_op jit(solution)/shard_map/all_to_all | solution.py:701
  54.1 1.6 collective-permute-start.6
  56.3 4.0 %all-to-all-done.2.refs_2_ = f32[16,2,2048]{2,1,0:T(2,128)S(1)} async-done(((f32[16,2,2048]{2,1,0:T(2,128)}), f32[16,2,2048]{2,1,0:T(2,128)S(1)}, u32[]{:S(2)}, u32[]{:S(2)}) %all-to-all-start.2) | async-done | bytes 262176 | tf_op jit(solution)/shard_map/all_to_all | solution.py:701
  60.3 5.5 %shard_map.233 = (bf16[256,2048]{1,0:T(8,128)(2,1)}, f32[256,512]{1,0:T(8,128)}, f32[4,2048]{1,0:T(4,128)}, f32[16,2,512]{2,1,0:T(2,128)}) custom-call(s32[2]{0:T(128)} %pad_add_fusion.refs_0_, s32[2,16]{1,0:T(2,128)} %bitcast.95, f32[16,2,2048]{2,1,0:T(2,128)S(1)} %all-to-all-done.2.refs_2_, bf16[256,2048]{1,0:T(8,128)(2,1)} %get-tuple-element.157.refs_3_.refs_9_.refs_4_, ...), custom_call_target="tpu_custom_call" | custom-call | tf_op jit(solution)/shard_map/pallas_call | solution.py:87
  65.9 5.9 %all-to-all-start.3 = ((f32[16,2,512]{2,1,0:T(2,128)}), f32[16,2,512]{2,1,0:T(2,128)S(1)}, u32[]{:S(2)}, u32[]{:S(2)}) async-start(f32[16,2,512]{2,1,0:T(2,128)} %get-tuple-element.160), calls=%async_computation.3 | async-start | bytes 131072 | tf_op jit(solution)/shard_map/all_to_all | solution.py:701
  71.8 5.4 %all-to-all-done.3.refs_2_ = f32[16,2,512]{2,1,0:T(2,128)S(1)} async-done(((f32[16,2,512]{2,1,0:T(2,128)}), f32[16,2,512]{2,1,0:T(2,128)S(1)}, u32[]{:S(2)}, u32[]{:S(2)}) %all-to-all-start.3) | async-done | bytes 65568 | tf_op jit(solution)/shard_map/all_to_all | solution.py:701
  77.3 5.9 %shard_map.234 = (bf16[256,4608]{1,0:T(8,128)(2,1)}, f32[256,512]{1,0:T(8,128)}, f32[2,512]{1,0:T(2,128)}, f32[16,2,512]{2,1,0:T(2,128)}) custom-call(s32[2]{0:T(128)} %pad_add_fusion.refs_0_, s32[2,16]{1,0:T(2,128)} %bitcast.96, f32[16,2,512]{2,1,0:T(2,128)S(1)} %all-to-all-done.3.refs_2_, f32[256,512]{1,0:T(8,128)} %get-tuple-element.163.refs_3_.refs_7_.refs_4_, ...), custom_call_target="tpu_custom_call" | custom-call | tf_op jit(solution)/shard_map/pallas_call | solution.py:87
  83.2 2.8 collective-permute-start.8
  86.1 9.9 %all_to_all.60.refs_2_ = f32[16,2,512]{2,1,0:T(2,128)S(1)} all-to-all(f32[16,2,512]{2,1,0:T(2,128)} %get-tuple-element.164), channel_id=1, replica_groups=mesh['section'=2,'dp'=16] {'dp'}, dimensions={0} | all-to-all | bytes 131072 | tf_op jit(solution)/shard_map/all_to_all | solution.py:701
  96.0 4.9 %shard_map.235 = (bf16[256,512]{1,0:T(8,128)(2,1)}, bf16[256,2048]{1,0:T(8,128)(2,1)}, f32[2,512]{1,0:T(2,128)}, f32[16,2,2048]{2,1,0:T(2,128)}) custom-call(s32[2]{0:T(128)} %pad_add_fusion.refs_0_, s32[2,16]{1,0:T(2,128)} %bitcast.97, f32[16,2,512]{2,1,0:T(2,128)S(1)} %all_to_all.60.refs_2_, f32[256,512]{1,0:T(8,128)} %get-tuple-element.167.refs_3_.refs_7_.refs_4_, ...), custom_call_target="tpu_custom_call" | custom-call | tf_op jit(solution)/shard_map/pallas_call | solution.py:87
  100.9 4.4 %all-to-all-start.5 = ((f32[16,2,2048]{2,1,0:T(2,128)}), f32[16,2,2048]{2,1,0:T(2,128)S(1)}, u32[]{:S(2)}, u32[]{:S(2)}) async-start(f32[16,2,2048]{2,1,0:T(2,128)} %get-tuple-element.168), calls=%async_computation.5 | async-start | bytes 524288 | tf_op jit(solution)/shard_map/all_to_all | solution.py:701
  105.3 1.9 collective-permute-start.9
  107.2 5.0 %all-to-all-done.5.refs_2_ = f32[16,2,2048]{2,1,0:T(2,128)S(1)} async-done(((f32[16,2,2048]{2,1,0:T(2,128)}), f32[16,2,2048]{2,1,0:T(2,128)S(1)}, u32[]{:S(2)}, u32[]{:S(2)}) %all-to-all-start.5) | async-done | bytes 262176 | tf_op jit(solution)/shard_map/all_to_all | solution.py:701
  112.1 6.2 %shard_map.236 = (bf16[1,7,7,4,2048]{4,3,2,1,0:T(4,128)(2,1)}, bf16[256,2048]{1,0:T(8,128)(2,1)}, f32[2,2048]{1,0:T(2,128)}, bf16[16,2,2048]{2,1,0:T(2,128)(2,1)}) custom-call(s32[2]{0:T(128)} %pad_add_fusion.refs_0_, s32[2,16]{1,0:T(2,128)} %bitcast.98, f32[16,2,2048]{2,1,0:T(2,128)S(1)} %all-to-all-done.5.refs_2_, ...), custom_call_target="tpu_custom_call" | custom-call | tf_op jit(solution)/shard_map/pallas_call | solution.py:87
  118.4 5.8 %all-to-all-start.6 = ((bf16[16,2,2048]{2,1,0:T(2,128)(2,1)}), bf16[16,2,2048]{2,1,0:T(2,128)(2,1)S(1)}, u32[]{:S(2)}, u32[]{:S(2)}) async-start(bf16[16,2,2048]{2,1,0:T(2,128)(2,1)} %get-tuple-element.173), calls=%async_computation.6 | async-start | bytes 262144 | tf_op jit(solution)/shard_map/all_to_all | solution.py:701
  124.2 5.8 %all-to-all-done.6.refs_2_ = bf16[16,2,2048]{2,1,0:T(2,128)(2,1)S(1)} async-done(((bf16[16,2,2048]{2,1,0:T(2,128)(2,1)}), bf16[16,2,2048]{2,1,0:T(2,128)(2,1)S(1)}, u32[]{:S(2)}, u32[]{:S(2)}) %all-to-all-start.6) | async-done | bytes 131104 | tf_op jit(solution)/shard_map/all_to_all | solution.py:701
  130.0 5.4 %shard_map.237 = (bf16[256,2048]{1,0:T(8,128)(2,1)}, f32[256,512]{1,0:T(8,128)}, f32[2,2048]{1,0:T(2,128)}, f32[16,2,512]{2,1,0:T(2,128)}) custom-call(s32[2]{0:T(128)} %pad_add_fusion.refs_0_, s32[2,16]{1,0:T(2,128)} %bitcast.99, bf16[16,2,2048]{2,1,0:T(2,128)(2,1)S(1)} %all-to-all-done.6.refs_2_, bf16[256,2048]{1,0:T(8,128)(2,1)} %get-tuple-element.176.refs_3_.refs_8_, ...), custom_call_target="tpu_custom_call" | custom-call | tf_op jit(solution)/shard_map/pallas_call | solution.py:87
  135.3 2.9 collective-permute-start.10
  138.3 9.9 %all_to_all.61.refs_2_ = f32[16,2,512]{2,1,0:T(2,128)S(1)} all-to-all(f32[16,2,512]{2,1,0:T(2,128)} %get-tuple-element.179), channel_id=1, replica_groups=mesh['section'=2,'dp'=16] {'dp'}, dimensions={0} | all-to-all | bytes 131072 | tf_op jit(solution)/shard_map/all_to_all | solution.py:701
  148.2 6.4 %shard_map.238 = (bf16[256,512]{1,0:T(8,128)(2,1)}, f32[256,512]{1,0:T(8,128)}, f32[2,512]{1,0:T(2,128)}, f32[16,2,512]{2,1,0:T(2,128)}) custom-call(s32[2]{0:T(128)} %pad_add_fusion.refs_0_, s32[2,16]{1,0:T(2,128)} %bitcast.100, f32[16,2,512]{2,1,0:T(2,128)S(1)} %all_to_all.61.refs_2_, f32[256,512]{1,0:T(8,128)} %get-tuple-element.182.refs_3_, ...), custom_call_target="tpu_custom_call" | custom-call | tf_op jit(solution)/shard_map/pallas_call | solution.py:87
  154.6 1.3 collective-permute-start.11
  155.9 4.4 %all-to-all-start.8 = ((f32[16,2,512]{2,1,0:T(2,128)}), f32[16,2,512]{2,1,0:T(2,128)S(1)}, u32[]{:S(2)}, u32[]{:S(2)}) async-start(f32[16,2,512]{2,1,0:T(2,128)} %get-tuple-element.184), calls=%async_computation.8 | async-start | bytes 131072 | tf_op jit(solution)/shard_map/all_to_all | solution.py:701
  160.3 7.2 %shard_map.239 = (bf16[2,4,208,256]{3,2,1,0:T(8,128)(2,1)}, bf16[2,4,208,256]{3,2,1,0:T(8,128)(2,1)}, bf16[2,4,208,256]{3,2,1,0:T(8,128)(2,1)}, bf16[2,4,208,256]{3,2,1,0:T(8,128)(2,1)}) custom-call(s32[2]{0:T(128)} %pad_add_fusion.refs_0_, bf16[256,512]{1,0:T(8,128)(2,1)} %get-tuple-element.174.refs_1_, bf16[256,512]{1,0:T(8,128)(2,1)} %copy-done.14, ...), custom_call_target="tpu_custom_call" | custom-call | tf_op jit(solution)/shard_map/pallas_call | solution.py:87
  167.6 1.3 collective-permute-start.13
  170.0 8.0 %shard_map.240 = (bf16[256,512]{1,0:T(8,128)(2,1)}, bf16[256,2048]{1,0:T(8,128)(2,1)}, f32[2,512]{1,0:T(2,128)}, bf16[16,2,3072]{2,1,0:T(2,128)(2,1)}) custom-call(s32[2]{0:T(128)} %pad_add_fusion.refs_0_, s32[2,16]{1,0:T(2,128)} %bitcast.101, f32[16,2,512]{2,1,0:T(2,128)S(1)} %all-to-all-done.8.refs_2_, f32[256,512]{1,0:T(8,128)} %get-tuple-element.192.refs_3_, ...), custom_call_target="tpu_custom_call" | custom-call | tf_op jit(solution)/shard_map/pallas_call | solution.py:87
  178.0 4.6 %all-to-all-start.9 = ((bf16[16,2,3072]{2,1,0:T(2,128)(2,1)}), bf16[16,2,3072]{2,1,0:T(2,128)(2,1)S(1)}, u32[]{:S(2)}, u32[]{:S(2)}) async-start(bf16[16,2,3072]{2,1,0:T(2,128)(2,1)} %get-tuple-element.194), calls=%async_computation.9 | async-start | bytes 393216 | tf_op jit(solution)/shard_map/all_to_all | solution.py:701
  182.7 1.4 collective-permute-start.12
  184.1 1.4 collective-permute-done.12.refs_4_
  185.5 5.5 %all-to-all-done.9.refs_2_ = bf16[16,2,3072]{2,1,0:T(2,128)(2,1)S(1)} async-done(((bf16[16,2,3072]{2,1,0:T(2,128)(2,1)}), bf16[16,2,3072]{2,1,0:T(2,128)(2,1)S(1)}, u32[]{:S(2)}, u32[]{:S(2)}) %all-to-all-start.9) | async-done | bytes 196640 | tf_op jit(solution)/shard_map/all_to_all | solution.py:701
  191.0 2.1 fusion.12
  193.1 6.7 %shard_map.241 = (bf16[256,2048]{1,0:T(8,128)(2,1)}, bf16[256,2048]{1,0:T(8,128)(2,1)}, f32[256,512]{1,0:T(8,128)}, f32[3,2048]{1,0:T(4,128)}, f32[16,2,512]{2,1,0:T(2,128)}) custom-call(s32[2]{0:T(128)} %pad_add_fusion.refs_0_, s32[2,16]{1,0:T(2,128)} %bitcast.102, bf16[16,2,3072]{2,1,0:T(2,128)(2,1)S(1)} %all-to-all-done.9.refs_2_, ...), custom_call_target="tpu_custom_call" | custom-call | tf_op jit(solution)/shard_map/pallas_call | solution.py:87
  199.8 1.7 collective-permute-start.15
  203.0 5.5 %all-to-all-start.10 = ((f32[16,2,512]{2,1,0:T(2,128)}), f32[16,2,512]{2,1,0:T(2,128)S(1)}, u32[]{:S(2)}, u32[]{:S(2)}) async-start(f32[16,2,512]{2,1,0:T(2,128)} %get-tuple-element.204), calls=%async_computation.10 | async-start | bytes 131072 | tf_op jit(solution)/shard_map/all_to_all | solution.py:701
  208.6 7.9 %shard_map.242 = (bf16[2,4,256,256]{3,2,1,0:T(8,128)(2,1)}, bf16[2,4,256,256]{3,2,1,0:T(8,128)(2,1)}, bf16[2,4,256,256]{3,2,1,0:T(8,128)(2,1)}, bf16[2,4,256,256]{3,2,1,0:T(8,128)(2,1)}) custom-call(s32[2]{0:T(128)} %pad_add_fusion.refs_0_, bf16[256,2048]{1,0:T(8,128)(2,1)} %get-tuple-element.165.refs_4_.refs_1_, bf16[256,2048]{1,0:T(8,128)(2,1)} %copy-done.2, ...), custom_call_target="tpu_custom_call" | custom-call | tf_op jit(solution)/shard_map/pallas_call | solution.py:87
  218.9 8.2 %shard_map.243 = (bf16[256,512]{1,0:T(8,128)(2,1)}, bf16[1024,512]{1,0:T(8,128)(2,1)}, f32[2,512]{1,0:T(2,128)}, f32[16,2,512]{2,1,0:T(2,128)}) custom-call(s32[2]{0:T(128)} %pad_add_fusion.refs_0_, s32[2,16]{1,0:T(2,128)} %bitcast.103, f32[16,2,512]{2,1,0:T(2,128)S(1)} %all-to-all-done.10.refs_2_, f32[256,512]{1,0:T(8,128)} %get-tuple-element.216.refs_3_, ...), custom_call_target="tpu_custom_call" | custom-call | tf_op jit(solution)/shard_map/pallas_call | solution.py:87
  227.1 4.6 %all-to-all-start.11 = ((f32[16,2,512]{2,1,0:T(2,128)}), f32[16,2,512]{2,1,0:T(2,128)S(1)}, u32[]{:S(2)}, u32[]{:S(2)}) async-start(f32[16,2,512]{2,1,0:T(2,128)} %get-tuple-element.218), calls=%async_computation.11 | async-start | bytes 131072 | tf_op jit(solution)/shard_map/all_to_all | solution.py:701
  231.7 2.7 collective-permute-start.19
  234.4 1.6 fusion.9
  236.9 4.6 %all-to-all-done.11.refs_2_ = f32[16,2,512]{2,1,0:T(2,128)S(1)} async-done(((f32[16,2,512]{2,1,0:T(2,128)}), f32[16,2,512]{2,1,0:T(2,128)S(1)}, u32[]{:S(2)}, u32[]{:S(2)}) %all-to-all-start.11) | async-done | bytes 65568 | tf_op jit(solution)/shard_map/all_to_all | solution.py:701
  243.9 4.2 %shard_map.244 = (bf16[1024,512]{1,0:T(8,128)(2,1)}, f32[2,512]{1,0:T(2,128)}) custom-call(s32[2]{0:T(128)} %pad_add_fusion.refs_0_, s32[2,16]{1,0:T(2,128)} %bitcast.104, f32[16,2,512]{2,1,0:T(2,128)S(1)} %all-to-all-done.11.refs_2_, bf16[1024,512]{1,0:T(8,128)(2,1)} %get-tuple-element.228.refs_3_, ...), custom_call_target="tpu_custom_call" | custom-call | tf_op jit(solution)/shard_map/pallas_call | solution.py:87
  248.1 2.8 collective-permute-start.22
  251.0 1.3 collective-permute-start.23
  253.4 2.1 collective-permute-start.26
  255.5 1.3 broadcast_select_fusion.7
  257.8 9.9 %shard_map.245 = (bf16[2,4,176,256]{3,2,1,0:T(8,128)(2,1)}, bf16[2,4,176,256]{3,2,1,0:T(8,128)(2,1)}, bf16[2,4,176,256]{3,2,1,0:T(8,128)(2,1)}, bf16[2,4,176,256]{3,2,1,0:T(8,128)(2,1)}) custom-call(s32[2]{0:T(128)} %pad_add_fusion.refs_0_, bf16[256,4608]{1,0:T(8,128)(2,1)} %get-tuple-element.155.refs_1_, bf16[256,4608]{1,0:T(8,128)(2,1)} %collective-permute-done.4.refs_2_, ...), custom_call_target="tpu_custom_call" | custom-call | tf_op jit(solution)/shard_map/pallas_call | solution.py:87
  270.1 4.2 %collective-permute-done.27 = bf16[208,512]{1,0:T(8,128)(2,1)} collective-permute-done((bf16[208,512]{1,0:T(8,128)(2,1)}, bf16[208,512]{1,0:T(8,128)(2,1)}, u32[]{:S(2)}, u32[]{:S(2)}) %collective-permute-start.27) | collective-permute-done | bytes 213024 | tf_op jit(solution)/shard_map/ppermute | solution.py:709
  274.3 1.7 collective-permute-start.29
  277.4 1.2 collective-permute-start.30
  278.9 5.9 %shard_map.246 = bf16[1,14,14,4,1024]{4,3,2,1,0:T(4,128)(2,1)} custom-call(bf16[1024,512]{1,0:T(8,128)(2,1)} %get-tuple-element.249.refs_7_.refs_0_, bf16[1024,512]{1,0:T(8,128)(2,1)} %refs_1_.1, bf16[256,2048]{1,0:T(8,128)(2,1)} %get-tuple-element.210.refs_11_.refs_2_, bf16[1024,2048]{1,0:T(8,128)(2,1)} %refs_3_.5), custom_call_target="tpu_custom_call" | custom-call | tf_op jit(solution)/shard_map/pallas_call | solution.py:87
  285.0 2.3 collective-permute-start.38
  290.2 4.7 %collective-permute-done.30 = bf16[2,4,176,256]{3,2,1,0:T(8,128)(2,1)S(1)} collective-permute-done((bf16[2,4,176,256]{3,2,1,0:T(8,128)(2,1)}, bf16[2,4,176,256]{3,2,1,0:T(8,128)(2,1)S(1)}, u32[]{:S(2)}, u32[]{:S(2)}) %collective-permute-start.30) | collective-permute-done | bytes 720928 | tf_op jit(solution)/shard_map/ppermute | solution.py:709
  298.3 11.3 %collective-permute-done.39 = bf16[256,512]{1,0:T(8,128)(2,1)S(1)} collective-permute-done((bf16[256,512]{1,0:T(8,128)(2,1)S(1)}, bf16[256,512]{1,0:T(8,128)(2,1)S(1)}, u32[]{:S(2)}, u32[]{:S(2)}) %collective-permute-start.39) | collective-permute-done | bytes 262176 | tf_op jit(solution)/shard_map/ppermute | solution.py:709
  310.4 2.3 collective-permute-start.41
  312.9 2.4 collective-permute-start.35
  316.3 4.0 %collective-permute-done.34 = bf16[176,512]{1,0:T(8,128)(2,1)S(1)} collective-permute-done((bf16[176,512]{1,0:T(8,128)(2,1)S(1)}, bf16[176,512]{1,0:T(8,128)(2,1)S(1)}, u32[]{:S(2)}, u32[]{:S(2)}) %collective-permute-start.34) | collective-permute-done | bytes 180256 | tf_op jit(solution)/shard_map/ppermute | solution.py:709
  320.3 6.2 %collective-permute-done.35 = bf16[176,512]{1,0:T(8,128)(2,1)S(1)} collective-permute-done((bf16[176,512]{1,0:T(8,128)(2,1)S(1)}, bf16[176,512]{1,0:T(8,128)(2,1)S(1)}, u32[]{:S(2)}, u32[]{:S(2)}) %collective-permute-start.35) | collective-permute-done | bytes 180256 | tf_op jit(solution)/shard_map/ppermute | solution.py:709
  326.6 5.0 %collective-permute-done.36 = bf16[176,512]{1,0:T(8,128)(2,1)S(1)} collective-permute-done((bf16[176,512]{1,0:T(8,128)(2,1)S(1)}, bf16[176,512]{1,0:T(8,128)(2,1)S(1)}, u32[]{:S(2)}, u32[]{:S(2)}) %collective-permute-start.36) | collective-permute-done | bytes 180256 | tf_op jit(solution)/shard_map/ppermute | solution.py:709
  (166 shorter events, 32.3 us)
Async XLA Ops:
  0.7 21.5 %collective-permute-start.1 = (bf16[1,4608,512]{2,1,0:T(8,128)(2,1)}, bf16[1,4608,512]{2,1,0:T(8,128)(2,1)}, u32[]{:S(2)}, u32[]{:S(2)}) collective-permute-start(bf16[1,4608,512]{2,1,0:T(8,128)(2,1)} %refs_9_.3), channel_id=1, source_target_pairs={{0,16},{16,0},{1,17},{17,1},{2,18},{18,2},{3,19},{19,3},{4,20},{20... | collective-permute-start | bytes 14155784 | tf_op jit(solution)/shard_map/ppermute | solution.py:705
  8.3 28.0 %collective-permute-start.2 = (bf16[1024,1024]{1,0:T(8,128)(2,1)}, bf16[1024,1024]{1,0:T(8,128)(2,1)}, u32[]{:S(2)}, u32[]{:S(2)}) collective-permute-start(bf16[1024,1024]{1,0:T(8,128)(2,1)} %get-tuple-element.149.refs_2_.refs_9_.refs_5_), channel_id=1, source_target_pairs={{0,16},{16,0},{1,17},{17,1},{2,18},{18,2},{3,19},{19,3},{4,20},{20... | collective-permute-start | bytes 6291464 | tf_op jit(solution)/shard_map/ppermute | solution.py:705
  8.4 34.5 %collective-permute-start.3 = (bf16[1,512,2048]{2,1,0:T(8,128)(2,1)S(1)}, bf16[1,512,2048]{2,1,0:T(8,128)(2,1)}, u32[]{:S(2)}, u32[]{:S(2)}) collective-permute-start(bf16[1,512,2048]{2,1,0:T(8,128)(2,1)S(1)} %copy-done), channel_id=1, source_target_pairs={{0,16},{16,0},{1,17},{17,1},{2,18},{18,2},{3,19},{19,3},{4,20},{20... | collective-permute-start | bytes 6291464 | tf_op jit(solution)/shard_map/ppermute | solution.py:705
  8.9 12.7 %collective-permute-start = (f32[4,512]{1,0:T(4,128)S(1)}, f32[4,512]{1,0:T(4,128)S(1)}, u32[]{:S(2)}, u32[]{:S(2)}) collective-permute-start(f32[4,512]{1,0:T(4,128)S(1)} %pad_maximum_fusion.11), channel_id=1, source_target_pairs={{0,16},{16,0},{1,17},{17,1},{2,18},{18,2},{3,19},{19,3},{4,20},{20... | collective-permute-start | bytes 24584 | tf_op jit(solution)/shard_map/ppermute | solution.py:705
  9.1 13.1 %all-to-all-start = ((f32[16,2,512]{2,1,0:T(2,128)}), f32[16,2,512]{2,1,0:T(2,128)S(1)}, u32[]{:S(2)}, u32[]{:S(2)}) async-start(f32[16,2,512]{2,1,0:T(2,128)} %get-tuple-element.147), calls=%async_computation | async-start | bytes 131072 | tf_op jit(solution)/shard_map/all_to_all | solution.py:701
  22.2 13.4 %copy-start.19 = (f32[1,2048]{1,0:T(1,128)S(1)}, f32[1,2048]{1,0:T(1,128)}, u32[]{:S(2)}) copy-start(f32[1,2048]{1,0:T(1,128)} %param.27) | copy-start | bytes 24580
  22.2 13.4 %copy-start.20 = (f32[1,2048]{1,0:T(1,128)S(1)}, f32[1,2048]{1,0:T(1,128)}, u32[]{:S(2)}) copy-start(f32[1,2048]{1,0:T(1,128)} %param.26) | copy-start | bytes 24580
  28.2 32.1 %collective-permute-start.4 = (bf16[256,4608]{1,0:T(8,128)(2,1)}, bf16[256,4608]{1,0:T(8,128)(2,1)}, u32[]{:S(2)}, u32[]{:S(2)}) collective-permute-start(bf16[256,4608]{1,0:T(8,128)(2,1)} %get-tuple-element.155.refs_1_), channel_id=1, source_target_pairs={{0,16},{16,0},{1,17},{17,1},{2,18},{18,2},{3,19},{19,3},{4,20},{20... | collective-permute-start | bytes 7077896 | tf_op jit(solution)/shard_map/ppermute | solution.py:705
  29.2 13.7 %all-to-all-start.1 = ((bf16[16,2,3840]{2,1,0:T(2,128)(2,1)}), bf16[16,2,3840]{2,1,0:T(2,128)(2,1)S(1)}, u32[]{:S(2)}, u32[]{:S(2)}) async-start(bf16[16,2,3840]{2,1,0:T(2,128)(2,1)} %get-tuple-element.151), calls=%async_computation.1 | async-start | bytes 491520 | tf_op jit(solution)/shard_map/all_to_all | solution.py:701
  35.6 20.1 %collective-permute-start.5 = (f32[2,2048]{1,0:T(2,128)S(1)}, f32[2,2048]{1,0:T(2,128)S(1)}, u32[]{:S(2)}, u32[]{:S(2)}) collective-permute-start(f32[2,2048]{1,0:T(2,128)S(1)} %pad_maximum_fusion.9), channel_id=1, source_target_pairs={{0,16},{16,0},{1,17},{17,1},{2,18},{18,2},{3,19},{19,3},{4,20},{20... | collective-permute-start | bytes 49160 | tf_op jit(solution)/shard_map/ppermute | solution.py:705
  43.0 10.5 %copy-start.27 = (f32[2048]{0:T(1024)S(1)}, f32[2048]{0:T(1024)}, u32[]{:S(2)}) copy-start(f32[2048]{0:T(1024)} %param.20) | copy-start | bytes 24580
  43.0 10.5 %copy-start.28 = (f32[2048]{0:T(1024)S(1)}, f32[2048]{0:T(1024)}, u32[]{:S(2)}) copy-start(f32[2048]{0:T(1024)} %param.19) | copy-start | bytes 24580
  48.1 12.2 %all-to-all-start.2 = ((f32[16,2,2048]{2,1,0:T(2,128)}), f32[16,2,2048]{2,1,0:T(2,128)S(1)}, u32[]{:S(2)}, u32[]{:S(2)}) async-start(f32[16,2,2048]{2,1,0:T(2,128)} %get-tuple-element.154), calls=%async_computation.2 | async-start | bytes 524288 | tf_op jit(solution)/shard_map/all_to_all | solution.py:701
  54.1 17.7 %collective-permute-start.6 = (bf16[256,512]{1,0:T(8,128)(2,1)}, bf16[256,512]{1,0:T(8,128)(2,1)S(1)}, u32[]{:S(2)}, u32[]{:S(2)}) collective-permute-start(bf16[256,512]{1,0:T(8,128)(2,1)} %get-tuple-element.161.refs_5_), channel_id=1, source_target_pairs={{0,16},{16,0},{1,17},{17,1},{2,18},{18,2},{3,19},{19,3},{4,20},{20... | collective-permute-start | bytes 786440 | tf_op jit(solution)/shard_map/ppermute | solution.py:705
  65.9 11.4 %all-to-all-start.3 = ((f32[16,2,512]{2,1,0:T(2,128)}), f32[16,2,512]{2,1,0:T(2,128)S(1)}, u32[]{:S(2)}, u32[]{:S(2)}) async-start(f32[16,2,512]{2,1,0:T(2,128)} %get-tuple-element.160), calls=%async_computation.3 | async-start | bytes 131072 | tf_op jit(solution)/shard_map/all_to_all | solution.py:701
  71.8 11.4 %copy-start.12 = (bf16[256,512]{1,0:T(8,128)(2,1)}, bf16[256,512]{1,0:T(8,128)(2,1)S(1)}, u32[]{:S(2)}) copy-start(bf16[256,512]{1,0:T(8,128)(2,1)S(1)} %collective-permute-done.6.refs_6_) | copy-start | bytes 786436
  83.2 29.0 %collective-permute-start.8 = (bf16[256,4608]{1,0:T(8,128)(2,1)}, bf16[256,4608]{1,0:T(8,128)(2,1)}, u32[]{:S(2)}, u32[]{:S(2)}) collective-permute-start(bf16[256,4608]{1,0:T(8,128)(2,1)} %get-tuple-element.169.refs_5_), channel_id=1, source_target_pairs={{0,16},{16,0},{1,17},{17,1},{2,18},{18,2},{3,19},{19,3},{4,20},{20... | collective-permute-start | bytes 7077896 | tf_op jit(solution)/shard_map/ppermute | solution.py:705
  86.0 10.0 %collective-permute-start.7 = (bf16[256,2048]{1,0:T(8,128)(2,1)S(1)}, bf16[256,2048]{1,0:T(8,128)(2,1)S(1)}, u32[]{:S(2)}, u32[]{:S(2)}) collective-permute-start(bf16[256,2048]{1,0:T(8,128)(2,1)S(1)} %copy-done.1), channel_id=1, source_target_pairs={{0,16},{16,0},{1,17},{17,1},{2,18},{18,2},{3,19},{19,3},{4,20},{20... | collective-permute-start | bytes 3145736 | tf_op jit(solution)/shard_map/ppermute | solution.py:705
  100.9 11.3 %all-to-all-start.5 = ((f32[16,2,2048]{2,1,0:T(2,128)}), f32[16,2,2048]{2,1,0:T(2,128)S(1)}, u32[]{:S(2)}, u32[]{:S(2)}) async-start(f32[16,2,2048]{2,1,0:T(2,128)} %get-tuple-element.168), calls=%async_computation.5 | async-start | bytes 524288 | tf_op jit(solution)/shard_map/all_to_all | solution.py:701
  105.3 18.9 %collective-permute-start.9 = (bf16[256,512]{1,0:T(8,128)(2,1)}, bf16[256,512]{1,0:T(8,128)(2,1)S(1)}, u32[]{:S(2)}, u32[]{:S(2)}) collective-permute-start(bf16[256,512]{1,0:T(8,128)(2,1)} %get-tuple-element.174.refs_1_), channel_id=1, source_target_pairs={{0,16},{16,0},{1,17},{17,1},{2,18},{18,2},{3,19},{19,3},{4,20},{20... | collective-permute-start | bytes 786440 | tf_op jit(solution)/shard_map/ppermute | solution.py:705
  118.4 11.6 %all-to-all-start.6 = ((bf16[16,2,2048]{2,1,0:T(2,128)(2,1)}), bf16[16,2,2048]{2,1,0:T(2,128)(2,1)S(1)}, u32[]{:S(2)}, u32[]{:S(2)}) async-start(bf16[16,2,2048]{2,1,0:T(2,128)(2,1)} %get-tuple-element.173), calls=%async_computation.6 | async-start | bytes 262144 | tf_op jit(solution)/shard_map/all_to_all | solution.py:701
  124.2 11.1 %copy-start.14 = (bf16[256,512]{1,0:T(8,128)(2,1)}, bf16[256,512]{1,0:T(8,128)(2,1)S(1)}, u32[]{:S(2)}) copy-start(bf16[256,512]{1,0:T(8,128)(2,1)S(1)} %collective-permute-done.9.refs_2_) | copy-start | bytes 786436
  135.3 12.8 %collective-permute-start.10 = (bf16[256,2048]{1,0:T(8,128)(2,1)}, bf16[256,2048]{1,0:T(8,128)(2,1)S(1)}, u32[]{:S(2)}, u32[]{:S(2)}) collective-permute-start(bf16[256,2048]{1,0:T(8,128)(2,1)} %get-tuple-element.180.refs_3_), channel_id=1, source_target_pairs={{0,16},{16,0},{1,17},{17,1},{2,18},{18,2},{3,19},{19,3},{4,20},{20... | collective-permute-start | bytes 3145736 | tf_op jit(solution)/shard_map/ppermute | solution.py:705
  154.6 5.7 %collective-permute-start.11 = (bf16[256,512]{1,0:T(8,128)(2,1)}, bf16[256,512]{1,0:T(8,128)(2,1)S(1)}, u32[]{:S(2)}, u32[]{:S(2)}) collective-permute-start(bf16[256,512]{1,0:T(8,128)(2,1)} %get-tuple-element.188.refs_7_), channel_id=1, source_target_pairs={{0,16},{16,0},{1,17},{17,1},{2,18},{18,2},{3,19},{19,3},{4,20},{20... | collective-permute-start | bytes 786440 | tf_op jit(solution)/shard_map/ppermute | solution.py:705
  155.9 11.7 %all-to-all-start.8 = ((f32[16,2,512]{2,1,0:T(2,128)}), f32[16,2,512]{2,1,0:T(2,128)S(1)}, u32[]{:S(2)}, u32[]{:S(2)}) async-start(f32[16,2,512]{2,1,0:T(2,128)} %get-tuple-element.184), calls=%async_computation.8 | async-start | bytes 131072 | tf_op jit(solution)/shard_map/all_to_all | solution.py:701
  167.6 23.3 %collective-permute-start.13 = (bf16[2,4,208,256]{3,2,1,0:T(8,128)(2,1)}, bf16[2,4,208,256]{3,2,1,0:T(8,128)(2,1)S(1)}, u32[]{:S(2)}, u32[]{:S(2)}) collective-permute-start(bf16[2,4,208,256]{3,2,1,0:T(8,128)(2,1)} %get-tuple-element.198), channel_id=1, source_target_pairs={{0,1},{1,0},{2,3},{3,2},{4,5},{5,4},{6,7},{7,6},{8,9},{9,8},{10,11... | collective-permute-start | bytes 2555912 | tf_op jit(solution)/shard_map/ppermute | solution.py:709
  168.8 22.1 %collective-permute-start.14 = (bf16[2,4,208,256]{3,2,1,0:T(8,128)(2,1)}, bf16[2,4,208,256]{3,2,1,0:T(8,128)(2,1)}, u32[]{:S(2)}, u32[]{:S(2)}) collective-permute-start(bf16[2,4,208,256]{3,2,1,0:T(8,128)(2,1)} %get-tuple-element.200), channel_id=1, source_target_pairs={{0,2},{1,3},{2,0},{3,1},{4,6},{5,7},{6,4},{7,5},{8,10},{9,11},{10,... | collective-permute-start | bytes 2555912 | tf_op jit(solution)/shard_map/ppermute | solution.py:709
  170.0 20.9 %copy-start.7 = (bf16[2,4,208,256]{3,2,1,0:T(8,128)(2,1)S(1)}, bf16[2,4,208,256]{3,2,1,0:T(8,128)(2,1)}, u32[]{:S(2)}) copy-start(bf16[2,4,208,256]{3,2,1,0:T(8,128)(2,1)} %get-tuple-element.197) | copy-start | bytes 2555908
  170.0 21.0 %copy-start.8 = (bf16[2,4,208,256]{3,2,1,0:T(8,128)(2,1)S(1)}, bf16[2,4,208,256]{3,2,1,0:T(8,128)(2,1)}, u32[]{:S(2)}) copy-start(bf16[2,4,208,256]{3,2,1,0:T(8,128)(2,1)} %get-tuple-element.199) | copy-start | bytes 2555908
  178.0 12.9 %all-to-all-start.9 = ((bf16[16,2,3072]{2,1,0:T(2,128)(2,1)}), bf16[16,2,3072]{2,1,0:T(2,128)(2,1)S(1)}, u32[]{:S(2)}, u32[]{:S(2)}) async-start(bf16[16,2,3072]{2,1,0:T(2,128)(2,1)} %get-tuple-element.194), calls=%async_computation.9 | async-start | bytes 393216 | tf_op jit(solution)/shard_map/all_to_all | solution.py:701
  182.7 2.8 collective-permute-start.12
  185.5 14.3 %copy-start.15 = (bf16[256,512]{1,0:T(8,128)(2,1)}, bf16[256,512]{1,0:T(8,128)(2,1)S(1)}, u32[]{:S(2)}) copy-start(bf16[256,512]{1,0:T(8,128)(2,1)S(1)} %collective-permute-done.12.refs_4_) | copy-start | bytes 786436
  190.9 10.6 %copy-start.9 = (bf16[2,4,208,256]{3,2,1,0:T(8,128)(2,1)}, bf16[2,4,208,256]{3,2,1,0:T(8,128)(2,1)S(1)}, u32[]{:S(2)}) copy-start(bf16[2,4,208,256]{3,2,1,0:T(8,128)(2,1)S(1)} %collective-permute-done.13) | copy-start | bytes 2555908
  199.8 8.8 %collective-permute-start.15 = (bf16[256,2048]{1,0:T(8,128)(2,1)}, bf16[256,2048]{1,0:T(8,128)(2,1)S(1)}, u32[]{:S(2)}, u32[]{:S(2)}) collective-permute-start(bf16[256,2048]{1,0:T(8,128)(2,1)} %get-tuple-element.208.refs_7_), channel_id=1, source_target_pairs={{0,16},{16,0},{1,17},{17,1},{2,18},{18,2},{3,19},{19,3},{4,20},{20... | collective-permute-start | bytes 3145736 | tf_op jit(solution)/shard_map/ppermute | solution.py:705
  201.5 7.1 %collective-permute-start.16 = (bf16[256,2048]{1,0:T(8,128)(2,1)}, bf16[256,2048]{1,0:T(8,128)(2,1)S(1)}, u32[]{:S(2)}, u32[]{:S(2)}) collective-permute-start(bf16[256,2048]{1,0:T(8,128)(2,1)} %get-tuple-element.210.refs_11_.refs_2_), channel_id=1, source_target_pairs={{0,16},{16,0},{1,17},{17,1},{2,18},{18,2},{3,19},{19,3},{4,20},{20... | collective-permute-start | bytes 3145736 | tf_op jit(solution)/shard_map/ppermute | solution.py:705
  201.6 14.9 %collective-permute-start.17 = (bf16[4,208,256]{2,1,0:T(8,128)(2,1)S(1)}, bf16[4,208,256]{2,1,0:T(8,128)(2,1)}, u32[]{:S(2)}, u32[]{:S(2)}) collective-permute-start(bf16[4,208,256]{2,1,0:T(8,128)(2,1)S(1)} %fusion.13), channel_id=1, source_target_pairs={{0,2},{1,3},{2,0},{3,1},{4,6},{5,7},{6,4},{7,5},{8,10},{9,11},{10,... | collective-permute-start | bytes 1277960 | tf_op jit(solution)/shard_map/ppermute | solution.py:709
  202.8 13.7 %collective-permute-start.18 = (bf16[4,208,256]{2,1,0:T(8,128)(2,1)}, bf16[4,208,256]{2,1,0:T(8,128)(2,1)}, u32[]{:S(2)}, u32[]{:S(2)}) collective-permute-start(bf16[4,208,256]{2,1,0:T(8,128)(2,1)} %fusion.12), channel_id=1, source_target_pairs={{0,1},{1,0},{2,3},{3,2},{4,5},{5,4},{6,7},{7,6},{8,9},{9,8},{10,11... | collective-permute-start | bytes 1277960 | tf_op jit(solution)/shard_map/ppermute | solution.py:709
  203.0 13.4 %all-to-all-start.10 = ((f32[16,2,512]{2,1,0:T(2,128)}), f32[16,2,512]{2,1,0:T(2,128)S(1)}, u32[]{:S(2)}, u32[]{:S(2)}) async-start(f32[16,2,512]{2,1,0:T(2,128)} %get-tuple-element.204), calls=%async_computation.10 | async-start | bytes 131072 | tf_op jit(solution)/shard_map/all_to_all | solution.py:701
  216.5 25.1 %collective-permute-start.20 = (bf16[2,4,256,256]{3,2,1,0:T(8,128)(2,1)}, bf16[2,4,256,256]{3,2,1,0:T(8,128)(2,1)}, u32[]{:S(2)}, u32[]{:S(2)}) collective-permute-start(bf16[2,4,256,256]{3,2,1,0:T(8,128)(2,1)} %get-tuple-element.222), channel_id=1, source_target_pairs={{0,1},{1,0},{2,3},{3,2},{4,5},{5,4},{6,7},{7,6},{8,9},{9,8},{10,11... | collective-permute-start | bytes 3145736 | tf_op jit(solution)/shard_map/ppermute | solution.py:709
  217.7 25.1 %collective-permute-start.21 = (bf16[2,4,256,256]{3,2,1,0:T(8,128)(2,1)}, bf16[2,4,256,256]{3,2,1,0:T(8,128)(2,1)}, u32[]{:S(2)}, u32[]{:S(2)}) collective-permute-start(bf16[2,4,256,256]{3,2,1,0:T(8,128)(2,1)} %get-tuple-element.224), channel_id=1, source_target_pairs={{0,2},{1,3},{2,0},{3,1},{4,6},{5,7},{6,4},{7,5},{8,10},{9,11},{10,... | collective-permute-start | bytes 3145736 | tf_op jit(solution)/shard_map/ppermute | solution.py:709
  227.1 14.4 %all-to-all-start.11 = ((f32[16,2,512]{2,1,0:T(2,128)}), f32[16,2,512]{2,1,0:T(2,128)S(1)}, u32[]{:S(2)}, u32[]{:S(2)}) async-start(f32[16,2,512]{2,1,0:T(2,128)} %get-tuple-element.218), calls=%async_computation.11 | async-start | bytes 131072 | tf_op jit(solution)/shard_map/all_to_all | solution.py:701
  231.7 9.8 %collective-permute-start.19 = (bf16[256,512]{1,0:T(8,128)(2,1)}, bf16[256,512]{1,0:T(8,128)(2,1)S(1)}, u32[]{:S(2)}, u32[]{:S(2)}) collective-permute-start(bf16[256,512]{1,0:T(8,128)(2,1)} %get-tuple-element.219.refs_3_), channel_id=1, source_target_pairs={{0,16},{16,0},{1,17},{17,1},{2,18},{18,2},{3,19},{19,3},{4,20},{20... | collective-permute-start | bytes 786440 | tf_op jit(solution)/shard_map/ppermute | solution.py:705
  248.1 8.7 %collective-permute-start.22 = (bf16[1024,512]{1,0:T(8,128)(2,1)}, bf16[1024,512]{1,0:T(8,128)(2,1)S(1)}, u32[]{:S(2)}, u32[]{:S(2)}) collective-permute-start(bf16[1024,512]{1,0:T(8,128)(2,1)} %get-tuple-element.249.refs_7_.refs_0_), channel_id=1, source_target_pairs={{0,16},{16,0},{1,17},{17,1},{2,18},{18,2},{3,19},{19,3},{4,20},{20... | collective-permute-start | bytes 3145736 | tf_op jit(solution)/shard_map/ppermute | solution.py:705
  251.0 16.8 %collective-permute-start.23 = (bf16[4,256,256]{2,1,0:T(8,128)(2,1)S(1)}, bf16[4,256,256]{2,1,0:T(8,128)(2,1)S(1)}, u32[]{:S(2)}, u32[]{:S(2)}) collective-permute-start(bf16[4,256,256]{2,1,0:T(8,128)(2,1)S(1)} %fusion.5), channel_id=1, source_target_pairs={{0,2},{1,3},{2,0},{3,1},{4,6},{5,7},{6,4},{7,5},{8,10},{9,11},{10,... | collective-permute-start | bytes 1572872 | tf_op jit(solution)/shard_map/ppermute | solution.py:709
  252.2 15.6 %collective-permute-start.24 = (bf16[4,256,256]{2,1,0:T(8,128)(2,1)S(1)}, bf16[4,256,256]{2,1,0:T(8,128)(2,1)S(1)}, u32[]{:S(2)}, u32[]{:S(2)}) collective-permute-start(bf16[4,256,256]{2,1,0:T(8,128)(2,1)S(1)} %fusion.4), channel_id=1, source_target_pairs={{0,1},{1,0},{2,3},{3,2},{4,5},{5,4},{6,7},{7,6},{8,9},{9,8},{10,11... | collective-permute-start | bytes 1572872 | tf_op jit(solution)/shard_map/ppermute | solution.py:709
  253.1 16.9 %collective-permute-start.25 = (bf16[208,512]{1,0:T(8,128)(2,1)}, bf16[208,512]{1,0:T(8,128)(2,1)}, u32[]{:S(2)}, u32[]{:S(2)}) collective-permute-start(bf16[208,512]{1,0:T(8,128)(2,1)} %get-tuple-element.239), channel_id=1, source_target_pairs={{0,4},{1,5},{2,6},{3,7},{4,0},{5,1},{6,2},{7,3},{8,12},{9,13},{10,... | collective-permute-start | bytes 638984 | tf_op jit(solution)/shard_map/ppermute | solution.py:709
  253.4 16.7 %collective-permute-start.26 = (bf16[208,512]{1,0:T(8,128)(2,1)}, bf16[208,512]{1,0:T(8,128)(2,1)}, u32[]{:S(2)}, u32[]{:S(2)}) collective-permute-start(bf16[208,512]{1,0:T(8,128)(2,1)} %get-tuple-element.240), channel_id=1, source_target_pairs={{0,8},{1,9},{2,10},{3,11},{4,12},{5,13},{6,14},{7,15},{8,0},{9,1},... | collective-permute-start | bytes 638984 | tf_op jit(solution)/shard_map/ppermute | solution.py:709
  256.8 17.5 %collective-permute-start.27 = (bf16[208,512]{1,0:T(8,128)(2,1)}, bf16[208,512]{1,0:T(8,128)(2,1)}, u32[]{:S(2)}, u32[]{:S(2)}) collective-permute-start(bf16[208,512]{1,0:T(8,128)(2,1)} %get-tuple-element.241), channel_id=1, source_target_pairs={{0,12},{1,13},{2,14},{3,15},{4,8},{5,9},{6,10},{7,11},{8,4},{9,5},... | collective-permute-start | bytes 638984 | tf_op jit(solution)/shard_map/ppermute | solution.py:709
  274.3 10.7 %collective-permute-start.29 = (f32[2,2,512]{2,1,0:T(2,128)}, f32[2,2,512]{2,1,0:T(2,128)S(1)}, u32[]{:S(2)}, u32[]{:S(2)}) collective-permute-start(f32[2,2,512]{2,1,0:T(2,128)} %broadcast_select_fusion.7), channel_id=1, source_target_pairs={{0,16},{16,0},{1,17},{17,1},{2,18},{18,2},{3,19},{19,3},{4,20},{20... | collective-permute-start | bytes 24584 | tf_op jit(solution)/shard_map/ppermute | solution.py:705
  276.1 11.3 %collective-permute-start.28 = (f32[4,2048]{1,0:T(4,128)}, f32[4,2048]{1,0:T(4,128)S(1)}, u32[]{:S(2)}, u32[]{:S(2)}) collective-permute-start(f32[4,2048]{1,0:T(4,128)} %pad_maximum_fusion.8), channel_id=1, source_target_pairs={{0,16},{16,0},{1,17},{17,1},{2,18},{18,2},{3,19},{19,3},{4,20},{20... | collective-permute-start | bytes 98312 | tf_op jit(solution)/shard_map/ppermute | solution.py:705
  277.4 18.4 %copy-start.10 = (bf16[2,4,176,256]{3,2,1,0:T(8,128)(2,1)S(1)}, bf16[2,4,176,256]{3,2,1,0:T(8,128)(2,1)}, u32[]{:S(2)}) copy-start(bf16[2,4,176,256]{3,2,1,0:T(8,128)(2,1)} %get-tuple-element.256) | copy-start | bytes 2162692
  277.4 18.4 %copy-start.11 = (bf16[2,4,176,256]{3,2,1,0:T(8,128)(2,1)S(1)}, bf16[2,4,176,256]{3,2,1,0:T(8,128)(2,1)}, u32[]{:S(2)}) copy-start(bf16[2,4,176,256]{3,2,1,0:T(8,128)(2,1)} %get-tuple-element.258) | copy-start | bytes 2162692
  277.4 17.5 %collective-permute-start.30 = (bf16[2,4,176,256]{3,2,1,0:T(8,128)(2,1)}, bf16[2,4,176,256]{3,2,1,0:T(8,128)(2,1)S(1)}, u32[]{:S(2)}, u32[]{:S(2)}) collective-permute-start(bf16[2,4,176,256]{3,2,1,0:T(8,128)(2,1)} %get-tuple-element.253), channel_id=1, source_target_pairs={{0,1},{1,0},{2,3},{3,2},{4,5},{5,4},{6,7},{7,6},{8,9},{9,8},{10,11... | collective-permute-start | bytes 2162696 | tf_op jit(solution)/shard_map/ppermute | solution.py:709
  278.7 17.1 %collective-permute-start.31 = (bf16[2,4,176,256]{3,2,1,0:T(8,128)(2,1)}, bf16[2,4,176,256]{3,2,1,0:T(8,128)(2,1)S(1)}, u32[]{:S(2)}, u32[]{:S(2)}) collective-permute-start(bf16[2,4,176,256]{3,2,1,0:T(8,128)(2,1)} %get-tuple-element.254), channel_id=1, source_target_pairs={{0,2},{1,3},{2,0},{3,1},{4,6},{5,7},{6,4},{7,5},{8,10},{9,11},{10,... | collective-permute-start | bytes 2162696 | tf_op jit(solution)/shard_map/ppermute | solution.py:709
  284.9 12.1 %collective-permute-start.37 = (bf16[256,512]{1,0:T(8,128)(2,1)S(1)}, bf16[256,512]{1,0:T(8,128)(2,1)S(1)}, u32[]{:S(2)}, u32[]{:S(2)}) collective-permute-start(bf16[256,512]{1,0:T(8,128)(2,1)S(1)} %get-tuple-element.274), channel_id=1, source_target_pairs={{0,4},{1,5},{2,6},{3,7},{4,0},{5,1},{6,2},{7,3},{8,12},{9,13},{10,... | collective-permute-start | bytes 786440 | tf_op jit(solution)/shard_map/ppermute | solution.py:709
  285.0 13.3 %collective-permute-start.38 = (bf16[256,512]{1,0:T(8,128)(2,1)S(1)}, bf16[256,512]{1,0:T(8,128)(2,1)S(1)}, u32[]{:S(2)}, u32[]{:S(2)}) collective-permute-start(bf16[256,512]{1,0:T(8,128)(2,1)S(1)} %get-tuple-element.275), channel_id=1, source_target_pairs={{0,8},{1,9},{2,10},{3,11},{4,12},{5,13},{6,14},{7,15},{8,0},{9,1},... | collective-permute-start | bytes 786440 | tf_op jit(solution)/shard_map/ppermute | solution.py:709
  287.3 22.2 %collective-permute-start.39 = (bf16[256,512]{1,0:T(8,128)(2,1)S(1)}, bf16[256,512]{1,0:T(8,128)(2,1)S(1)}, u32[]{:S(2)}, u32[]{:S(2)}) collective-permute-start(bf16[256,512]{1,0:T(8,128)(2,1)S(1)} %get-tuple-element.276), channel_id=1, source_target_pairs={{0,12},{1,13},{2,14},{3,15},{4,8},{5,9},{6,10},{7,11},{8,4},{9,5},... | collective-permute-start | bytes 786440 | tf_op jit(solution)/shard_map/ppermute | solution.py:709
  295.9 16.8 %collective-permute-start.32 = (bf16[4,176,256]{2,1,0:T(8,128)(2,1)S(1)}, bf16[4,176,256]{2,1,0:T(8,128)(2,1)S(1)}, u32[]{:S(2)}, u32[]{:S(2)}) collective-permute-start(bf16[4,176,256]{2,1,0:T(8,128)(2,1)S(1)} %add_bitcast_fusion.1), channel_id=1, source_target_pairs={{0,2},{1,3},{2,0},{3,1},{4,6},{5,7},{6,4},{7,5},{8,10},{9,11},{10,... | collective-permute-start | bytes 1081352 | tf_op jit(solution)/shard_map/ppermute | solution.py:709
  296.2 16.5 %collective-permute-start.33 = (bf16[4,176,256]{2,1,0:T(8,128)(2,1)S(1)}, bf16[4,176,256]{2,1,0:T(8,128)(2,1)S(1)}, u32[]{:S(2)}, u32[]{:S(2)}) collective-permute-start(bf16[4,176,256]{2,1,0:T(8,128)(2,1)S(1)} %add_bitcast_fusion), channel_id=1, source_target_pairs={{0,1},{1,0},{2,3},{3,2},{4,5},{5,4},{6,7},{7,6},{8,9},{9,8},{10,11... | collective-permute-start | bytes 1081352 | tf_op jit(solution)/shard_map/ppermute | solution.py:709
  310.4 22.6 %collective-permute-start.41 = (f32[32,1024]{1,0:T(8,128)S(1)}, f32[32,1024]{1,0:T(8,128)S(1)}, u32[]{:S(2)}, u32[]{:S(2)}) collective-permute-start(f32[32,1024]{1,0:T(8,128)S(1)} %fusion.41), channel_id=1, source_target_pairs={{0,16},{16,0},{1,17},{17,1},{2,18},{18,2},{3,19},{19,3},{4,20},{20... | collective-permute-start | bytes 393224 | tf_op jit(solution)/shard_map/ppermute | solution.py:705
  312.9 7.5 %collective-permute-start.34 = (bf16[176,512]{1,0:T(8,128)(2,1)S(1)}, bf16[176,512]{1,0:T(8,128)(2,1)S(1)}, u32[]{:S(2)}, u32[]{:S(2)}) collective-permute-start(bf16[176,512]{1,0:T(8,128)(2,1)S(1)} %get-tuple-element.267), channel_id=1, source_target_pairs={{0,4},{1,5},{2,6},{3,7},{4,0},{5,1},{6,2},{7,3},{8,12},{9,13},{10,... | collective-permute-start | bytes 540680 | tf_op jit(solution)/shard_map/ppermute | solution.py:709
  312.9 13.6 %collective-permute-start.35 = (bf16[176,512]{1,0:T(8,128)(2,1)S(1)}, bf16[176,512]{1,0:T(8,128)(2,1)S(1)}, u32[]{:S(2)}, u32[]{:S(2)}) collective-permute-start(bf16[176,512]{1,0:T(8,128)(2,1)S(1)} %get-tuple-element.268), channel_id=1, source_target_pairs={{0,8},{1,9},{2,10},{3,11},{4,12},{5,13},{6,14},{7,15},{8,0},{9,1},... | collective-permute-start | bytes 540680 | tf_op jit(solution)/shard_map/ppermute | solution.py:709
  315.3 16.3 %collective-permute-start.36 = (bf16[176,512]{1,0:T(8,128)(2,1)S(1)}, bf16[176,512]{1,0:T(8,128)(2,1)S(1)}, u32[]{:S(2)}, u32[]{:S(2)}) collective-permute-start(bf16[176,512]{1,0:T(8,128)(2,1)S(1)} %get-tuple-element.269), channel_id=1, source_target_pairs={{0,12},{1,13},{2,14},{3,15},{4,8},{5,9},{6,10},{7,11},{8,4},{9,5},... | collective-permute-start | bytes 540680 | tf_op jit(solution)/shard_map/ppermute | solution.py:709
  331.7 2.6 collective-permute-start.40
  (17 other events, 138.7 us)

commit v3 on v2

--- a/solution.py
+++ b/solution.py
@@ -412,7 +412,11 @@
     choice.wait()
     z_out.ref[...] = dot(a_out.ref[...], weight[...]).astype(BF16)
     z_out.send()
-    send_rows(sent, (local_stats(z_out.ref, geo, count, 1),))
+    values = local_stats(z_out.ref, geo, count, 1)
+    if extra:
+        send_rows(sent, (values,))
+    else:
+        send_short(sent, packed_stats((values,)))
     sent.send()
     if extra:
         lanes = slice(z_ref.shape[1], got.shape[2])
@@ -454,7 +458,7 @@
     count = counts[section, place[0]]
     load = pltpu.make_async_copy(out_grad.at[section], raw, sem.at[0])
     load.start()
-    average, inverse = combined(got, slice(None), counts, section, geo.pixels)
+    average, inverse = combined(Unpacked(got), slice(None), counts, section, geo.pixels)
     moments[0:1, :] = average
     moments[1:2, :] = inverse
     g_ref = flat
@@ -956,7 +960,12 @@
     got, joined_other = partner(joined, got)
     c2, u3, mom5, sent = stage(
         bound(expand_kernel, 1, False),
-        (spec((rows, mid), BF16), spec((rows, out), BF16), spec((2, mid)), spec((devices, 2, out))),
+        (
+            spec((rows, mid), BF16),
+            spec((rows, out), BF16),
+            spec((2, mid)),
+            spec((devices, 2, 3 * out // 2), BF16),
+        ),
         "dddd",
         (place, counts, got, u2, narrow1, w_expand, expand_other),
         "ssgddaa",

time: 337 us -> 336 us (level)
  no operation moved by 1% of the time
where the time goes in v3:
time: 336 us; the launch traced here: 334 us
  Pallas kernels  116 us (35%)
  starting transfers between devices  99.3 us (30%)
  waiting for transfers between devices  75.4 us (22%)
  blocking collectives  19.6 us (6%)
  other arithmetic  18.5 us (6%)
  local copies, waits for them, and re-layouts  4.02 us (1%)
    pallas_call x18, Pallas kernels, stage(): pl.pallas_call(run, out_shape=list(outs), in_specs=[kinds[kind] for kind...  116 us
    all_to_all x10, starting transfers between devices, exchange(): return lax.all_to_all(sent, 'dp', 0, 0)  53 us
    ppermute x21, waiting for transfers between devices, across(): lax.ppermute(value, 'dp', [(i, i ^ mask) for i in range(lax.axis_size('dp...  37.6 us
    all_to_all x10, waiting for transfers between devices, exchange(): return lax.all_to_all(sent, 'dp', 0, 0)  36.4 us
    ppermute x21, starting transfers between devices, swapped(): return lax.ppermute(value, 'section', [(0, 1), (1, 0)])  27.6 us
    all_to_all x2, blocking collectives, exchange(): return lax.all_to_all(sent, 'dp', 0, 0)  19.6 us
    ppermute x21, starting transfers between devices, across(): lax.ppermute(value, 'dp', [(i, i ^ mask) for i in range(lax.axis_size('dp...  18.7 us
  transfers between devices with their start and end apart: 52, of which 16 were waited for; matrix products, arithmetic and copies ran while one was open for 5% of the time, Pallas kernels for 26%

profile of v3, /device:TPU:9, one launch (start us, length us, event | category | flops | bytes accessed | tf_op | source)
XLA Modules:
  0.0 334.0 jit_solution(4510044481628911817)
XLA Ops:
  2.1 6.2 %shard_map.229 = (bf16[1024,1024]{1,0:T(8,128)(2,1)}, bf16[1024,512]{1,0:T(8,128)(2,1)}, f32[16,2,512]{2,1,0:T(2,128)}) custom-call(s32[2]{0:T(128)} %pad_add_fusion.refs_0_, s32[2,16]{1,0:T(2,128)} %bitcast.91, bf16[2,14,14,4,1024]{4,3,2,1,0:T(4,128)(2,1)} %bitcast.88, bf16[1024,512]{1,0:T(8,128)(2,1)} %refs_1_.1), custom_call_target="tpu_custom_call" | custom-call | tf_op jit(solution)/shard_map/pallas_call | solution.py:87
  9.1 6.7 %all-to-all-start = ((f32[16,2,512]{2,1,0:T(2,128)}), f32[16,2,512]{2,1,0:T(2,128)S(1)}, u32[]{:S(2)}, u32[]{:S(2)}) async-start(f32[16,2,512]{2,1,0:T(2,128)} %get-tuple-element.147), calls=%async_computation | async-start | bytes 131072 | tf_op jit(solution)/shard_map/all_to_all | solution.py:705
  15.7 5.8 %shard_map.230 = (bf16[256,2048]{1,0:T(8,128)(2,1)}, f32[2,2048]{1,0:T(2,128)}) custom-call(s32[2]{0:T(128)} %pad_add_fusion.refs_0_, s32[2,16]{1,0:T(2,128)} %bitcast.92, bf16[1024,1024]{1,0:T(8,128)(2,1)} %get-tuple-element.149.refs_2_.refs_9_.refs_5_, bf16[1024,2048]{1,0:T(8,128)(2,1)} %refs_3_.5), custom_call_target="tpu_custom_call" | custom-call | tf_op jit(solution)/shard_map/pallas_call | solution.py:87
  22.2 6.0 %shard_map.231 = (bf16[256,4608]{1,0:T(8,128)(2,1)}, f32[256,512]{1,0:T(8,128)}, f32[2,512]{1,0:T(2,128)}, bf16[16,2,3840]{2,1,0:T(2,128)(2,1)}) custom-call(s32[2]{0:T(128)} %pad_add_fusion.refs_0_, s32[2,16]{1,0:T(2,128)} %bitcast.93, f32[16,2,512]{2,1,0:T(2,128)S(1)} %all-to-all-done.refs_2_, ...), custom_call_target="tpu_custom_call" | custom-call | tf_op jit(solution)/shard_map/pallas_call | solution.py:87
  29.2 6.4 %all-to-all-start.1 = ((bf16[16,2,3840]{2,1,0:T(2,128)(2,1)}), bf16[16,2,3840]{2,1,0:T(2,128)(2,1)S(1)}, u32[]{:S(2)}, u32[]{:S(2)}) async-start(bf16[16,2,3840]{2,1,0:T(2,128)(2,1)} %get-tuple-element.151), calls=%async_computation.1 | async-start | bytes 491520 | tf_op jit(solution)/shard_map/all_to_all | solution.py:705
  36.3 6.7 %all-to-all-done.1.refs_2_ = bf16[16,2,3840]{2,1,0:T(2,128)(2,1)S(1)} async-done(((bf16[16,2,3840]{2,1,0:T(2,128)(2,1)}), bf16[16,2,3840]{2,1,0:T(2,128)(2,1)S(1)}, u32[]{:S(2)}, u32[]{:S(2)}) %all-to-all-start.1) | async-done | bytes 245792 | tf_op jit(solution)/shard_map/all_to_all | solution.py:705
  43.0 5.2 %shard_map.232 = (bf16[256,512]{1,0:T(8,128)(2,1)}, bf16[256,2048]{1,0:T(8,128)(2,1)}, f32[2,512]{1,0:T(2,128)}, f32[2,2048]{1,0:T(2,128)}, f32[16,2,2048]{2,1,0:T(2,128)}) custom-call(s32[2]{0:T(128)} %pad_add_fusion.refs_0_, s32[2,16]{1,0:T(2,128)} %bitcast.94, bf16[16,2,3840]{2,1,0:T(2,128)(2,1)S(1)} %all-to-all-done.1.refs_2_, ...), custom_call_target="tpu_custom_call" | custom-call | tf_op jit(solution)/shard_map/pallas_call | solution.py:87
  48.1 5.4 %all-to-all-start.2 = ((f32[16,2,2048]{2,1,0:T(2,128)}), f32[16,2,2048]{2,1,0:T(2,128)S(1)}, u32[]{:S(2)}, u32[]{:S(2)}) async-start(f32[16,2,2048]{2,1,0:T(2,128)} %get-tuple-element.154), calls=%async_computation.2 | async-start | bytes 524288 | tf_op jit(solution)/shard_map/all_to_all | solution.py:705
  54.1 1.6 collective-permute-start.6
  56.3 4.0 %all-to-all-done.2.refs_2_ = f32[16,2,2048]{2,1,0:T(2,128)S(1)} async-done(((f32[16,2,2048]{2,1,0:T(2,128)}), f32[16,2,2048]{2,1,0:T(2,128)S(1)}, u32[]{:S(2)}, u32[]{:S(2)}) %all-to-all-start.2) | async-done | bytes 262176 | tf_op jit(solution)/shard_map/all_to_all | solution.py:705
  60.3 5.5 %shard_map.233 = (bf16[256,2048]{1,0:T(8,128)(2,1)}, f32[256,512]{1,0:T(8,128)}, f32[4,2048]{1,0:T(4,128)}, f32[16,2,512]{2,1,0:T(2,128)}) custom-call(s32[2]{0:T(128)} %pad_add_fusion.refs_0_, s32[2,16]{1,0:T(2,128)} %bitcast.95, f32[16,2,2048]{2,1,0:T(2,128)S(1)} %all-to-all-done.2.refs_2_, bf16[256,2048]{1,0:T(8,128)(2,1)} %get-tuple-element.157.refs_3_.refs_9_.refs_4_, ...), custom_call_target="tpu_custom_call" | custom-call | tf_op jit(solution)/shard_map/pallas_call | solution.py:87
  65.9 5.9 %all-to-all-start.3 = ((f32[16,2,512]{2,1,0:T(2,128)}), f32[16,2,512]{2,1,0:T(2,128)S(1)}, u32[]{:S(2)}, u32[]{:S(2)}) async-start(f32[16,2,512]{2,1,0:T(2,128)} %get-tuple-element.160), calls=%async_computation.3 | async-start | bytes 131072 | tf_op jit(solution)/shard_map/all_to_all | solution.py:705
  71.8 5.4 %all-to-all-done.3.refs_2_ = f32[16,2,512]{2,1,0:T(2,128)S(1)} async-done(((f32[16,2,512]{2,1,0:T(2,128)}), f32[16,2,512]{2,1,0:T(2,128)S(1)}, u32[]{:S(2)}, u32[]{:S(2)}) %all-to-all-start.3) | async-done | bytes 65568 | tf_op jit(solution)/shard_map/all_to_all | solution.py:705
  77.3 5.9 %shard_map.234 = (bf16[256,4608]{1,0:T(8,128)(2,1)}, f32[256,512]{1,0:T(8,128)}, f32[2,512]{1,0:T(2,128)}, f32[16,2,512]{2,1,0:T(2,128)}) custom-call(s32[2]{0:T(128)} %pad_add_fusion.refs_0_, s32[2,16]{1,0:T(2,128)} %bitcast.96, f32[16,2,512]{2,1,0:T(2,128)S(1)} %all-to-all-done.3.refs_2_, f32[256,512]{1,0:T(8,128)} %get-tuple-element.163.refs_3_.refs_7_.refs_4_, ...), custom_call_target="tpu_custom_call" | custom-call | tf_op jit(solution)/shard_map/pallas_call | solution.py:87
  83.2 2.8 collective-permute-start.8
  86.1 9.9 %all_to_all.60.refs_2_ = f32[16,2,512]{2,1,0:T(2,128)S(1)} all-to-all(f32[16,2,512]{2,1,0:T(2,128)} %get-tuple-element.164), channel_id=1, replica_groups=mesh['section'=2,'dp'=16] {'dp'}, dimensions={0} | all-to-all | bytes 131072 | tf_op jit(solution)/shard_map/all_to_all | solution.py:705
  96.0 4.9 %shard_map.235 = (bf16[256,512]{1,0:T(8,128)(2,1)}, bf16[256,2048]{1,0:T(8,128)(2,1)}, f32[2,512]{1,0:T(2,128)}, bf16[16,2,3072]{2,1,0:T(2,128)(2,1)}) custom-call(s32[2]{0:T(128)} %pad_add_fusion.refs_0_, s32[2,16]{1,0:T(2,128)} %bitcast.97, f32[16,2,512]{2,1,0:T(2,128)S(1)} %all_to_all.60.refs_2_, f32[256,512]{1,0:T(8,128)} %get-tuple-element.167.refs_3_.refs_7_.refs_4_, ...), custom_call_target="tpu_custom_call" | custom-call | tf_op jit(solution)/shard_map/pallas_call | solution.py:87
  100.8 4.4 %all-to-all-start.5 = ((bf16[16,2,3072]{2,1,0:T(2,128)(2,1)}), bf16[16,2,3072]{2,1,0:T(2,128)(2,1)S(1)}, u32[]{:S(2)}, u32[]{:S(2)}) async-start(bf16[16,2,3072]{2,1,0:T(2,128)(2,1)} %get-tuple-element.168), calls=%async_computation.5 | async-start | bytes 393216 | tf_op jit(solution)/shard_map/all_to_all | solution.py:705
  105.3 1.9 collective-permute-start.9
  107.1 4.4 %all-to-all-done.5.refs_2_ = bf16[16,2,3072]{2,1,0:T(2,128)(2,1)S(1)} async-done(((bf16[16,2,3072]{2,1,0:T(2,128)(2,1)}), bf16[16,2,3072]{2,1,0:T(2,128)(2,1)S(1)}, u32[]{:S(2)}, u32[]{:S(2)}) %all-to-all-start.5) | async-done | bytes 196640 | tf_op jit(solution)/shard_map/all_to_all | solution.py:705
  111.6 6.3 %shard_map.236 = (bf16[1,7,7,4,2048]{4,3,2,1,0:T(4,128)(2,1)}, bf16[256,2048]{1,0:T(8,128)(2,1)}, f32[2,2048]{1,0:T(2,128)}, bf16[16,2,2048]{2,1,0:T(2,128)(2,1)}) custom-call(s32[2]{0:T(128)} %pad_add_fusion.refs_0_, s32[2,16]{1,0:T(2,128)} %bitcast.98, bf16[16,2,3072]{2,1,0:T(2,128)(2,1)S(1)} %all-to-all-done.5.refs_2_, ...), custom_call_target="tpu_custom_call" | custom-call | tf_op jit(solution)/shard_map/pallas_call | solution.py:87
  117.9 5.2 %all-to-all-start.6 = ((bf16[16,2,2048]{2,1,0:T(2,128)(2,1)}), bf16[16,2,2048]{2,1,0:T(2,128)(2,1)S(1)}, u32[]{:S(2)}, u32[]{:S(2)}) async-start(bf16[16,2,2048]{2,1,0:T(2,128)(2,1)} %get-tuple-element.173), calls=%async_computation.6 | async-start | bytes 262144 | tf_op jit(solution)/shard_map/all_to_all | solution.py:705
  123.0 5.8 %all-to-all-done.6.refs_2_ = bf16[16,2,2048]{2,1,0:T(2,128)(2,1)S(1)} async-done(((bf16[16,2,2048]{2,1,0:T(2,128)(2,1)}), bf16[16,2,2048]{2,1,0:T(2,128)(2,1)S(1)}, u32[]{:S(2)}, u32[]{:S(2)}) %all-to-all-start.6) | async-done | bytes 131104 | tf_op jit(solution)/shard_map/all_to_all | solution.py:705
  128.8 5.4 %shard_map.237 = (bf16[256,2048]{1,0:T(8,128)(2,1)}, f32[256,512]{1,0:T(8,128)}, f32[2,2048]{1,0:T(2,128)}, f32[16,2,512]{2,1,0:T(2,128)}) custom-call(s32[2]{0:T(128)} %pad_add_fusion.refs_0_, s32[2,16]{1,0:T(2,128)} %bitcast.99, bf16[16,2,2048]{2,1,0:T(2,128)(2,1)S(1)} %all-to-all-done.6.refs_2_, bf16[256,2048]{1,0:T(8,128)(2,1)} %get-tuple-element.176.refs_3_.refs_8_, ...), custom_call_target="tpu_custom_call" | custom-call | tf_op jit(solution)/shard_map/pallas_call | solution.py:87
  134.2 2.9 collective-permute-start.10
  137.1 9.8 %all_to_all.61.refs_2_ = f32[16,2,512]{2,1,0:T(2,128)S(1)} all-to-all(f32[16,2,512]{2,1,0:T(2,128)} %get-tuple-element.179), channel_id=1, replica_groups=mesh['section'=2,'dp'=16] {'dp'}, dimensions={0} | all-to-all | bytes 131072 | tf_op jit(solution)/shard_map/all_to_all | solution.py:705
  146.9 6.4 %shard_map.238 = (bf16[256,512]{1,0:T(8,128)(2,1)}, f32[256,512]{1,0:T(8,128)}, f32[2,512]{1,0:T(2,128)}, f32[16,2,512]{2,1,0:T(2,128)}) custom-call(s32[2]{0:T(128)} %pad_add_fusion.refs_0_, s32[2,16]{1,0:T(2,128)} %bitcast.100, f32[16,2,512]{2,1,0:T(2,128)S(1)} %all_to_all.61.refs_2_, f32[256,512]{1,0:T(8,128)} %get-tuple-element.182.refs_3_, ...), custom_call_target="tpu_custom_call" | custom-call | tf_op jit(solution)/shard_map/pallas_call | solution.py:87
  153.3 1.3 collective-permute-start.11
  154.6 4.4 %all-to-all-start.8 = ((f32[16,2,512]{2,1,0:T(2,128)}), f32[16,2,512]{2,1,0:T(2,128)S(1)}, u32[]{:S(2)}, u32[]{:S(2)}) async-start(f32[16,2,512]{2,1,0:T(2,128)} %get-tuple-element.184), calls=%async_computation.8 | async-start | bytes 131072 | tf_op jit(solution)/shard_map/all_to_all | solution.py:705
  159.0 7.2 %shard_map.239 = (bf16[2,4,208,256]{3,2,1,0:T(8,128)(2,1)}, bf16[2,4,208,256]{3,2,1,0:T(8,128)(2,1)}, bf16[2,4,208,256]{3,2,1,0:T(8,128)(2,1)}, bf16[2,4,208,256]{3,2,1,0:T(8,128)(2,1)}) custom-call(s32[2]{0:T(128)} %pad_add_fusion.refs_0_, bf16[256,512]{1,0:T(8,128)(2,1)} %get-tuple-element.174.refs_1_, bf16[256,512]{1,0:T(8,128)(2,1)} %copy-done.14, ...), custom_call_target="tpu_custom_call" | custom-call | tf_op jit(solution)/shard_map/pallas_call | solution.py:87
  166.3 1.3 collective-permute-start.13
  168.8 8.0 %shard_map.240 = (bf16[256,512]{1,0:T(8,128)(2,1)}, bf16[256,2048]{1,0:T(8,128)(2,1)}, f32[2,512]{1,0:T(2,128)}, bf16[16,2,3072]{2,1,0:T(2,128)(2,1)}) custom-call(s32[2]{0:T(128)} %pad_add_fusion.refs_0_, s32[2,16]{1,0:T(2,128)} %bitcast.101, f32[16,2,512]{2,1,0:T(2,128)S(1)} %all-to-all-done.8.refs_2_, f32[256,512]{1,0:T(8,128)} %get-tuple-element.192.refs_3_, ...), custom_call_target="tpu_custom_call" | custom-call | tf_op jit(solution)/shard_map/pallas_call | solution.py:87
  176.7 4.6 %all-to-all-start.9 = ((bf16[16,2,3072]{2,1,0:T(2,128)(2,1)}), bf16[16,2,3072]{2,1,0:T(2,128)(2,1)S(1)}, u32[]{:S(2)}, u32[]{:S(2)}) async-start(bf16[16,2,3072]{2,1,0:T(2,128)(2,1)} %get-tuple-element.194), calls=%async_computation.9 | async-start | bytes 393216 | tf_op jit(solution)/shard_map/all_to_all | solution.py:705
  181.4 1.4 collective-permute-start.12
  182.8 1.4 collective-permute-done.12.refs_4_
  184.2 5.5 %all-to-all-done.9.refs_2_ = bf16[16,2,3072]{2,1,0:T(2,128)(2,1)S(1)} async-done(((bf16[16,2,3072]{2,1,0:T(2,128)(2,1)}), bf16[16,2,3072]{2,1,0:T(2,128)(2,1)S(1)}, u32[]{:S(2)}, u32[]{:S(2)}) %all-to-all-start.9) | async-done | bytes 196640 | tf_op jit(solution)/shard_map/all_to_all | solution.py:705
  189.7 2.1 fusion.12
  191.8 6.7 %shard_map.241 = (bf16[256,2048]{1,0:T(8,128)(2,1)}, bf16[256,2048]{1,0:T(8,128)(2,1)}, f32[256,512]{1,0:T(8,128)}, f32[3,2048]{1,0:T(4,128)}, f32[16,2,512]{2,1,0:T(2,128)}) custom-call(s32[2]{0:T(128)} %pad_add_fusion.refs_0_, s32[2,16]{1,0:T(2,128)} %bitcast.102, bf16[16,2,3072]{2,1,0:T(2,128)(2,1)S(1)} %all-to-all-done.9.refs_2_, ...), custom_call_target="tpu_custom_call" | custom-call | tf_op jit(solution)/shard_map/pallas_call | solution.py:87
  198.5 1.7 collective-permute-start.15
  201.7 5.5 %all-to-all-start.10 = ((f32[16,2,512]{2,1,0:T(2,128)}), f32[16,2,512]{2,1,0:T(2,128)S(1)}, u32[]{:S(2)}, u32[]{:S(2)}) async-start(f32[16,2,512]{2,1,0:T(2,128)} %get-tuple-element.204), calls=%async_computation.10 | async-start | bytes 131072 | tf_op jit(solution)/shard_map/all_to_all | solution.py:705
  207.3 7.9 %shard_map.242 = (bf16[2,4,256,256]{3,2,1,0:T(8,128)(2,1)}, bf16[2,4,256,256]{3,2,1,0:T(8,128)(2,1)}, bf16[2,4,256,256]{3,2,1,0:T(8,128)(2,1)}, bf16[2,4,256,256]{3,2,1,0:T(8,128)(2,1)}) custom-call(s32[2]{0:T(128)} %pad_add_fusion.refs_0_, bf16[256,2048]{1,0:T(8,128)(2,1)} %get-tuple-element.165.refs_4_.refs_1_, bf16[256,2048]{1,0:T(8,128)(2,1)} %copy-done.2, ...), custom_call_target="tpu_custom_call" | custom-call | tf_op jit(solution)/shard_map/pallas_call | solution.py:87
  215.2 1.2 collective-permute-start.20
  217.6 8.2 %shard_map.243 = (bf16[256,512]{1,0:T(8,128)(2,1)}, bf16[1024,512]{1,0:T(8,128)(2,1)}, f32[2,512]{1,0:T(2,128)}, f32[16,2,512]{2,1,0:T(2,128)}) custom-call(s32[2]{0:T(128)} %pad_add_fusion.refs_0_, s32[2,16]{1,0:T(2,128)} %bitcast.103, f32[16,2,512]{2,1,0:T(2,128)S(1)} %all-to-all-done.10.refs_2_, f32[256,512]{1,0:T(8,128)} %get-tuple-element.216.refs_3_, ...), custom_call_target="tpu_custom_call" | custom-call | tf_op jit(solution)/shard_map/pallas_call | solution.py:87
  225.8 4.6 %all-to-all-start.11 = ((f32[16,2,512]{2,1,0:T(2,128)}), f32[16,2,512]{2,1,0:T(2,128)S(1)}, u32[]{:S(2)}, u32[]{:S(2)}) async-start(f32[16,2,512]{2,1,0:T(2,128)} %get-tuple-element.218), calls=%async_computation.11 | async-start | bytes 131072 | tf_op jit(solution)/shard_map/all_to_all | solution.py:705
  230.4 2.7 collective-permute-start.19
  233.1 1.6 fusion.9
  235.6 4.6 %all-to-all-done.11.refs_2_ = f32[16,2,512]{2,1,0:T(2,128)S(1)} async-done(((f32[16,2,512]{2,1,0:T(2,128)}), f32[16,2,512]{2,1,0:T(2,128)S(1)}, u32[]{:S(2)}, u32[]{:S(2)}) %all-to-all-start.11) | async-done | bytes 65568 | tf_op jit(solution)/shard_map/all_to_all | solution.py:705
  242.6 4.2 %shard_map.244 = (bf16[1024,512]{1,0:T(8,128)(2,1)}, f32[2,512]{1,0:T(2,128)}) custom-call(s32[2]{0:T(128)} %pad_add_fusion.refs_0_, s32[2,16]{1,0:T(2,128)} %bitcast.104, f32[16,2,512]{2,1,0:T(2,128)S(1)} %all-to-all-done.11.refs_2_, bf16[1024,512]{1,0:T(8,128)(2,1)} %get-tuple-element.228.refs_3_, ...), custom_call_target="tpu_custom_call" | custom-call | tf_op jit(solution)/shard_map/pallas_call | solution.py:87
  246.8 2.8 collective-permute-start.22
  252.1 2.1 collective-permute-start.26
  254.2 1.3 broadcast_select_fusion.7
  256.5 9.9 %shard_map.245 = (bf16[2,4,176,256]{3,2,1,0:T(8,128)(2,1)}, bf16[2,4,176,256]{3,2,1,0:T(8,128)(2,1)}, bf16[2,4,176,256]{3,2,1,0:T(8,128)(2,1)}, bf16[2,4,176,256]{3,2,1,0:T(8,128)(2,1)}) custom-call(s32[2]{0:T(128)} %pad_add_fusion.refs_0_, bf16[256,4608]{1,0:T(8,128)(2,1)} %get-tuple-element.155.refs_1_, bf16[256,4608]{1,0:T(8,128)(2,1)} %collective-permute-done.4.refs_2_, ...), custom_call_target="tpu_custom_call" | custom-call | tf_op jit(solution)/shard_map/pallas_call | solution.py:87
  268.8 4.2 %collective-permute-done.27 = bf16[208,512]{1,0:T(8,128)(2,1)} collective-permute-done((bf16[208,512]{1,0:T(8,128)(2,1)}, bf16[208,512]{1,0:T(8,128)(2,1)}, u32[]{:S(2)}, u32[]{:S(2)}) %collective-permute-start.27) | collective-permute-done | bytes 213024 | tf_op jit(solution)/shard_map/ppermute | solution.py:713
  273.0 1.7 collective-permute-start.29
  276.1 1.2 collective-permute-start.30
  277.7 5.9 %shard_map.246 = bf16[1,14,14,4,1024]{4,3,2,1,0:T(4,128)(2,1)} custom-call(bf16[1024,512]{1,0:T(8,128)(2,1)} %get-tuple-element.249.refs_7_.refs_0_, bf16[1024,512]{1,0:T(8,128)(2,1)} %refs_1_.1, bf16[256,2048]{1,0:T(8,128)(2,1)} %get-tuple-element.210.refs_11_.refs_2_, bf16[1024,2048]{1,0:T(8,128)(2,1)} %refs_3_.5), custom_call_target="tpu_custom_call" | custom-call | tf_op jit(solution)/shard_map/pallas_call | solution.py:87
  283.7 2.3 collective-permute-start.38
  288.9 4.7 %collective-permute-done.30 = bf16[2,4,176,256]{3,2,1,0:T(8,128)(2,1)S(1)} collective-permute-done((bf16[2,4,176,256]{3,2,1,0:T(8,128)(2,1)}, bf16[2,4,176,256]{3,2,1,0:T(8,128)(2,1)S(1)}, u32[]{:S(2)}, u32[]{:S(2)}) %collective-permute-start.30) | collective-permute-done | bytes 720928 | tf_op jit(solution)/shard_map/ppermute | solution.py:713
  297.0 11.3 %collective-permute-done.39 = bf16[256,512]{1,0:T(8,128)(2,1)S(1)} collective-permute-done((bf16[256,512]{1,0:T(8,128)(2,1)S(1)}, bf16[256,512]{1,0:T(8,128)(2,1)S(1)}, u32[]{:S(2)}, u32[]{:S(2)}) %collective-permute-start.39) | collective-permute-done | bytes 262176 | tf_op jit(solution)/shard_map/ppermute | solution.py:713
  309.1 2.3 collective-permute-start.41
  311.7 2.3 collective-permute-start.35
  315.0 4.0 %collective-permute-done.34 = bf16[176,512]{1,0:T(8,128)(2,1)S(1)} collective-permute-done((bf16[176,512]{1,0:T(8,128)(2,1)S(1)}, bf16[176,512]{1,0:T(8,128)(2,1)S(1)}, u32[]{:S(2)}, u32[]{:S(2)}) %collective-permute-start.34) | collective-permute-done | bytes 180256 | tf_op jit(solution)/shard_map/ppermute | solution.py:713
  319.0 6.2 %collective-permute-done.35 = bf16[176,512]{1,0:T(8,128)(2,1)S(1)} collective-permute-done((bf16[176,512]{1,0:T(8,128)(2,1)S(1)}, bf16[176,512]{1,0:T(8,128)(2,1)S(1)}, u32[]{:S(2)}, u32[]{:S(2)}) %collective-permute-start.35) | collective-permute-done | bytes 180256 | tf_op jit(solution)/shard_map/ppermute | solution.py:713
  325.3 5.0 %collective-permute-done.36 = bf16[176,512]{1,0:T(8,128)(2,1)S(1)} collective-permute-done((bf16[176,512]{1,0:T(8,128)(2,1)S(1)}, bf16[176,512]{1,0:T(8,128)(2,1)S(1)}, u32[]{:S(2)}, u32[]{:S(2)}) %collective-permute-start.36) | collective-permute-done | bytes 180256 | tf_op jit(solution)/shard_map/ppermute | solution.py:713
  (166 shorter events, 32.4 us)
Async XLA Ops:
  0.7 21.5 %collective-permute-start.1 = (bf16[1,4608,512]{2,1,0:T(8,128)(2,1)}, bf16[1,4608,512]{2,1,0:T(8,128)(2,1)}, u32[]{:S(2)}, u32[]{:S(2)}) collective-permute-start(bf16[1,4608,512]{2,1,0:T(8,128)(2,1)} %refs_9_.3), channel_id=1, source_target_pairs={{0,16},{16,0},{1,17},{17,1},{2,18},{18,2},{3,19},{19,3},{4,20},{20... | collective-permute-start | bytes 14155784 | tf_op jit(solution)/shard_map/ppermute | solution.py:709
  8.3 28.0 %collective-permute-start.2 = (bf16[1024,1024]{1,0:T(8,128)(2,1)}, bf16[1024,1024]{1,0:T(8,128)(2,1)}, u32[]{:S(2)}, u32[]{:S(2)}) collective-permute-start(bf16[1024,1024]{1,0:T(8,128)(2,1)} %get-tuple-element.149.refs_2_.refs_9_.refs_5_), channel_id=1, source_target_pairs={{0,16},{16,0},{1,17},{17,1},{2,18},{18,2},{3,19},{19,3},{4,20},{20... | collective-permute-start | bytes 6291464 | tf_op jit(solution)/shard_map/ppermute | solution.py:709
  8.4 34.5 %collective-permute-start.3 = (bf16[1,512,2048]{2,1,0:T(8,128)(2,1)S(1)}, bf16[1,512,2048]{2,1,0:T(8,128)(2,1)}, u32[]{:S(2)}, u32[]{:S(2)}) collective-permute-start(bf16[1,512,2048]{2,1,0:T(8,128)(2,1)S(1)} %copy-done), channel_id=1, source_target_pairs={{0,16},{16,0},{1,17},{17,1},{2,18},{18,2},{3,19},{19,3},{4,20},{20... | collective-permute-start | bytes 6291464 | tf_op jit(solution)/shard_map/ppermute | solution.py:709
  8.9 12.7 %collective-permute-start = (f32[4,512]{1,0:T(4,128)S(1)}, f32[4,512]{1,0:T(4,128)S(1)}, u32[]{:S(2)}, u32[]{:S(2)}) collective-permute-start(f32[4,512]{1,0:T(4,128)S(1)} %pad_maximum_fusion.11), channel_id=1, source_target_pairs={{0,16},{16,0},{1,17},{17,1},{2,18},{18,2},{3,19},{19,3},{4,20},{20... | collective-permute-start | bytes 24584 | tf_op jit(solution)/shard_map/ppermute | solution.py:709
  9.1 13.1 %all-to-all-start = ((f32[16,2,512]{2,1,0:T(2,128)}), f32[16,2,512]{2,1,0:T(2,128)S(1)}, u32[]{:S(2)}, u32[]{:S(2)}) async-start(f32[16,2,512]{2,1,0:T(2,128)} %get-tuple-element.147), calls=%async_computation | async-start | bytes 131072 | tf_op jit(solution)/shard_map/all_to_all | solution.py:705
  22.2 13.4 %copy-start.19 = (f32[1,2048]{1,0:T(1,128)S(1)}, f32[1,2048]{1,0:T(1,128)}, u32[]{:S(2)}) copy-start(f32[1,2048]{1,0:T(1,128)} %param.27) | copy-start | bytes 24580
  22.2 13.4 %copy-start.20 = (f32[1,2048]{1,0:T(1,128)S(1)}, f32[1,2048]{1,0:T(1,128)}, u32[]{:S(2)}) copy-start(f32[1,2048]{1,0:T(1,128)} %param.26) | copy-start | bytes 24580
  28.2 32.1 %collective-permute-start.4 = (bf16[256,4608]{1,0:T(8,128)(2,1)}, bf16[256,4608]{1,0:T(8,128)(2,1)}, u32[]{:S(2)}, u32[]{:S(2)}) collective-permute-start(bf16[256,4608]{1,0:T(8,128)(2,1)} %get-tuple-element.155.refs_1_), channel_id=1, source_target_pairs={{0,16},{16,0},{1,17},{17,1},{2,18},{18,2},{3,19},{19,3},{4,20},{20... | collective-permute-start | bytes 7077896 | tf_op jit(solution)/shard_map/ppermute | solution.py:709
  29.2 13.7 %all-to-all-start.1 = ((bf16[16,2,3840]{2,1,0:T(2,128)(2,1)}), bf16[16,2,3840]{2,1,0:T(2,128)(2,1)S(1)}, u32[]{:S(2)}, u32[]{:S(2)}) async-start(bf16[16,2,3840]{2,1,0:T(2,128)(2,1)} %get-tuple-element.151), calls=%async_computation.1 | async-start | bytes 491520 | tf_op jit(solution)/shard_map/all_to_all | solution.py:705
  35.6 20.1 %collective-permute-start.5 = (f32[2,2048]{1,0:T(2,128)S(1)}, f32[2,2048]{1,0:T(2,128)S(1)}, u32[]{:S(2)}, u32[]{:S(2)}) collective-permute-start(f32[2,2048]{1,0:T(2,128)S(1)} %pad_maximum_fusion.9), channel_id=1, source_target_pairs={{0,16},{16,0},{1,17},{17,1},{2,18},{18,2},{3,19},{19,3},{4,20},{20... | collective-permute-start | bytes 49160 | tf_op jit(solution)/shard_map/ppermute | solution.py:709
  43.0 10.5 %copy-start.27 = (f32[2048]{0:T(1024)S(1)}, f32[2048]{0:T(1024)}, u32[]{:S(2)}) copy-start(f32[2048]{0:T(1024)} %param.20) | copy-start | bytes 24580
  43.0 10.5 %copy-start.28 = (f32[2048]{0:T(1024)S(1)}, f32[2048]{0:T(1024)}, u32[]{:S(2)}) copy-start(f32[2048]{0:T(1024)} %param.19) | copy-start | bytes 24580
  48.1 12.2 %all-to-all-start.2 = ((f32[16,2,2048]{2,1,0:T(2,128)}), f32[16,2,2048]{2,1,0:T(2,128)S(1)}, u32[]{:S(2)}, u32[]{:S(2)}) async-start(f32[16,2,2048]{2,1,0:T(2,128)} %get-tuple-element.154), calls=%async_computation.2 | async-start | bytes 524288 | tf_op jit(solution)/shard_map/all_to_all | solution.py:705
  54.1 17.7 %collective-permute-start.6 = (bf16[256,512]{1,0:T(8,128)(2,1)}, bf16[256,512]{1,0:T(8,128)(2,1)S(1)}, u32[]{:S(2)}, u32[]{:S(2)}) collective-permute-start(bf16[256,512]{1,0:T(8,128)(2,1)} %get-tuple-element.161.refs_5_), channel_id=1, source_target_pairs={{0,16},{16,0},{1,17},{17,1},{2,18},{18,2},{3,19},{19,3},{4,20},{20... | collective-permute-start | bytes 786440 | tf_op jit(solution)/shard_map/ppermute | solution.py:709
  65.9 11.4 %all-to-all-start.3 = ((f32[16,2,512]{2,1,0:T(2,128)}), f32[16,2,512]{2,1,0:T(2,128)S(1)}, u32[]{:S(2)}, u32[]{:S(2)}) async-start(f32[16,2,512]{2,1,0:T(2,128)} %get-tuple-element.160), calls=%async_computation.3 | async-start | bytes 131072 | tf_op jit(solution)/shard_map/all_to_all | solution.py:705
  71.8 11.4 %copy-start.12 = (bf16[256,512]{1,0:T(8,128)(2,1)}, bf16[256,512]{1,0:T(8,128)(2,1)S(1)}, u32[]{:S(2)}) copy-start(bf16[256,512]{1,0:T(8,128)(2,1)S(1)} %collective-permute-done.6.refs_6_) | copy-start | bytes 786436
  83.2 28.4 %collective-permute-start.8 = (bf16[256,4608]{1,0:T(8,128)(2,1)}, bf16[256,4608]{1,0:T(8,128)(2,1)}, u32[]{:S(2)}, u32[]{:S(2)}) collective-permute-start(bf16[256,4608]{1,0:T(8,128)(2,1)} %get-tuple-element.169.refs_5_), channel_id=1, source_target_pairs={{0,16},{16,0},{1,17},{17,1},{2,18},{18,2},{3,19},{19,3},{4,20},{20... | collective-permute-start | bytes 7077896 | tf_op jit(solution)/shard_map/ppermute | solution.py:709
  86.0 10.0 %collective-permute-start.7 = (bf16[256,2048]{1,0:T(8,128)(2,1)S(1)}, bf16[256,2048]{1,0:T(8,128)(2,1)S(1)}, u32[]{:S(2)}, u32[]{:S(2)}) collective-permute-start(bf16[256,2048]{1,0:T(8,128)(2,1)S(1)} %copy-done.1), channel_id=1, source_target_pairs={{0,16},{16,0},{1,17},{17,1},{2,18},{18,2},{3,19},{19,3},{4,20},{20... | collective-permute-start | bytes 3145736 | tf_op jit(solution)/shard_map/ppermute | solution.py:709
  100.8 10.7 %all-to-all-start.5 = ((bf16[16,2,3072]{2,1,0:T(2,128)(2,1)}), bf16[16,2,3072]{2,1,0:T(2,128)(2,1)S(1)}, u32[]{:S(2)}, u32[]{:S(2)}) async-start(bf16[16,2,3072]{2,1,0:T(2,128)(2,1)} %get-tuple-element.168), calls=%async_computation.5 | async-start | bytes 393216 | tf_op jit(solution)/shard_map/all_to_all | solution.py:705
  105.3 17.8 %collective-permute-start.9 = (bf16[256,512]{1,0:T(8,128)(2,1)}, bf16[256,512]{1,0:T(8,128)(2,1)S(1)}, u32[]{:S(2)}, u32[]{:S(2)}) collective-permute-start(bf16[256,512]{1,0:T(8,128)(2,1)} %get-tuple-element.174.refs_1_), channel_id=1, source_target_pairs={{0,16},{16,0},{1,17},{17,1},{2,18},{18,2},{3,19},{19,3},{4,20},{20... | collective-permute-start | bytes 786440 | tf_op jit(solution)/shard_map/ppermute | solution.py:709
  117.9 10.9 %all-to-all-start.6 = ((bf16[16,2,2048]{2,1,0:T(2,128)(2,1)}), bf16[16,2,2048]{2,1,0:T(2,128)(2,1)S(1)}, u32[]{:S(2)}, u32[]{:S(2)}) async-start(bf16[16,2,2048]{2,1,0:T(2,128)(2,1)} %get-tuple-element.173), calls=%async_computation.6 | async-start | bytes 262144 | tf_op jit(solution)/shard_map/all_to_all | solution.py:705
  123.0 11.2 %copy-start.14 = (bf16[256,512]{1,0:T(8,128)(2,1)}, bf16[256,512]{1,0:T(8,128)(2,1)S(1)}, u32[]{:S(2)}) copy-start(bf16[256,512]{1,0:T(8,128)(2,1)S(1)} %collective-permute-done.9.refs_2_) | copy-start | bytes 786436
  134.2 12.7 %collective-permute-start.10 = (bf16[256,2048]{1,0:T(8,128)(2,1)}, bf16[256,2048]{1,0:T(8,128)(2,1)S(1)}, u32[]{:S(2)}, u32[]{:S(2)}) collective-permute-start(bf16[256,2048]{1,0:T(8,128)(2,1)} %get-tuple-element.180.refs_3_), channel_id=1, source_target_pairs={{0,16},{16,0},{1,17},{17,1},{2,18},{18,2},{3,19},{19,3},{4,20},{20... | collective-permute-start | bytes 3145736 | tf_op jit(solution)/shard_map/ppermute | solution.py:709
  153.3 5.7 %collective-permute-start.11 = (bf16[256,512]{1,0:T(8,128)(2,1)}, bf16[256,512]{1,0:T(8,128)(2,1)S(1)}, u32[]{:S(2)}, u32[]{:S(2)}) collective-permute-start(bf16[256,512]{1,0:T(8,128)(2,1)} %get-tuple-element.188.refs_7_), channel_id=1, source_target_pairs={{0,16},{16,0},{1,17},{17,1},{2,18},{18,2},{3,19},{19,3},{4,20},{20... | collective-permute-start | bytes 786440 | tf_op jit(solution)/shard_map/ppermute | solution.py:709
  154.6 11.7 %all-to-all-start.8 = ((f32[16,2,512]{2,1,0:T(2,128)}), f32[16,2,512]{2,1,0:T(2,128)S(1)}, u32[]{:S(2)}, u32[]{:S(2)}) async-start(f32[16,2,512]{2,1,0:T(2,128)} %get-tuple-element.184), calls=%async_computation.8 | async-start | bytes 131072 | tf_op jit(solution)/shard_map/all_to_all | solution.py:705
  166.3 23.3 %collective-permute-start.13 = (bf16[2,4,208,256]{3,2,1,0:T(8,128)(2,1)}, bf16[2,4,208,256]{3,2,1,0:T(8,128)(2,1)S(1)}, u32[]{:S(2)}, u32[]{:S(2)}) collective-permute-start(bf16[2,4,208,256]{3,2,1,0:T(8,128)(2,1)} %get-tuple-element.198), channel_id=1, source_target_pairs={{0,1},{1,0},{2,3},{3,2},{4,5},{5,4},{6,7},{7,6},{8,9},{9,8},{10,11... | collective-permute-start | bytes 2555912 | tf_op jit(solution)/shard_map/ppermute | solution.py:713
  167.5 22.1 %collective-permute-start.14 = (bf16[2,4,208,256]{3,2,1,0:T(8,128)(2,1)}, bf16[2,4,208,256]{3,2,1,0:T(8,128)(2,1)}, u32[]{:S(2)}, u32[]{:S(2)}) collective-permute-start(bf16[2,4,208,256]{3,2,1,0:T(8,128)(2,1)} %get-tuple-element.200), channel_id=1, source_target_pairs={{0,2},{1,3},{2,0},{3,1},{4,6},{5,7},{6,4},{7,5},{8,10},{9,11},{10,... | collective-permute-start | bytes 2555912 | tf_op jit(solution)/shard_map/ppermute | solution.py:713
  168.7 20.9 %copy-start.7 = (bf16[2,4,208,256]{3,2,1,0:T(8,128)(2,1)S(1)}, bf16[2,4,208,256]{3,2,1,0:T(8,128)(2,1)}, u32[]{:S(2)}) copy-start(bf16[2,4,208,256]{3,2,1,0:T(8,128)(2,1)} %get-tuple-element.197) | copy-start | bytes 2555908
  168.7 21.0 %copy-start.8 = (bf16[2,4,208,256]{3,2,1,0:T(8,128)(2,1)S(1)}, bf16[2,4,208,256]{3,2,1,0:T(8,128)(2,1)}, u32[]{:S(2)}) copy-start(bf16[2,4,208,256]{3,2,1,0:T(8,128)(2,1)} %get-tuple-element.199) | copy-start | bytes 2555908
  176.7 12.9 %all-to-all-start.9 = ((bf16[16,2,3072]{2,1,0:T(2,128)(2,1)}), bf16[16,2,3072]{2,1,0:T(2,128)(2,1)S(1)}, u32[]{:S(2)}, u32[]{:S(2)}) async-start(bf16[16,2,3072]{2,1,0:T(2,128)(2,1)} %get-tuple-element.194), calls=%async_computation.9 | async-start | bytes 393216 | tf_op jit(solution)/shard_map/all_to_all | solution.py:705
  181.4 2.8 collective-permute-start.12
  184.2 14.3 %copy-start.15 = (bf16[256,512]{1,0:T(8,128)(2,1)}, bf16[256,512]{1,0:T(8,128)(2,1)S(1)}, u32[]{:S(2)}) copy-start(bf16[256,512]{1,0:T(8,128)(2,1)S(1)} %collective-permute-done.12.refs_4_) | copy-start | bytes 786436
  189.6 10.6 %copy-start.9 = (bf16[2,4,208,256]{3,2,1,0:T(8,128)(2,1)}, bf16[2,4,208,256]{3,2,1,0:T(8,128)(2,1)S(1)}, u32[]{:S(2)}) copy-start(bf16[2,4,208,256]{3,2,1,0:T(8,128)(2,1)S(1)} %collective-permute-done.13) | copy-start | bytes 2555908
  198.5 8.8 %collective-permute-start.15 = (bf16[256,2048]{1,0:T(8,128)(2,1)}, bf16[256,2048]{1,0:T(8,128)(2,1)S(1)}, u32[]{:S(2)}, u32[]{:S(2)}) collective-permute-start(bf16[256,2048]{1,0:T(8,128)(2,1)} %get-tuple-element.208.refs_7_), channel_id=1, source_target_pairs={{0,16},{16,0},{1,17},{17,1},{2,18},{18,2},{3,19},{19,3},{4,20},{20... | collective-permute-start | bytes 3145736 | tf_op jit(solution)/shard_map/ppermute | solution.py:709
  200.2 7.1 %collective-permute-start.16 = (bf16[256,2048]{1,0:T(8,128)(2,1)}, bf16[256,2048]{1,0:T(8,128)(2,1)S(1)}, u32[]{:S(2)}, u32[]{:S(2)}) collective-permute-start(bf16[256,2048]{1,0:T(8,128)(2,1)} %get-tuple-element.210.refs_11_.refs_2_), channel_id=1, source_target_pairs={{0,16},{16,0},{1,17},{17,1},{2,18},{18,2},{3,19},{19,3},{4,20},{20... | collective-permute-start | bytes 3145736 | tf_op jit(solution)/shard_map/ppermute | solution.py:709
  200.3 14.9 %collective-permute-start.17 = (bf16[4,208,256]{2,1,0:T(8,128)(2,1)S(1)}, bf16[4,208,256]{2,1,0:T(8,128)(2,1)}, u32[]{:S(2)}, u32[]{:S(2)}) collective-permute-start(bf16[4,208,256]{2,1,0:T(8,128)(2,1)S(1)} %fusion.13), channel_id=1, source_target_pairs={{0,2},{1,3},{2,0},{3,1},{4,6},{5,7},{6,4},{7,5},{8,10},{9,11},{10,... | collective-permute-start | bytes 1277960 | tf_op jit(solution)/shard_map/ppermute | solution.py:713
  201.5 13.7 %collective-permute-start.18 = (bf16[4,208,256]{2,1,0:T(8,128)(2,1)}, bf16[4,208,256]{2,1,0:T(8,128)(2,1)}, u32[]{:S(2)}, u32[]{:S(2)}) collective-permute-start(bf16[4,208,256]{2,1,0:T(8,128)(2,1)} %fusion.12), channel_id=1, source_target_pairs={{0,1},{1,0},{2,3},{3,2},{4,5},{5,4},{6,7},{7,6},{8,9},{9,8},{10,11... | collective-permute-start | bytes 1277960 | tf_op jit(solution)/shard_map/ppermute | solution.py:713
  201.7 13.4 %all-to-all-start.10 = ((f32[16,2,512]{2,1,0:T(2,128)}), f32[16,2,512]{2,1,0:T(2,128)S(1)}, u32[]{:S(2)}, u32[]{:S(2)}) async-start(f32[16,2,512]{2,1,0:T(2,128)} %get-tuple-element.204), calls=%async_computation.10 | async-start | bytes 131072 | tf_op jit(solution)/shard_map/all_to_all | solution.py:705
  215.2 25.1 %collective-permute-start.20 = (bf16[2,4,256,256]{3,2,1,0:T(8,128)(2,1)}, bf16[2,4,256,256]{3,2,1,0:T(8,128)(2,1)}, u32[]{:S(2)}, u32[]{:S(2)}) collective-permute-start(bf16[2,4,256,256]{3,2,1,0:T(8,128)(2,1)} %get-tuple-element.222), channel_id=1, source_target_pairs={{0,1},{1,0},{2,3},{3,2},{4,5},{5,4},{6,7},{7,6},{8,9},{9,8},{10,11... | collective-permute-start | bytes 3145736 | tf_op jit(solution)/shard_map/ppermute | solution.py:713
  216.4 25.1 %collective-permute-start.21 = (bf16[2,4,256,256]{3,2,1,0:T(8,128)(2,1)}, bf16[2,4,256,256]{3,2,1,0:T(8,128)(2,1)}, u32[]{:S(2)}, u32[]{:S(2)}) collective-permute-start(bf16[2,4,256,256]{3,2,1,0:T(8,128)(2,1)} %get-tuple-element.224), channel_id=1, source_target_pairs={{0,2},{1,3},{2,0},{3,1},{4,6},{5,7},{6,4},{7,5},{8,10},{9,11},{10,... | collective-permute-start | bytes 3145736 | tf_op jit(solution)/shard_map/ppermute | solution.py:713
  225.8 14.4 %all-to-all-start.11 = ((f32[16,2,512]{2,1,0:T(2,128)}), f32[16,2,512]{2,1,0:T(2,128)S(1)}, u32[]{:S(2)}, u32[]{:S(2)}) async-start(f32[16,2,512]{2,1,0:T(2,128)} %get-tuple-element.218), calls=%async_computation.11 | async-start | bytes 131072 | tf_op jit(solution)/shard_map/all_to_all | solution.py:705
  230.4 9.9 %collective-permute-start.19 = (bf16[256,512]{1,0:T(8,128)(2,1)}, bf16[256,512]{1,0:T(8,128)(2,1)S(1)}, u32[]{:S(2)}, u32[]{:S(2)}) collective-permute-start(bf16[256,512]{1,0:T(8,128)(2,1)} %get-tuple-element.219.refs_3_), channel_id=1, source_target_pairs={{0,16},{16,0},{1,17},{17,1},{2,18},{18,2},{3,19},{19,3},{4,20},{20... | collective-permute-start | bytes 786440 | tf_op jit(solution)/shard_map/ppermute | solution.py:709
  246.8 8.7 %collective-permute-start.22 = (bf16[1024,512]{1,0:T(8,128)(2,1)}, bf16[1024,512]{1,0:T(8,128)(2,1)S(1)}, u32[]{:S(2)}, u32[]{:S(2)}) collective-permute-start(bf16[1024,512]{1,0:T(8,128)(2,1)} %get-tuple-element.249.refs_7_.refs_0_), channel_id=1, source_target_pairs={{0,16},{16,0},{1,17},{17,1},{2,18},{18,2},{3,19},{19,3},{4,20},{20... | collective-permute-start | bytes 3145736 | tf_op jit(solution)/shard_map/ppermute | solution.py:709
  249.7 16.8 %collective-permute-start.23 = (bf16[4,256,256]{2,1,0:T(8,128)(2,1)S(1)}, bf16[4,256,256]{2,1,0:T(8,128)(2,1)S(1)}, u32[]{:S(2)}, u32[]{:S(2)}) collective-permute-start(bf16[4,256,256]{2,1,0:T(8,128)(2,1)S(1)} %fusion.5), channel_id=1, source_target_pairs={{0,2},{1,3},{2,0},{3,1},{4,6},{5,7},{6,4},{7,5},{8,10},{9,11},{10,... | collective-permute-start | bytes 1572872 | tf_op jit(solution)/shard_map/ppermute | solution.py:713
  250.9 15.6 %collective-permute-start.24 = (bf16[4,256,256]{2,1,0:T(8,128)(2,1)S(1)}, bf16[4,256,256]{2,1,0:T(8,128)(2,1)S(1)}, u32[]{:S(2)}, u32[]{:S(2)}) collective-permute-start(bf16[4,256,256]{2,1,0:T(8,128)(2,1)S(1)} %fusion.4), channel_id=1, source_target_pairs={{0,1},{1,0},{2,3},{3,2},{4,5},{5,4},{6,7},{7,6},{8,9},{9,8},{10,11... | collective-permute-start | bytes 1572872 | tf_op jit(solution)/shard_map/ppermute | solution.py:713
  251.8 16.9 %collective-permute-start.25 = (bf16[208,512]{1,0:T(8,128)(2,1)}, bf16[208,512]{1,0:T(8,128)(2,1)}, u32[]{:S(2)}, u32[]{:S(2)}) collective-permute-start(bf16[208,512]{1,0:T(8,128)(2,1)} %get-tuple-element.239), channel_id=1, source_target_pairs={{0,4},{1,5},{2,6},{3,7},{4,0},{5,1},{6,2},{7,3},{8,12},{9,13},{10,... | collective-permute-start | bytes 638984 | tf_op jit(solution)/shard_map/ppermute | solution.py:713
  252.1 16.7 %collective-permute-start.26 = (bf16[208,512]{1,0:T(8,128)(2,1)}, bf16[208,512]{1,0:T(8,128)(2,1)}, u32[]{:S(2)}, u32[]{:S(2)}) collective-permute-start(bf16[208,512]{1,0:T(8,128)(2,1)} %get-tuple-element.240), channel_id=1, source_target_pairs={{0,8},{1,9},{2,10},{3,11},{4,12},{5,13},{6,14},{7,15},{8,0},{9,1},... | collective-permute-start | bytes 638984 | tf_op jit(solution)/shard_map/ppermute | solution.py:713
  255.5 17.5 %collective-permute-start.27 = (bf16[208,512]{1,0:T(8,128)(2,1)}, bf16[208,512]{1,0:T(8,128)(2,1)}, u32[]{:S(2)}, u32[]{:S(2)}) collective-permute-start(bf16[208,512]{1,0:T(8,128)(2,1)} %get-tuple-element.241), channel_id=1, source_target_pairs={{0,12},{1,13},{2,14},{3,15},{4,8},{5,9},{6,10},{7,11},{8,4},{9,5},... | collective-permute-start | bytes 638984 | tf_op jit(solution)/shard_map/ppermute | solution.py:713
  273.0 10.7 %collective-permute-start.29 = (f32[2,2,512]{2,1,0:T(2,128)}, f32[2,2,512]{2,1,0:T(2,128)S(1)}, u32[]{:S(2)}, u32[]{:S(2)}) collective-permute-start(f32[2,2,512]{2,1,0:T(2,128)} %broadcast_select_fusion.7), channel_id=1, source_target_pairs={{0,16},{16,0},{1,17},{17,1},{2,18},{18,2},{3,19},{19,3},{4,20},{20... | collective-permute-start | bytes 24584 | tf_op jit(solution)/shard_map/ppermute | solution.py:709
  274.8 11.3 %collective-permute-start.28 = (f32[4,2048]{1,0:T(4,128)}, f32[4,2048]{1,0:T(4,128)S(1)}, u32[]{:S(2)}, u32[]{:S(2)}) collective-permute-start(f32[4,2048]{1,0:T(4,128)} %pad_maximum_fusion.8), channel_id=1, source_target_pairs={{0,16},{16,0},{1,17},{17,1},{2,18},{18,2},{3,19},{19,3},{4,20},{20... | collective-permute-start | bytes 98312 | tf_op jit(solution)/shard_map/ppermute | solution.py:709
  276.1 18.4 %copy-start.10 = (bf16[2,4,176,256]{3,2,1,0:T(8,128)(2,1)S(1)}, bf16[2,4,176,256]{3,2,1,0:T(8,128)(2,1)}, u32[]{:S(2)}) copy-start(bf16[2,4,176,256]{3,2,1,0:T(8,128)(2,1)} %get-tuple-element.256) | copy-start | bytes 2162692
  276.1 18.4 %copy-start.11 = (bf16[2,4,176,256]{3,2,1,0:T(8,128)(2,1)S(1)}, bf16[2,4,176,256]{3,2,1,0:T(8,128)(2,1)}, u32[]{:S(2)}) copy-start(bf16[2,4,176,256]{3,2,1,0:T(8,128)(2,1)} %get-tuple-element.258) | copy-start | bytes 2162692
  276.1 17.5 %collective-permute-start.30 = (bf16[2,4,176,256]{3,2,1,0:T(8,128)(2,1)}, bf16[2,4,176,256]{3,2,1,0:T(8,128)(2,1)S(1)}, u32[]{:S(2)}, u32[]{:S(2)}) collective-permute-start(bf16[2,4,176,256]{3,2,1,0:T(8,128)(2,1)} %get-tuple-element.253), channel_id=1, source_target_pairs={{0,1},{1,0},{2,3},{3,2},{4,5},{5,4},{6,7},{7,6},{8,9},{9,8},{10,11... | collective-permute-start | bytes 2162696 | tf_op jit(solution)/shard_map/ppermute | solution.py:713
  277.4 17.1 %collective-permute-start.31 = (bf16[2,4,176,256]{3,2,1,0:T(8,128)(2,1)}, bf16[2,4,176,256]{3,2,1,0:T(8,128)(2,1)S(1)}, u32[]{:S(2)}, u32[]{:S(2)}) collective-permute-start(bf16[2,4,176,256]{3,2,1,0:T(8,128)(2,1)} %get-tuple-element.254), channel_id=1, source_target_pairs={{0,2},{1,3},{2,0},{3,1},{4,6},{5,7},{6,4},{7,5},{8,10},{9,11},{10,... | collective-permute-start | bytes 2162696 | tf_op jit(solution)/shard_map/ppermute | solution.py:713
  283.6 12.1 %collective-permute-start.37 = (bf16[256,512]{1,0:T(8,128)(2,1)S(1)}, bf16[256,512]{1,0:T(8,128)(2,1)S(1)}, u32[]{:S(2)}, u32[]{:S(2)}) collective-permute-start(bf16[256,512]{1,0:T(8,128)(2,1)S(1)} %get-tuple-element.274), channel_id=1, source_target_pairs={{0,4},{1,5},{2,6},{3,7},{4,0},{5,1},{6,2},{7,3},{8,12},{9,13},{10,... | collective-permute-start | bytes 786440 | tf_op jit(solution)/shard_map/ppermute | solution.py:713
  283.7 13.3 %collective-permute-start.38 = (bf16[256,512]{1,0:T(8,128)(2,1)S(1)}, bf16[256,512]{1,0:T(8,128)(2,1)S(1)}, u32[]{:S(2)}, u32[]{:S(2)}) collective-permute-start(bf16[256,512]{1,0:T(8,128)(2,1)S(1)} %get-tuple-element.275), channel_id=1, source_target_pairs={{0,8},{1,9},{2,10},{3,11},{4,12},{5,13},{6,14},{7,15},{8,0},{9,1},... | collective-permute-start | bytes 786440 | tf_op jit(solution)/shard_map/ppermute | solution.py:713
  286.0 22.2 %collective-permute-start.39 = (bf16[256,512]{1,0:T(8,128)(2,1)S(1)}, bf16[256,512]{1,0:T(8,128)(2,1)S(1)}, u32[]{:S(2)}, u32[]{:S(2)}) collective-permute-start(bf16[256,512]{1,0:T(8,128)(2,1)S(1)} %get-tuple-element.276), channel_id=1, source_target_pairs={{0,12},{1,13},{2,14},{3,15},{4,8},{5,9},{6,10},{7,11},{8,4},{9,5},... | collective-permute-start | bytes 786440 | tf_op jit(solution)/shard_map/ppermute | solution.py:713
  294.6 16.8 %collective-permute-start.32 = (bf16[4,176,256]{2,1,0:T(8,128)(2,1)S(1)}, bf16[4,176,256]{2,1,0:T(8,128)(2,1)S(1)}, u32[]{:S(2)}, u32[]{:S(2)}) collective-permute-start(bf16[4,176,256]{2,1,0:T(8,128)(2,1)S(1)} %add_bitcast_fusion.1), channel_id=1, source_target_pairs={{0,2},{1,3},{2,0},{3,1},{4,6},{5,7},{6,4},{7,5},{8,10},{9,11},{10,... | collective-permute-start | bytes 1081352 | tf_op jit(solution)/shard_map/ppermute | solution.py:713
  294.9 16.5 %collective-permute-start.33 = (bf16[4,176,256]{2,1,0:T(8,128)(2,1)S(1)}, bf16[4,176,256]{2,1,0:T(8,128)(2,1)S(1)}, u32[]{:S(2)}, u32[]{:S(2)}) collective-permute-start(bf16[4,176,256]{2,1,0:T(8,128)(2,1)S(1)} %add_bitcast_fusion), channel_id=1, source_target_pairs={{0,1},{1,0},{2,3},{3,2},{4,5},{5,4},{6,7},{7,6},{8,9},{9,8},{10,11... | collective-permute-start | bytes 1081352 | tf_op jit(solution)/shard_map/ppermute | solution.py:713
  309.1 22.5 %collective-permute-start.41 = (f32[32,1024]{1,0:T(8,128)S(1)}, f32[32,1024]{1,0:T(8,128)S(1)}, u32[]{:S(2)}, u32[]{:S(2)}) collective-permute-start(f32[32,1024]{1,0:T(8,128)S(1)} %fusion.41), channel_id=1, source_target_pairs={{0,16},{16,0},{1,17},{17,1},{2,18},{18,2},{3,19},{19,3},{4,20},{20... | collective-permute-start | bytes 393224 | tf_op jit(solution)/shard_map/ppermute | solution.py:709
  311.6 7.5 %collective-permute-start.34 = (bf16[176,512]{1,0:T(8,128)(2,1)S(1)}, bf16[176,512]{1,0:T(8,128)(2,1)S(1)}, u32[]{:S(2)}, u32[]{:S(2)}) collective-permute-start(bf16[176,512]{1,0:T(8,128)(2,1)S(1)} %get-tuple-element.267), channel_id=1, source_target_pairs={{0,4},{1,5},{2,6},{3,7},{4,0},{5,1},{6,2},{7,3},{8,12},{9,13},{10,... | collective-permute-start | bytes 540680 | tf_op jit(solution)/shard_map/ppermute | solution.py:713
  311.7 13.6 %collective-permute-start.35 = (bf16[176,512]{1,0:T(8,128)(2,1)S(1)}, bf16[176,512]{1,0:T(8,128)(2,1)S(1)}, u32[]{:S(2)}, u32[]{:S(2)}) collective-permute-start(bf16[176,512]{1,0:T(8,128)(2,1)S(1)} %get-tuple-element.268), channel_id=1, source_target_pairs={{0,8},{1,9},{2,10},{3,11},{4,12},{5,13},{6,14},{7,15},{8,0},{9,1},... | collective-permute-start | bytes 540680 | tf_op jit(solution)/shard_map/ppermute | solution.py:713
  314.0 16.3 %collective-permute-start.36 = (bf16[176,512]{1,0:T(8,128)(2,1)S(1)}, bf16[176,512]{1,0:T(8,128)(2,1)S(1)}, u32[]{:S(2)}, u32[]{:S(2)}) collective-permute-start(bf16[176,512]{1,0:T(8,128)(2,1)S(1)} %get-tuple-element.269), channel_id=1, source_target_pairs={{0,12},{1,13},{2,14},{3,15},{4,8},{5,9},{6,10},{7,11},{8,4},{9,5},... | collective-permute-start | bytes 540680 | tf_op jit(solution)/shard_map/ppermute | solution.py:713
  330.5 2.6 collective-permute-start.40
  (17 other events, 138.8 us)
